TPU v7x, 128 devices: a whole 4x4x4 slice. The times are simulated.
128 devices in a mesh: slot: 4 (over x_hi, core), ctx: 32 (over z, x_lo, y).
Axes of the slice: x: 4 (x_hi: 2, x_lo: 2; x = x_hi * 2 + x_lo), y: 4, z: 4, core: 2. Of those that a mesh axis runs over, the one named last changes fastest.
Arguments:
- latents: bfloat16 [4, 2048, 3072], P('slot', 'ctx'), may hold values from -6 to 6
- fresh: bfloat16 [2048, 3072], P('ctx'), may hold values from -6 to 6
- span_ids: int32 [4], replicated, may hold values from 0 to 3, each once
- noise_step: int32 [4], replicated, may hold values from 0 to 1
- ada_table: float32 [9, 3, 3072], replicated, may hold values from -3 to 3
- w_qkv: bfloat16 [3072, 5120], P(None, 'slot'), may hold values from -1 to 1
- w_out: bfloat16 [3072, 3072], P(None, 'slot'), may hold values from -0.109375 to 0.109375
Outputs:
- velocity: bfloat16 [2, 4, 2048, 3072], P(None, 'slot', 'ctx')
- finished: bfloat16 [2048, 3072], P('ctx', 'slot')
Inputs may be any that keep to these rules, and one draw needn't show every extreme that they name: `span_ids`: each slot holds another span number.
All inputs are finite; a program needn't handle non-finite values.
Results may differ from a plain program's by a relative error of at most 0.02.
Values may be sent and summed in bfloat16 or wider, within the bound.
No kernel may reach another device: no remote copies, remote signals or barrier semaphores. Data moves between devices by JAX's collectives and lax.ppermute only.
A program may use at most 128 MiB of HBM per device.

v0:
```python
import math

import jax
import jax.numpy as jnp
from jax import lax
from jax.experimental import pallas as pl
from jax.experimental.pallas import tpu as pltpu
from jax.sharding import PartitionSpec as P

HD = 128
EPS = 1e-06
BF = jnp.bfloat16
F32 = jnp.float32
AXES = ("slot", "ctx")
VM = pl.BlockSpec(memory_space=pltpu.VMEM)
SM = pl.BlockSpec(memory_space=pltpu.SMEM)
SLOTS = 4
PER = 2
TOK = 64
HALF = 32
ROWS = SLOTS * HALF
WIDTH = 3072
COLS = WIDTH // SLOTS
LOG2E = 1.4426950408889634


def where_is(flat):
    s, c = flat // 32, flat % 32
    return dict(h=s // 2, i=s % 2, z=c // 8, xl=(c // 4) % 2, y=c % 4)


def flat_of(d):
    return (d["h"] * 2 + d["i"]) * 32 + d["z"] * 8 + d["xl"] * 4 + d["y"]


def move(x, h=0, i=0, z=0, y=0):
    pairs = []
    for f in range(128):
        d = where_is(f)
        d["h"] = (d["h"] + h) % 2
        d["i"] = (d["i"] + i) % 2
        d["z"] = (d["z"] + z) % 4
        d["y"] = (d["y"] + y) % 4
        pairs.append((f, flat_of(d)))
    return lax.ppermute(x, AXES, pairs)


def group_lists():
    out = []
    for i in range(2):
        for z in range(4):
            for yh in range(2):
                out.append(
                    [
                        flat_of(dict(h=h, i=i, z=z, xl=xl, y=2 * yh + yl))
                        for h in range(2)
                        for xl in range(2)
                        for yl in range(2)
                    ]
                )
    return out


def exchange(x):
    return lax.all_to_all(x, AXES, 0, 0, tiled=True, axis_index_groups=group_lists())


def params(mib, **kw):
    return pltpu.CompilerParams(vmem_limit_bytes=mib * 1024 * 1024, **kw)


def first_slot(sc):
    best, at = sc[0], jnp.int32(0)
    for j in range(1, SLOTS):
        less = sc[j] < best
        best = jnp.where(less, sc[j], best)
        at = jnp.where(less, j, at)
    return at


def rank_of(sc, t, step):
    mine = sc[t]
    rank = jnp.int32(0)
    for j in range(SLOTS):
        rank = rank + (sc[j] < mine).astype(jnp.int32)
    if step == 0:
        return rank
    return jnp.where(rank == 0, SLOTS - 1, rank - 1)


def level_of(sc, t, step):
    rank = rank_of(sc, t, 0)
    level = PER * rank + sc[SLOTS + t] + 1
    if step == 0:
        return level
    return jnp.where(rank == 0, SLOTS * PER, level - 1)


def row_of(half, slot):
    return pl.ds(pl.multiple_of((half * SLOTS + slot) * HALF, HALF), HALF)


def col_of(slot, width=COLS):
    return pl.ds(pl.multiple_of(slot * width, 128), width)


def modulated(values, ada, level):
    center = jnp.mean(values, axis=-1, keepdims=True)
    off = values - center
    spread = jnp.mean(off * off, axis=-1, keepdims=True)
    normed = off * lax.rsqrt(spread + EPS)
    return (normed * (1.0 + ada[level, 1:2, :]) + ada[level, 0:1, :]).astype(BF)


def project(hidden, w, mine, theirs):
    out = jnp.dot(hidden[...], w[...], preferred_element_type=F32).astype(BF)
    cut = out.shape[0] // 2
    for k in range(mine.shape[0]):
        mine[k] = out[:cut, k * HD : (k + 1) * HD]
        theirs[k] = out[cut:, k * HD : (k + 1) * HD]


PAIR = 2 * HALF


def first_body(sc, x0, x1, ada, w, mine, theirs, hidden, *, far):
    s = sc[8]
    i = s % 2
    for r, x in enumerate((x0, x1)):
        t = s ^ (r + far)
        level = level_of(sc, t, 0)
        for a in range(2):
            values = x[a * HALF : (a + 1) * HALF, :].astype(F32)
            to = pl.ds(pl.multiple_of(((i ^ a) * 2 + t % 2) * HALF, HALF), HALF)
            hidden[to, :] = modulated(values, ada, level)
    project(hidden, w, mine, theirs)


def second_body(
    sc, x0, x1, x2, x3, here, away, fresh, ada, w, w_pair,
    mine, other, vel, fin, theirs, hidden, vall,
):
    s = sc[8]
    i = s % 2
    step_size = 1.0 / (SLOTS * PER)
    half = pl.ds(pl.multiple_of(i * HALF, HALF), HALF)
    for k in range(2):
        vall[:, col_of(s ^ k)] = here[k]
        vall[:, col_of(s ^ (2 + k))] = away[k]
    first = first_slot(sc)
    for r, x in enumerate((x0, x1, x2, x3)):
        t = s ^ r
        level = level_of(sc, t, 1)
        where = row_of(0, t)
        moved = x[half, :].astype(F32) - vall[where, :].astype(F32) * step_size
        taken = jnp.where(t == first, fresh[half, :], moved.astype(BF))
        hidden[where, :] = modulated(taken.astype(F32), ada, level)
    for r, x in enumerate((x0, x1, x2, x3)):

        @pl.when(s ^ r == first)
        def _():
            def done(slot):
                drift = vall[row_of(0, s ^ r), col_of(slot)].astype(F32)
                return (x[half, col_of(slot)].astype(F32) - drift * step_size).astype(BF)

            fin[...] = done(s)
            theirs[:, WIDTH:] = done(s ^ 1)

    vel[...] = vall[row_of(0, s), :]
    theirs[:, :WIDTH] = vall[row_of(0, s ^ 1), :]
    for out, weights in ((mine, w), (other, w_pair)):
        product = jnp.dot(hidden[...], weights[...], preferred_element_type=F32).astype(BF)
        for k in range(out.shape[0]):
            out[k] = product[:, k * HD : (k + 1) * HD]


def projected_shapes(heads, rows):
    return [jax.ShapeDtypeStruct((heads, rows, HD), BF)] * 2


def first_projection(sc, xs, far, ada, w):
    def body(*refs):
        first_body(*refs, far=far)

    return pl.pallas_call(
        body,
        in_specs=[SM] + [VM] * 4,
        out_specs=[VM] * 2,
        out_shape=projected_shapes(w.shape[1] // HD, PAIR),
        scratch_shapes=[pltpu.VMEM((2 * PAIR, WIDTH), BF)],
        compiler_params=params(12),
        cost_estimate=pl.CostEstimate(flops=4 * 10**9, bytes_accessed=10**7, transcendentals=0),
        name="modulate_project",
    )(sc, *xs, ada, w)


def second_projection(sc, xs, here, away, fresh, ada, w, w_pair):
    return pl.pallas_call(
        second_body,
        in_specs=[SM] + [VM] * 10,
        out_specs=[VM] * 5,
        out_shape=projected_shapes(w.shape[1] // HD, ROWS)
        + [jax.ShapeDtypeStruct((HALF, n), BF) for n in (WIDTH, COLS, WIDTH + COLS)],
        scratch_shapes=[pltpu.VMEM((ROWS, WIDTH), BF)] * 2,
        compiler_params=params(14),
        cost_estimate=pl.CostEstimate(flops=4 * 10**9, bytes_accessed=10**7, transcendentals=0),
        name="advance_modulate_project",
    )(sc, *xs, here, away, fresh, ada, w, w_pair)


def pack_body(step, sc, *refs):
    parts, (out, chip) = refs[:-2], refs[-2:]
    i, h = sc[8] % 2, sc[8] // 2
    for k in range(2):
        to = pl.ds(10 * jnp.where(k == 0, i, 1 - i), 10)
        if step == 1:
            chip[to] = parts[k][...]
            continue
        for n in range(2):
            at = pl.multiple_of((h ^ n) * PAIR, PAIR)
            chip[to, pl.ds(at, PAIR)] = parts[2 * k + n][...]
    for g in range(8):
        out[g, 3] = chip[4 + g]
        out[g, 4] = chip[12 + g]

    def queries(low, high, at):
        for n in range(24):
            if low <= n < high:
                out[n // 3, n % 3] = chip[n - at]
            else:
                out[n // 3, n % 3] = jnp.zeros((ROWS, HD), BF)

    @pl.when(h == 0)
    def _():
        queries(0, 20, 0)

    @pl.when(h != 0)
    def _():
        queries(20, 24, 20)


def pack(step, sc, *parts):
    def body(*refs):
        pack_body(step, *refs)

    return pl.pallas_call(
        body,
        in_specs=[SM] + [VM] * len(parts),
        out_specs=VM,
        out_shape=jax.ShapeDtypeStruct((8, 5, ROWS, HD), BF),
        scratch_shapes=[pltpu.VMEM((20, ROWS, HD), BF)],
        compiler_params=params(8),
        name="pack_heads",
    )(sc, *parts)


QROWS = 4 * 3 * HALF


def attend_body(step, parts, chunk, block, last, sc, q, *refs):
    blocks, refs = refs[:parts], refs[parts:]
    if last:
        top_in, acc_in, out, qs, ks, vs = refs
    else:
        top_out, acc_out, qs, ks, vs = refs
    keys = ks.shape[0] // SLOTS
    ranks = [rank_of(sc, t, step) for t in range(SLOTS)]
    at = 0
    for ref in blocks:
        for b in range(ref.shape[0]):
            for j in range(SLOTS):
                rows = slice(j * HALF, (j + 1) * HALF)
                to = pl.ds(pl.multiple_of(ranks[j] * keys + at * HALF, HALF), HALF)
                ks[to, :] = ref[b, 0, rows, :]
                vs[to, :HD] = ref[b, 1, rows, :]
            at += 1
    vs[:, HD:] = jnp.ones((SLOTS * keys, HD), BF)
    factor = LOG2E / math.sqrt(HD)
    for c in range(4):
        for m in range(3):
            both = ((q[c, m].astype(F32) + q[4 + c, m].astype(F32)) * factor).astype(BF)
            for j in range(SLOTS):
                to = pl.ds(pl.multiple_of(ranks[j] * QROWS + (c * 3 + m) * HALF, HALF), HALF)
                qs[to, :] = both[j * HALF : (j + 1) * HALF]

    def some_rows(index, _):
        r = pl.multiple_of(index * block, block)
        rows = pl.ds(r, block)

        def scores_of(rank, n, size):
            return lax.dot_general(
                qs[pl.ds(rank * QROWS + r, block), :], ks[n : n + size, :],
                (((1,), (1,)), ((), ())), preferred_element_type=F32,
            )

        todo = []
        for rank in reversed(range(SLOTS)):
            span = (rank + 1) * keys
            todo += [(rank, n, min(chunk, span - n)) for n in range(0, span, chunk)]
        ahead = scores_of(*todo[0])
        for x, (rank, n, size) in enumerate(todo):
            scores = ahead
            if n == 0 and last:
                old, total = top_in[rank, rows], acc_in[rank, rows]
            if x + 1 < len(todo):
                ahead = scores_of(*todo[x + 1])
            new = jnp.max(scores, axis=-1, keepdims=True)
            fresh = n == 0 and not last
            new = jnp.broadcast_to(new, (block, HD)) if fresh else jnp.maximum(old, new)
            weights = jnp.exp2(scores - new[:, :1]).astype(BF)
            part = jnp.dot(weights, vs[n : n + size, :], preferred_element_type=F32)
            if fresh:
                total = part
            else:
                shrink = jnp.exp2(old - new)
                total = total * jnp.concatenate([shrink, shrink], axis=1) + part
            old = new
            if n + size < (rank + 1) * keys:
                continue
            if not last:
                top_out[rank, rows] = new
                acc_out[rank, rows] = total
                continue
            res = (total[:, :HD] / total[:, HD:]).astype(BF)
            slot = jnp.int32(0)
            for j in range(1, SLOTS):
                slot = jnp.where(ranks[j] == rank, j, slot)
            to = pl.ds(pl.multiple_of(slot * HALF, HALF), HALF)
            for k in range(block // HALF):
                head = index * (block // HALF) + k
                out[head, to, :] = res[k * HALF : (k + 1) * HALF]
                out[12 + head, to, :] = res[k * HALF : (k + 1) * HALF]
        return 0

    lax.fori_loop(0, QROWS // block, some_rows, 0)


def attend(step, sc, q, blocks, chunk, block, state=None):
    last = state is not None
    keys = sum(b.shape[0] for b in blocks) * HALF

    def body(*refs):
        attend_body(step, len(blocks), chunk, block, last, *refs)

    scratch = [
        pltpu.VMEM((SLOTS * QROWS, HD), BF),
        pltpu.VMEM((SLOTS * keys, HD), BF),
        pltpu.VMEM((SLOTS * keys, 2 * HD), BF),
    ]
    if last:
        out_shape = jax.ShapeDtypeStruct((24, ROWS, HD), BF)
    else:
        out_shape = [
            jax.ShapeDtypeStruct((SLOTS, QROWS, HD), F32),
            jax.ShapeDtypeStruct((SLOTS, QROWS, 2 * HD), F32),
        ]
    pairs = 10 * QROWS * keys
    return pl.pallas_call(
        body,
        in_specs=[SM] + [VM] * (1 + len(blocks) + (2 if last else 0)),
        out_specs=VM if last else [VM, VM],
        out_shape=out_shape,
        scratch_shapes=scratch,
        compiler_params=params(20 if last else 12),
        cost_estimate=pl.CostEstimate(
            flops=pairs * HD * 8, bytes_accessed=8 * 10**6, transcendentals=pairs
        ),
        name="span_attention_end" if last else "span_attention_begin",
    )(sc, q, *blocks, *(state or ()))


def out_body(step, sc, mine, ada, w, w_pair, out, attn):
    s = sc[8]
    for m in range(24):
        attn[:, m * HD : (m + 1) * HD] = mine[m // 3, m % 3]
    for k, weights in enumerate((w, w_pair)):
        product = jnp.dot(attn[...], weights[...], preferred_element_type=F32)
        for t in range(SLOTS):
            gate = ada[level_of(sc, t, step), 2:3, col_of(s ^ k)]
            piece = (product[t * HALF : (t + 1) * HALF] * gate).astype(BF)
            if step == 0:
                out[k, t * HALF : (t + 1) * HALF, :] = piece
            else:
                out[s ^ t, k] = piece


def out_projection(step, sc, mine, ada, w, w_pair):
    shape = (2, ROWS, COLS) if step == 0 else (SLOTS, 2, HALF, COLS)

    def body(*refs):
        out_body(step, *refs)

    return pl.pallas_call(
        body,
        in_specs=[SM] + [VM] * 4,
        out_specs=VM,
        out_shape=jax.ShapeDtypeStruct(shape, BF),
        scratch_shapes=[pltpu.VMEM((ROWS, WIDTH), BF)],
        compiler_params=params(10),
        cost_estimate=pl.CostEstimate(flops=2 * 10**9, bytes_accessed=6 * 10**6, transcendentals=0),
        name="out_projection",
    )(sc, mine, ada, w, w_pair)


def finish_body(sc, vel, fin, theirs, r0, r1, r2, r3, out, done):
    s = sc[8]
    i = s % 2
    halves = [pl.ds(pl.multiple_of((i ^ a) * HALF, HALF), HALF) for a in range(2)]
    out[0, halves[0], :] = vel[...]
    out[0, halves[1], :] = theirs[:, :WIDTH]
    done[halves[0], :] = fin[...]
    done[halves[1], :] = theirs[:, WIDTH:]
    for k, r in enumerate((r0, r1, r2, r3)):
        for c in range(2):
            out[1, halves[k % 2], col_of(s ^ k ^ c)] = r[c]


def finish(sc, vel, fin, theirs, rs):
    return pl.pallas_call(
        finish_body,
        in_specs=[SM] + [VM] * 7,
        out_specs=[VM, VM],
        out_shape=[
            jax.ShapeDtypeStruct((2, TOK, WIDTH), BF),
            jax.ShapeDtypeStruct((TOK, COLS), BF),
        ],
        compiler_params=params(8),
        name="collect_velocity",
    )(sc, vel, fin, theirs, *rs)


def begin_keys(low, high):
    low_y = move(low, y=2)
    high_z = [move(high, z=k) for k in (1, -1, 2)]
    early = jnp.concatenate([low, high, low_y, *high_z])
    lows = jnp.concatenate([low, low_y])
    highs = jnp.concatenate([high, *high_z])
    late = [move(lows, z=k) for k in (1, -1, 2)] + [move(highs, y=2)]
    return early, late


def both_cores(x):
    return [x, move(x, i=1)]


def after(x, *others):
    return lax.optimization_barrier((x, *others))


def shards(latents, fresh, span_ids, noise_step, ada_table, w_qkv, w_out):
    pos = lax.axis_index("slot").astype(jnp.int32).reshape(1)
    sc = jnp.concatenate([span_ids, noise_step, pos])
    own = latents[0]

    def beside(x, other):
        x, other = after(x, other)
        other = move(other, i=1)
        return after(exchange(x), other)

    def attention(step, got):
        early, late = begin_keys(got[4:6, 3:], got[6:, 3:])
        state = attend(step, sc, got, both_cores(early), 768, 192)
        late, state = after(late, state)
        late = jnp.concatenate(late)
        attn = attend(step, sc, got, both_cores(late), 1280, 192, state)
        return attn.reshape(8, 3, ROWS, HD)

    far = move(own, h=1)
    near = move(own, i=1)
    a = first_projection(sc, (own, near), 0, ada_table, w_qkv)
    far, a = after(far, a)
    far_near = move(far, i=1)
    b = first_projection(sc, (far, far_near), 2, ada_table, w_qkv)
    xs = (own, near, far, far_near)

    packed = pack(0, sc, a[0], b[0], move(a[1], i=1), move(b[1], i=1))
    got, w_out_pair = beside(packed, w_out)
    attn, w_pair = beside(attention(0, got), w_qkv)
    vel = out_projection(0, sc, attn, ada_table, w_out, w_out_pair)
    mine, other, vel, fin, theirs = second_projection(
        sc, xs, vel, move(vel, h=1), fresh, ada_table, w_qkv, w_pair
    )
    attn = attention(1, exchange(pack(1, sc, mine, other)))
    attn, theirs = after(exchange(attn), theirs)
    theirs = move(theirs, i=1)
    out = out_projection(1, sc, attn, ada_table, w_out, w_out_pair)
    rs = [out[0], move(out[1], i=1), move(out[2], h=1), move(out[3], h=1, i=1)]
    vel, fin = finish(sc, vel, fin, theirs, rs)
    return vel[:, None], fin


def solution(mesh):
    in_specs = (
        P("slot", "ctx", None),
        P("ctx", None),
        P(),
        P(),
        P(),
        P(None, "slot"),
        P(None, "slot"),
    )
    out_specs = (P(None, "slot", "ctx", None), P("ctx", "slot"))
    return jax.shard_map(shards, mesh=mesh, in_specs=in_specs, out_specs=out_specs, check_vma=False)
```

profile of v0, /device:TPU:1, one launch (start us, length us, event | category | flops | bytes accessed | tf_op | source)
XLA Modules:
  0.0 209.8 jit_solution(18252767505195903714)
XLA Ops:
  2.1 2.8 %collective-permute-start.1 = (bf16[64,3072]{1,0:T(8,128)(2,1)}, bf16[64,3072]{1,0:T(8,128)(2,1)S(1)}, u32[]{:S(2)}, u32[]{:S(2)}) collective-permute-start(bf16[64,3072]{1,0:T(8,128)(2,1)} %bitcast.20), channel_id=1, source_target_pairs={{0,64},{1,65},{2,66},{3,67},{4,68},{5,69},{6,70},{7,71},{8,72},{9,... | collective-permute-start | bytes 1179656 | tf_op jit(solution)/shard_map/ppermute | solution.py:45
  5.7 3.2 %copy-done = bf16[3072,1280]{1,0:T(8,128)(2,1)S(1)} copy-done((bf16[3072,1280]{1,0:T(8,128)(2,1)S(1)}, bf16[3072,1280]{1,0:T(8,128)(2,1)}, u32[]{:S(2)}) %copy-start) | copy-done | bytes 7864344
  21.9 22.5 %all_to_all.20.refs_1_ = bf16[8,5,128,128]{3,2,1,0:T(8,128)(2,1)S(1)} all-to-all(bf16[8,5,128,128]{3,2,1,0:T(8,128)(2,1)S(1)} %pack_heads.2), channel_id=1, replica_groups={{0,1,4,5,64,65,68,69},{2,3,6,7,66,67,70,71},{8,9,12,13,72,73,76,77},{10..., dimensions={0} | all-to-all | bytes 2621440 | tf_op jit(solution)/shard_map/all_to_all | solution.py:65
  44.4 3.7 %collective-permute-start.12 = (bf16[2,2,128,128]{3,2,1,0:T(8,128)(2,1)S(1)}, bf16[2,2,128,128]{3,2,1,0:T(8,128)(2,1)S(1)}, u32[]{:S(2)}, u32[]{:S(2)}) collective-permute-start(bf16[2,2,128,128]{3,2,1,0:T(8,128)(2,1)S(1)} %get-tuple-element.86), channel_id=1, source_target_pairs={{0,16},{1,17},{2,18},{3,19},{4,20},{5,21},{6,22},{7,23},{8,24},{9,... | collective-permute-start | bytes 393224 | tf_op jit(solution)/shard_map/ppermute | solution.py:45
  49.5 2.6 %collective-permute-start.6 = (bf16[2,2,128,128]{3,2,1,0:T(8,128)(2,1)S(1)}, bf16[2,2,128,128]{3,2,1,0:T(8,128)(2,1)S(1)}, u32[]{:S(2)}, u32[]{:S(2)}) collective-permute-start(bf16[2,2,128,128]{3,2,1,0:T(8,128)(2,1)S(1)} %get-tuple-element.87), channel_id=1, source_target_pairs={{0,2},{1,3},{2,0},{3,1},{4,6},{5,7},{6,4},{7,5},{8,10},{9,11},{10,... | collective-permute-start | bytes 393224 | tf_op jit(solution)/shard_map/ppermute | solution.py:45
  52.2 2.7 %collective-permute-done.6 = bf16[2,2,128,128]{3,2,1,0:T(8,128)(2,1)S(1)} collective-permute-done((bf16[2,2,128,128]{3,2,1,0:T(8,128)(2,1)S(1)}, bf16[2,2,128,128]{3,2,1,0:T(8,128)(2,1)S(1)}, u32[]{:S(2)}, u32[]{:S(2)}) %collective-permute-start.6) | collective-permute-done | bytes 131104 | tf_op jit(solution)/shard_map/ppermute | solution.py:45
  55.0 3.6 %collective-permute-start.14 = (bf16[12,2,128,128]{3,2,1,0:T(8,128)(2,1)S(1)}, bf16[12,2,128,128]{3,2,1,0:T(8,128)(2,1)S(1)}, u32[]{:S(2)}, u32[]{:S(2)}) collective-permute-start(bf16[12,2,128,128]{3,2,1,0:T(8,128)(2,1)S(1)} %constant_dynamic-update-slice_fusion.refs_2_), channel_id=1, source_target_pairs={{0,32},{1,33},{2,34},{3,35},{4,36},{5,37},{6,38},{7,39},{8,40},{9,... | collective-permute-start | bytes 2359304 | tf_op jit(solution)/shard_map/ppermute | solution.py:45
  58.7 2.7 %collective-permute-start.13 = (bf16[8,2,128,128]{3,2,1,0:T(8,128)(2,1)S(1)}, bf16[8,2,128,128]{3,2,1,0:T(8,128)(2,1)S(1)}, u32[]{:S(2)}, u32[]{:S(2)}) collective-permute-start(bf16[8,2,128,128]{3,2,1,0:T(8,128)(2,1)S(1)} %pad_maximum_fusion), channel_id=1, source_target_pairs={{0,2},{1,3},{2,0},{3,1},{4,6},{5,7},{6,4},{7,5},{8,10},{9,11},{10,... | collective-permute-start | bytes 1572872 | tf_op jit(solution)/shard_map/ppermute | solution.py:45
  64.6 5.0 %span_attention_begin.2 = (f32[4,384,128]{2,1,0:T(8,128)S(1)}, f32[4,384,256]{2,1,0:T(8,128)S(1)}) custom-call(s32[9]{0:T(128)S(1)} %pad_add_fusion.refs_0_.sc, bf16[8,5,128,128]{3,2,1,0:T(8,128)(2,1)S(1)} %all_to_all.20.refs_1_, bf16[12,2,128,128]{3,2,1,0:T(8,128)(2,1)S(1)} %constant_dynamic-update-slice_fusion.refs_2_, ...), custom_call_target="tpu_custom_call" | custom-call | flops 3019898880 | bytes 8000000 | tf_op jit(solution)/shard_map/span_attention_begin/pallas_call | solution.py:358
  70.6 4.9 %collective-permute-done.8 = bf16[4,2,128,128]{3,2,1,0:T(8,128)(2,1)S(1)} collective-permute-done((bf16[4,2,128,128]{3,2,1,0:T(8,128)(2,1)S(1)}, bf16[4,2,128,128]{3,2,1,0:T(8,128)(2,1)S(1)}, u32[]{:S(2)}, u32[]{:S(2)}) %collective-permute-start.8) | collective-permute-done | bytes 262176 | tf_op jit(solution)/shard_map/ppermute | solution.py:45
  77.8 2.7 %collective-permute-done.15.refs_3_ = bf16[20,2,128,128]{3,2,1,0:T(8,128)(2,1)S(1)} collective-permute-done((bf16[20,2,128,128]{3,2,1,0:T(8,128)(2,1)S(1)}, bf16[20,2,128,128]{3,2,1,0:T(8,128)(2,1)S(1)}, u32[]{:S(2)}, u32[]{:S(2)}) %collective-permute-start.15) | collective-permute-done | bytes 1310752 | tf_op jit(solution)/shard_map/ppermute | solution.py:45
  80.5 7.7 %span_attention_end.2 = bf16[24,128,128]{2,1,0:T(8,128)(2,1)S(1)} custom-call(s32[9]{0:T(128)S(1)} %pad_add_fusion.refs_0_.sc, bf16[8,5,128,128]{3,2,1,0:T(8,128)(2,1)S(1)} %all_to_all.20.refs_1_, bf16[20,2,128,128]{3,2,1,0:T(8,128)(2,1)S(1)} %constant_dynamic-update-slice_fusion.4.refs_2_, bf16[20,2,128,128]{3,2,1,0:T(8,128)(2,1)S(1)} %collective-permute-done.15.refs_3_, ...), custom_call_target="tpu_custom_call" | custom-call | flops 5033164800 | bytes 8000000 | tf_op jit(solution)/shard_map/span_attention_end/pallas_call | solution.py:358
  88.6 14.7 %all_to_all.21.refs_1_ = bf16[8,3,128,128]{3,2,1,0:T(8,128)(2,1)S(1)} all-to-all(bf16[8,3,128,128]{3,2,1,0:T(8,128)(2,1)S(1)} %bitcast.17), channel_id=1, replica_groups={{0,1,4,5,64,65,68,69},{2,3,6,7,66,67,70,71},{8,9,12,13,72,73,76,77},{10..., dimensions={0} | all-to-all | bytes 1572864 | tf_op jit(solution)/shard_map/all_to_all | solution.py:65
  106.1 10.3 %collective-permute-done.17.away = bf16[2,128,768]{2,1,0:T(8,128)(2,1)S(1)} collective-permute-done((bf16[2,128,768]{2,1,0:T(8,128)(2,1)S(1)}, bf16[2,128,768]{2,1,0:T(8,128)(2,1)S(1)}, u32[]{:S(2)}, u32[]{:S(2)}) %collective-permute-start.17) | collective-permute-done | bytes 393248 | tf_op jit(solution)/shard_map/ppermute | solution.py:45
  116.4 3.9 %advance_modulate_project.1 = (bf16[10,128,128]{2,1,0:T(8,128)(2,1)S(1)}, bf16[10,128,128]{2,1,0:T(8,128)(2,1)S(1)}, bf16[32,3072]{1,0:T(8,128)(2,1)S(1)}, bf16[...) custom-call(s32[9]{0:T(128)S(1)} %pad_add_fusion.refs_0_.sc, bf16[64,3072]{1,0:T(8,128)(2,1)S(1)} %bitcast.22, ...), custom_call_target="tpu_custom_call" | custom-call | flops 4000000000 | bytes 10000000 | tf_op jit(solution)/shard_map/advance_modulate_project/pallas_call | solution.py:198
  121.0 18.7 %all_to_all.22.refs_1_ = bf16[8,5,128,128]{3,2,1,0:T(8,128)(2,1)S(1)} all-to-all(bf16[8,5,128,128]{3,2,1,0:T(8,128)(2,1)S(1)} %pack_heads.3), channel_id=1, replica_groups={{0,1,4,5,64,65,68,69},{2,3,6,7,66,67,70,71},{8,9,12,13,72,73,76,77},{10..., dimensions={0} | all-to-all | bytes 2621440 | tf_op jit(solution)/shard_map/all_to_all | solution.py:65
  144.7 3.8 %collective-permute-done.18 = bf16[2,2,128,128]{3,2,1,0:T(8,128)(2,1)S(1)} collective-permute-done((bf16[2,2,128,128]{3,2,1,0:T(8,128)(2,1)S(1)}, bf16[2,2,128,128]{3,2,1,0:T(8,128)(2,1)S(1)}, u32[]{:S(2)}, u32[]{:S(2)}) %collective-permute-start.18) | collective-permute-done | bytes 131104 | tf_op jit(solution)/shard_map/ppermute | solution.py:45
  149.5 4.2 %collective-permute-start.26 = (bf16[12,2,128,128]{3,2,1,0:T(8,128)(2,1)S(1)}, bf16[12,2,128,128]{3,2,1,0:T(8,128)(2,1)S(1)}, u32[]{:S(2)}, u32[]{:S(2)}) collective-permute-start(bf16[12,2,128,128]{3,2,1,0:T(8,128)(2,1)S(1)} %constant_dynamic-update-slice_fusion.8.refs_2_), channel_id=1, source_target_pairs={{0,32},{1,33},{2,34},{3,35},{4,36},{5,37},{6,38},{7,39},{8,40},{9,... | collective-permute-start | bytes 2359304 | tf_op jit(solution)/shard_map/ppermute | solution.py:45
  158.9 5.0 %span_attention_begin.3 = (f32[4,384,128]{2,1,0:T(8,128)S(1)}, f32[4,384,256]{2,1,0:T(8,128)S(1)}) custom-call(s32[9]{0:T(128)S(1)} %pad_add_fusion.refs_0_.sc, bf16[8,5,128,128]{3,2,1,0:T(8,128)(2,1)S(1)} %all_to_all.22.refs_1_, bf16[12,2,128,128]{3,2,1,0:T(8,128)(2,1)S(1)} %constant_dynamic-update-slice_fusion.8.refs_2_, ...), custom_call_target="tpu_custom_call" | custom-call | flops 3019898880 | bytes 8000000 | tf_op jit(solution)/shard_map/span_attention_begin/pallas_call | solution.py:358
  164.6 6.2 %collective-permute-done.20 = bf16[4,2,128,128]{3,2,1,0:T(8,128)(2,1)S(1)} collective-permute-done((bf16[4,2,128,128]{3,2,1,0:T(8,128)(2,1)S(1)}, bf16[4,2,128,128]{3,2,1,0:T(8,128)(2,1)S(1)}, u32[]{:S(2)}, u32[]{:S(2)}) %collective-permute-start.20) | collective-permute-done | bytes 262176 | tf_op jit(solution)/shard_map/ppermute | solution.py:45
  172.1 2.7 %collective-permute-done.27.refs_3_ = bf16[20,2,128,128]{3,2,1,0:T(8,128)(2,1)S(1)} collective-permute-done((bf16[20,2,128,128]{3,2,1,0:T(8,128)(2,1)S(1)}, bf16[20,2,128,128]{3,2,1,0:T(8,128)(2,1)S(1)}, u32[]{:S(2)}, u32[]{:S(2)}) %collective-permute-start.27) | collective-permute-done | bytes 1310752 | tf_op jit(solution)/shard_map/ppermute | solution.py:45
  174.8 7.7 %span_attention_end.3 = bf16[24,128,128]{2,1,0:T(8,128)(2,1)S(1)} custom-call(s32[9]{0:T(128)S(1)} %pad_add_fusion.refs_0_.sc, bf16[8,5,128,128]{3,2,1,0:T(8,128)(2,1)S(1)} %all_to_all.22.refs_1_, bf16[20,2,128,128]{3,2,1,0:T(8,128)(2,1)S(1)} %constant_dynamic-update-slice_fusion.12.refs_2_, bf16[20,2,128,128]{3,2,1,0:T(8,128)(2,1)S(1)} %collective-permute-done.27.refs_3_, ...), custom_call_target="tpu_custom_call" | custom-call | flops 5033164800 | bytes 8000000 | tf_op jit(solution)/shard_map/span_attention_end/pallas_call | solution.py:358
  182.5 14.3 %all_to_all.23.refs_1_ = bf16[8,3,128,128]{3,2,1,0:T(8,128)(2,1)S(1)} all-to-all(bf16[8,3,128,128]{3,2,1,0:T(8,128)(2,1)S(1)} %bitcast.18), channel_id=1, replica_groups={{0,1,4,5,64,65,68,69},{2,3,6,7,66,67,70,71},{8,9,12,13,72,73,76,77},{10..., dimensions={0} | all-to-all | bytes 1572864 | tf_op jit(solution)/shard_map/all_to_all | solution.py:65
  204.2 2.9 %collective-permute-done.31.r3 = bf16[2,32,768]{2,1,0:T(8,128)(2,1)S(1)} collective-permute-done((bf16[2,32,768]{2,1,0:T(8,128)(2,1)S(1)}, bf16[2,32,768]{2,1,0:T(8,128)(2,1)S(1)}, u32[]{:S(2)}, u32[]{:S(2)}) %collective-permute-start.31) | collective-permute-done | bytes 98336 | tf_op jit(solution)/shard_map/ppermute | solution.py:45
  (101 shorter events, 50.4 us)
Async XLA Ops:
  2.1 12.4 %collective-permute-start.1 = (bf16[64,3072]{1,0:T(8,128)(2,1)}, bf16[64,3072]{1,0:T(8,128)(2,1)S(1)}, u32[]{:S(2)}, u32[]{:S(2)}) collective-permute-start(bf16[64,3072]{1,0:T(8,128)(2,1)} %bitcast.20), channel_id=1, source_target_pairs={{0,64},{1,65},{2,66},{3,67},{4,68},{5,69},{6,70},{7,71},{8,72},{9,... | collective-permute-start | bytes 1179656 | tf_op jit(solution)/shard_map/ppermute | solution.py:45
  21.4 22.9 %collective-permute-start.5 = (bf16[3072,768]{1,0:T(8,128)(2,1)S(1)}, bf16[3072,768]{1,0:T(8,128)(2,1)S(1)}, u32[]{:S(2)}, u32[]{:S(2)}) collective-permute-start(bf16[3072,768]{1,0:T(8,128)(2,1)S(1)} %bitcast.16), channel_id=1, source_target_pairs={{0,32},{1,33},{2,34},{3,35},{4,36},{5,37},{6,38},{7,39},{8,40},{9,... | collective-permute-start | bytes 14155784 | tf_op jit(solution)/shard_map/ppermute | solution.py:45
  44.4 10.6 %collective-permute-start.12 = (bf16[2,2,128,128]{3,2,1,0:T(8,128)(2,1)S(1)}, bf16[2,2,128,128]{3,2,1,0:T(8,128)(2,1)S(1)}, u32[]{:S(2)}, u32[]{:S(2)}) collective-permute-start(bf16[2,2,128,128]{3,2,1,0:T(8,128)(2,1)S(1)} %get-tuple-element.86), channel_id=1, source_target_pairs={{0,16},{1,17},{2,18},{3,19},{4,20},{5,21},{6,22},{7,23},{8,24},{9,... | collective-permute-start | bytes 393224 | tf_op jit(solution)/shard_map/ppermute | solution.py:45
  48.1 6.9 %collective-permute-start.11 = (bf16[2,2,128,128]{3,2,1,0:T(8,128)(2,1)S(1)}, bf16[2,2,128,128]{3,2,1,0:T(8,128)(2,1)S(1)}, u32[]{:S(2)}, u32[]{:S(2)}) collective-permute-start(bf16[2,2,128,128]{3,2,1,0:T(8,128)(2,1)S(1)} %get-tuple-element.86), channel_id=1, source_target_pairs={{0,24},{1,25},{2,26},{3,27},{4,28},{5,29},{6,30},{7,31},{8,0},{9,1... | collective-permute-start | bytes 393224 | tf_op jit(solution)/shard_map/ppermute | solution.py:45
  48.5 6.3 %collective-permute-start.10 = (bf16[2,2,128,128]{3,2,1,0:T(8,128)(2,1)S(1)}, bf16[2,2,128,128]{3,2,1,0:T(8,128)(2,1)S(1)}, u32[]{:S(2)}, u32[]{:S(2)}) collective-permute-start(bf16[2,2,128,128]{3,2,1,0:T(8,128)(2,1)S(1)} %get-tuple-element.86), channel_id=1, source_target_pairs={{0,8},{1,9},{2,10},{3,11},{4,12},{5,13},{6,14},{7,15},{8,16},{9,17... | collective-permute-start | bytes 393224 | tf_op jit(solution)/shard_map/ppermute | solution.py:45
  55.0 9.6 %collective-permute-start.14 = (bf16[12,2,128,128]{3,2,1,0:T(8,128)(2,1)S(1)}, bf16[12,2,128,128]{3,2,1,0:T(8,128)(2,1)S(1)}, u32[]{:S(2)}, u32[]{:S(2)}) collective-permute-start(bf16[12,2,128,128]{3,2,1,0:T(8,128)(2,1)S(1)} %constant_dynamic-update-slice_fusion.refs_2_), channel_id=1, source_target_pairs={{0,32},{1,33},{2,34},{3,35},{4,36},{5,37},{6,38},{7,39},{8,40},{9,... | collective-permute-start | bytes 2359304 | tf_op jit(solution)/shard_map/ppermute | solution.py:45
  58.7 18.2 %collective-permute-start.13 = (bf16[8,2,128,128]{3,2,1,0:T(8,128)(2,1)S(1)}, bf16[8,2,128,128]{3,2,1,0:T(8,128)(2,1)S(1)}, u32[]{:S(2)}, u32[]{:S(2)}) collective-permute-start(bf16[8,2,128,128]{3,2,1,0:T(8,128)(2,1)S(1)} %pad_maximum_fusion), channel_id=1, source_target_pairs={{0,2},{1,3},{2,0},{3,1},{4,6},{5,7},{6,4},{7,5},{8,10},{9,11},{10,... | collective-permute-start | bytes 1572872 | tf_op jit(solution)/shard_map/ppermute | solution.py:45
  61.4 9.2 %collective-permute-start.9 = (bf16[4,2,128,128]{3,2,1,0:T(8,128)(2,1)S(1)}, bf16[4,2,128,128]{3,2,1,0:T(8,128)(2,1)S(1)}, u32[]{:S(2)}, u32[]{:S(2)}) collective-permute-start(bf16[4,2,128,128]{3,2,1,0:T(8,128)(2,1)S(1)} %pad_maximum_fusion.2), channel_id=1, source_target_pairs={{0,16},{1,17},{2,18},{3,19},{4,20},{5,21},{6,22},{7,23},{8,24},{9,... | collective-permute-start | bytes 786440 | tf_op jit(solution)/shard_map/ppermute | solution.py:45
  62.3 13.2 %collective-permute-start.8 = (bf16[4,2,128,128]{3,2,1,0:T(8,128)(2,1)S(1)}, bf16[4,2,128,128]{3,2,1,0:T(8,128)(2,1)S(1)}, u32[]{:S(2)}, u32[]{:S(2)}) collective-permute-start(bf16[4,2,128,128]{3,2,1,0:T(8,128)(2,1)S(1)} %pad_maximum_fusion.2), channel_id=1, source_target_pairs={{0,24},{1,25},{2,26},{3,27},{4,28},{5,29},{6,30},{7,31},{8,0},{9,1... | collective-permute-start | bytes 786440 | tf_op jit(solution)/shard_map/ppermute | solution.py:45
  64.6 12.2 %collective-permute-start.7 = (bf16[4,2,128,128]{3,2,1,0:T(8,128)(2,1)S(1)}, bf16[4,2,128,128]{3,2,1,0:T(8,128)(2,1)S(1)}, u32[]{:S(2)}, u32[]{:S(2)}) collective-permute-start(bf16[4,2,128,128]{3,2,1,0:T(8,128)(2,1)S(1)} %pad_maximum_fusion.2), channel_id=1, source_target_pairs={{0,8},{1,9},{2,10},{3,11},{4,12},{5,13},{6,14},{7,15},{8,16},{9,17... | collective-permute-start | bytes 786440 | tf_op jit(solution)/shard_map/ppermute | solution.py:45
  88.2 15.2 %collective-permute-start.16 = (bf16[3072,1280]{1,0:T(8,128)(2,1)S(1)}, bf16[3072,1280]{1,0:T(8,128)(2,1)S(1)}, u32[]{:S(2)}, u32[]{:S(2)}) collective-permute-start(bf16[3072,1280]{1,0:T(8,128)(2,1)S(1)} %copy-done.1), channel_id=1, source_target_pairs={{0,32},{1,33},{2,34},{3,35},{4,36},{5,37},{6,38},{7,39},{8,40},{9,... | collective-permute-start | bytes 23592968 | tf_op jit(solution)/shard_map/ppermute | solution.py:45
  105.4 11.0 %collective-permute-start.17 = (bf16[2,128,768]{2,1,0:T(8,128)(2,1)S(1)}, bf16[2,128,768]{2,1,0:T(8,128)(2,1)S(1)}, u32[]{:S(2)}, u32[]{:S(2)}) collective-permute-start(bf16[2,128,768]{2,1,0:T(8,128)(2,1)S(1)} %out_projection.2.here), channel_id=1, source_target_pairs={{0,64},{1,65},{2,66},{3,67},{4,68},{5,69},{6,70},{7,71},{8,72},{9,... | collective-permute-start | bytes 1179656 | tf_op jit(solution)/shard_map/ppermute | solution.py:45
  139.7 9.7 %collective-permute-start.24 = (bf16[2,2,128,128]{3,2,1,0:T(8,128)(2,1)S(1)}, bf16[2,2,128,128]{3,2,1,0:T(8,128)(2,1)S(1)}, u32[]{:S(2)}, u32[]{:S(2)}) collective-permute-start(bf16[2,2,128,128]{3,2,1,0:T(8,128)(2,1)S(1)} %get-tuple-element.84), channel_id=1, source_target_pairs={{0,16},{1,17},{2,18},{3,19},{4,20},{5,21},{6,22},{7,23},{8,24},{9,... | collective-permute-start | bytes 393224 | tf_op jit(solution)/shard_map/ppermute | solution.py:45
  141.2 8.2 %collective-permute-start.23 = (bf16[2,2,128,128]{3,2,1,0:T(8,128)(2,1)S(1)}, bf16[2,2,128,128]{3,2,1,0:T(8,128)(2,1)S(1)}, u32[]{:S(2)}, u32[]{:S(2)}) collective-permute-start(bf16[2,2,128,128]{3,2,1,0:T(8,128)(2,1)S(1)} %get-tuple-element.84), channel_id=1, source_target_pairs={{0,24},{1,25},{2,26},{3,27},{4,28},{5,29},{6,30},{7,31},{8,0},{9,1... | collective-permute-start | bytes 393224 | tf_op jit(solution)/shard_map/ppermute | solution.py:45
  142.9 6.5 %collective-permute-start.22 = (bf16[2,2,128,128]{3,2,1,0:T(8,128)(2,1)S(1)}, bf16[2,2,128,128]{3,2,1,0:T(8,128)(2,1)S(1)}, u32[]{:S(2)}, u32[]{:S(2)}) collective-permute-start(bf16[2,2,128,128]{3,2,1,0:T(8,128)(2,1)S(1)} %get-tuple-element.84), channel_id=1, source_target_pairs={{0,8},{1,9},{2,10},{3,11},{4,12},{5,13},{6,14},{7,15},{8,16},{9,17... | collective-permute-start | bytes 393224 | tf_op jit(solution)/shard_map/ppermute | solution.py:45
  142.9 5.6 %collective-permute-start.18 = (bf16[2,2,128,128]{3,2,1,0:T(8,128)(2,1)S(1)}, bf16[2,2,128,128]{3,2,1,0:T(8,128)(2,1)S(1)}, u32[]{:S(2)}, u32[]{:S(2)}) collective-permute-start(bf16[2,2,128,128]{3,2,1,0:T(8,128)(2,1)S(1)} %get-tuple-element.85), channel_id=1, source_target_pairs={{0,2},{1,3},{2,0},{3,1},{4,6},{5,7},{6,4},{7,5},{8,10},{9,11},{10,... | collective-permute-start | bytes 393224 | tf_op jit(solution)/shard_map/ppermute | solution.py:45
  149.5 9.4 %collective-permute-start.26 = (bf16[12,2,128,128]{3,2,1,0:T(8,128)(2,1)S(1)}, bf16[12,2,128,128]{3,2,1,0:T(8,128)(2,1)S(1)}, u32[]{:S(2)}, u32[]{:S(2)}) collective-permute-start(bf16[12,2,128,128]{3,2,1,0:T(8,128)(2,1)S(1)} %constant_dynamic-update-slice_fusion.8.refs_2_), channel_id=1, source_target_pairs={{0,32},{1,33},{2,34},{3,35},{4,36},{5,37},{6,38},{7,39},{8,40},{9,... | collective-permute-start | bytes 2359304 | tf_op jit(solution)/shard_map/ppermute | solution.py:45
  153.8 17.0 %collective-permute-start.25 = (bf16[8,2,128,128]{3,2,1,0:T(8,128)(2,1)S(1)}, bf16[8,2,128,128]{3,2,1,0:T(8,128)(2,1)S(1)}, u32[]{:S(2)}, u32[]{:S(2)}) collective-permute-start(bf16[8,2,128,128]{3,2,1,0:T(8,128)(2,1)S(1)} %pad_maximum_fusion.1), channel_id=1, source_target_pairs={{0,2},{1,3},{2,0},{3,1},{4,6},{5,7},{6,4},{7,5},{8,10},{9,11},{10,... | collective-permute-start | bytes 1572872 | tf_op jit(solution)/shard_map/ppermute | solution.py:45
  155.1 9.4 %collective-permute-start.21 = (bf16[4,2,128,128]{3,2,1,0:T(8,128)(2,1)S(1)}, bf16[4,2,128,128]{3,2,1,0:T(8,128)(2,1)S(1)}, u32[]{:S(2)}, u32[]{:S(2)}) collective-permute-start(bf16[4,2,128,128]{3,2,1,0:T(8,128)(2,1)S(1)} %pad_maximum_fusion.3), channel_id=1, source_target_pairs={{0,16},{1,17},{2,18},{3,19},{4,20},{5,21},{6,22},{7,23},{8,24},{9,... | collective-permute-start | bytes 786440 | tf_op jit(solution)/shard_map/ppermute | solution.py:45
  157.0 13.7 %collective-permute-start.20 = (bf16[4,2,128,128]{3,2,1,0:T(8,128)(2,1)S(1)}, bf16[4,2,128,128]{3,2,1,0:T(8,128)(2,1)S(1)}, u32[]{:S(2)}, u32[]{:S(2)}) collective-permute-start(bf16[4,2,128,128]{3,2,1,0:T(8,128)(2,1)S(1)} %pad_maximum_fusion.3), channel_id=1, source_target_pairs={{0,24},{1,25},{2,26},{3,27},{4,28},{5,29},{6,30},{7,31},{8,0},{9,1... | collective-permute-start | bytes 786440 | tf_op jit(solution)/shard_map/ppermute | solution.py:45
  158.7 12.1 %collective-permute-start.19 = (bf16[4,2,128,128]{3,2,1,0:T(8,128)(2,1)S(1)}, bf16[4,2,128,128]{3,2,1,0:T(8,128)(2,1)S(1)}, u32[]{:S(2)}, u32[]{:S(2)}) collective-permute-start(bf16[4,2,128,128]{3,2,1,0:T(8,128)(2,1)S(1)} %pad_maximum_fusion.3), channel_id=1, source_target_pairs={{0,8},{1,9},{2,10},{3,11},{4,12},{5,13},{6,14},{7,15},{8,16},{9,17... | collective-permute-start | bytes 786440 | tf_op jit(solution)/shard_map/ppermute | solution.py:45
  198.8 9.5 %collective-permute-start.28 = (bf16[32,3840]{1,0:T(8,128)(2,1)S(1)}, bf16[32,3840]{1,0:T(8,128)(2,1)S(1)}, u32[]{:S(2)}, u32[]{:S(2)}) collective-permute-start(bf16[32,3840]{1,0:T(8,128)(2,1)S(1)} %get-tuple-element.78), channel_id=1, source_target_pairs={{0,32},{1,33},{2,34},{3,35},{4,36},{5,37},{6,38},{7,39},{8,40},{9,... | collective-permute-start | bytes 737288 | tf_op jit(solution)/shard_map/ppermute | solution.py:45
  200.5 6.6 %collective-permute-start.31 = (bf16[2,32,768]{2,1,0:T(8,128)(2,1)S(1)}, bf16[2,32,768]{2,1,0:T(8,128)(2,1)S(1)}, u32[]{:S(2)}, u32[]{:S(2)}) collective-permute-start(bf16[2,32,768]{2,1,0:T(8,128)(2,1)S(1)} %get-tuple-element.88), channel_id=1, source_target_pairs={{0,96},{1,97},{2,98},{3,99},{4,100},{5,101},{6,102},{7,103},{8,104... | collective-permute-start | bytes 294920 | tf_op jit(solution)/shard_map/ppermute | solution.py:45
  201.7 6.6 %collective-permute-start.30 = (bf16[2,32,768]{2,1,0:T(8,128)(2,1)S(1)}, bf16[2,32,768]{2,1,0:T(8,128)(2,1)S(1)}, u32[]{:S(2)}, u32[]{:S(2)}) collective-permute-start(bf16[2,32,768]{2,1,0:T(8,128)(2,1)S(1)} %get-tuple-element.89), channel_id=1, source_target_pairs={{0,64},{1,65},{2,66},{3,67},{4,68},{5,69},{6,70},{7,71},{8,72},{9,... | collective-permute-start | bytes 294920 | tf_op jit(solution)/shard_map/ppermute | solution.py:45
  (17 other events, 96.6 us)
where the time goes:
time: 210 us
  blocking collectives  70.2 us (33%)
  starting transfers between devices  46.2 us (22%)
  waiting for transfers between devices  44.4 us (21%)
  Pallas kernels  41.2 us (20%)
  local copies, waits for them, and re-layouts  5.84 us (3%)
    all_to_all x4, blocking collectives, exchange(): lax.all_to_all(x, AXES, 0, 0, tiled=True, axis_index_groups=group_lists())  70.2 us
    ppermute x32, starting transfers between devices, move(): return lax.ppermute(x, AXES, pairs)  46.2 us
    ppermute x32, waiting for transfers between devices, move(): return lax.ppermute(x, AXES, pairs)  44.4 us
    pallas_call x4, Pallas kernels, attend(): pl.pallas_call(body, in_specs=[SM] + [VM] * (1 + len(blocks) + (2 if last...  25.4 us
    unnamed x32, local copies, waits for them, and re-layouts  5.6 us
    pallas_call x2, Pallas kernels, first_projection(): pl.pallas_call(body, in_specs=[SM] + [VM] * 4, out_specs=[VM] * 2, out_sh...  4.97 us
  transfers between devices with their start and end apart: 32, of which 16 were waited for; matrix products, arithmetic and copies ran while one was open for 1% of the time, Pallas kernels for 7%

commit v1 on v0

--- a/solution.py
+++ b/solution.py
@@ -209,7 +209,7 @@
 
 
 def pack_body(step, sc, *refs):
-    parts, (out, chip) = refs[:-2], refs[-2:]
+    parts, (out, last, chip) = refs[:-3], refs[-3:]
     i, h = sc[8] % 2, sc[8] // 2
     for k in range(2):
         to = pl.ds(10 * jnp.where(k == 0, i, 1 - i), 10)
@@ -219,24 +219,23 @@
         for n in range(2):
             at = pl.multiple_of((h ^ n) * PAIR, PAIR)
             chip[to, pl.ds(at, PAIR)] = parts[2 * k + n][...]
-    for g in range(8):
-        out[g, 3] = chip[4 + g]
-        out[g, 4] = chip[12 + g]
-
-    def queries(low, high, at):
-        for n in range(24):
-            if low <= n < high:
-                out[n // 3, n % 3] = chip[n - at]
-            else:
-                out[n // 3, n % 3] = jnp.zeros((ROWS, HD), BF)
+    nothing = jnp.zeros((ROWS, HD), BF)
+    last[0] = chip[11]
+    last[1] = chip[19]
 
     @pl.when(h == 0)
     def _():
-        queries(0, 20, 0)
+        for n in range(24):
+            out[n // 3, n % 3] = chip[n] if n < 20 else nothing
 
     @pl.when(h != 0)
     def _():
-        queries(20, 24, 20)
+        for g in range(7):
+            out[g, 0] = chip[4 + g]
+            out[g, 1] = chip[12 + g]
+            out[g, 2] = chip[0] if g == 6 else nothing
+        for m in range(3):
+            out[7, m] = chip[1 + m]
 
 
 def pack(step, sc, *parts):
@@ -246,8 +245,11 @@
     return pl.pallas_call(
         body,
         in_specs=[SM] + [VM] * len(parts),
-        out_specs=VM,
-        out_shape=jax.ShapeDtypeStruct((8, 5, ROWS, HD), BF),
+        out_specs=[VM, VM],
+        out_shape=[
+            jax.ShapeDtypeStruct((8, 3, ROWS, HD), BF),
+            jax.ShapeDtypeStruct((2, ROWS, HD), BF),
+        ],
         scratch_shapes=[pltpu.VMEM((20, ROWS, HD), BF)],
         compiler_params=params(8),
         name="pack_heads",
@@ -278,7 +280,11 @@
     factor = LOG2E / math.sqrt(HD)
     for c in range(4):
         for m in range(3):
-            both = ((q[c, m].astype(F32) + q[4 + c, m].astype(F32)) * factor).astype(BF)
+            near = q[c, m].astype(F32)
+            other = q[4 + c, m].astype(F32)
+            if m == 2:
+                near = near + other
+            both = (jnp.where(sc[9] == 7, other, near) * factor).astype(BF)
             for j in range(SLOTS):
                 to = pl.ds(pl.multiple_of(ranks[j] * QROWS + (c * 3 + m) * HALF, HALF), HALF)
                 qs[to, :] = both[j * HALF : (j + 1) * HALF]
@@ -402,6 +408,23 @@
     )(sc, mine, ada, w, w_pair)
 
 
+def hold(w):
+    def body(x, y, sem):
+        copy = pltpu.make_async_copy(x, y, sem)
+        copy.start()
+        copy.wait()
+
+    return pl.pallas_call(
+        body,
+        in_specs=[pl.BlockSpec(memory_space=pl.ANY)],
+        out_specs=VM,
+        out_shape=jax.ShapeDtypeStruct(w.shape, w.dtype),
+        scratch_shapes=[pltpu.SemaphoreType.DMA(())],
+        compiler_params=params(6),
+        name="hold_weights",
+    )(w)
+
+
 def finish_body(sc, vel, fin, theirs, r0, r1, r2, r3, out, done):
     s = sc[8]
     i = s % 2
@@ -429,6 +452,18 @@
     )(sc, vel, fin, theirs, *rs)
 
 
+def seventh(x):
+    out = []
+    for xl, yl in ((0, 0), (0, 1), (1, 0)):
+        pairs = []
+        for f in range(128):
+            d = where_is(f)
+            if (d["h"], d["xl"], d["y"] % 2) == (1, xl, yl):
+                pairs.append((f, flat_of(dict(d, xl=1, y=d["y"] // 2 * 2 + 1))))
+        out.append(lax.ppermute(x, AXES, pairs))
+    return out
+
+
 def begin_keys(low, high):
     low_y = move(low, y=2)
     high_z = [move(high, z=k) for k in (1, -1, 2)]
@@ -449,21 +484,24 @@
 
 def shards(latents, fresh, span_ids, noise_step, ada_table, w_qkv, w_out):
     pos = lax.axis_index("slot").astype(jnp.int32).reshape(1)
-    sc = jnp.concatenate([span_ids, noise_step, pos])
+    ctx = lax.axis_index("ctx").astype(jnp.int32).reshape(1)
+    group = 4 * (pos // 2) + ctx // 4 % 2 * 2 + ctx % 2
+    sc = jnp.concatenate([span_ids, noise_step, pos, group])
     own = latents[0]
 
-    def beside(x, other):
-        x, other = after(x, other)
-        other = move(other, i=1)
-        return after(exchange(x), other)
-
-    def attention(step, got):
-        early, late = begin_keys(got[4:6, 3:], got[6:, 3:])
+    def beside(x, *others):
+        return after(exchange(x), *others)
+
+    def attention(step, got, last, weights):
+        keys = jnp.where(group[0] == 7, jnp.stack(last), got[4:, :2])
+        early, late = begin_keys(keys[:2], keys[2:])
         state = attend(step, sc, got, both_cores(early), 768, 192)
-        late, state = after(late, state)
+        state, weights = after(state, weights)
+        weights = [hold(w) for w in weights]
+        late, state, weights = after(late, state, weights)
         late = jnp.concatenate(late)
         attn = attend(step, sc, got, both_cores(late), 1280, 192, state)
-        return attn.reshape(8, 3, ROWS, HD)
+        return attn.reshape(8, 3, ROWS, HD), weights
 
     far = move(own, h=1)
     near = move(own, i=1)
@@ -473,17 +511,22 @@
     b = first_projection(sc, (far, far_near), 2, ada_table, w_qkv)
     xs = (own, near, far, far_near)
 
-    packed = pack(0, sc, a[0], b[0], move(a[1], i=1), move(b[1], i=1))
-    got, w_out_pair = beside(packed, w_out)
-    attn, w_pair = beside(attention(0, got), w_qkv)
-    vel = out_projection(0, sc, attn, ada_table, w_out, w_out_pair)
+    packed, last = pack(0, sc, a[0], b[0], move(a[1], i=1), move(b[1], i=1))
+    packed, last, w_out_pair = after(packed, last, w_out)
+    got, w_out_pair, *others = beside(packed, move(w_out_pair, i=1), *seventh(last))
+    attn, held = attention(0, got, [*others, last], [w_out, w_out_pair])
+    attn, w_pair = after(attn, w_qkv)
+    attn, w_pair = beside(attn, move(w_pair, i=1))
+    vel = out_projection(0, sc, attn, ada_table, *held)
     mine, other, vel, fin, theirs = second_projection(
         sc, xs, vel, move(vel, h=1), fresh, ada_table, w_qkv, w_pair
     )
-    attn = attention(1, exchange(pack(1, sc, mine, other)))
+    packed, last = pack(1, sc, mine, other)
+    got, *others = beside(packed, *seventh(last))
+    attn, held = attention(1, got, [*others, last], [w_out, w_out_pair])
     attn, theirs = after(exchange(attn), theirs)
     theirs = move(theirs, i=1)
-    out = out_projection(1, sc, attn, ada_table, w_out, w_out_pair)
+    out = out_projection(1, sc, attn, ada_table, *held)
     rs = [out[0], move(out[1], i=1), move(out[2], h=1), move(out[3], h=1, i=1)]
     vel, fin = finish(sc, vel, fin, theirs, rs)
     return vel[:, None], fin

time: 210 us -> 206 us (0.981)
  blocking collectives: 70.2 us -> 32.8 us
  starting transfers between devices: 46.2 us -> 59.3 us
  Pallas kernels: 41.2 us -> 52.3 us
  waiting for transfers between devices: 44.4 us -> 52.6 us
    all_to_all x4 -> x2, blocking collectives: 70.2 us -> 32.8 us  [exchange(): lax.all_to_all(x, AXES, 0, 0, tiled=True, axis_index_groups=group_lists())]
    all_to_all x0 -> x2, waiting for transfers between devices: none -> 18.7 us  [exchange(): lax.all_to_all(x, AXES, 0, 0, tiled=True, axis_index_groups=group_lists())]
    pallas_call x2 -> x6, Pallas kernels: 1.39 us -> 12.5 us  [the longest x4 9.39 us: hold(): pl.pallas_call(body, in_specs=[pl.BlockSpec(memory_space=pl.ANY)], out_sp...]
    ppermute x32, waiting for transfers between devices: 44.4 us -> 33.9 us  [move(): return lax.ppermute(x, AXES, pairs)]
    all_to_all x0 -> x2, starting transfers between devices: none -> 9.18 us  [exchange(): lax.all_to_all(x, AXES, 0, 0, tiled=True, axis_index_groups=group_lists())]
    ppermute x0 -> x6, starting transfers between devices: none -> 3.96 us  [seventh(): out.append(lax.ppermute(x, AXES, pairs))]
    unnamed x32 -> x30, local copies, waits for them, and re-layouts: 5.6 us -> 5.57 us
  transfers between devices with their start and end apart: 32 -> 40, of which waited for: 16 -> 18; matrix products, arithmetic and copies ran while one was open for 1% -> 1% of each run, Pallas kernels for 7% -> 13%
where the time goes in v1:
time: 206 us; the launch traced here: 205 us
  starting transfers between devices  59.3 us (29%)
  waiting for transfers between devices  52.6 us (26%)
  Pallas kernels  52.3 us (25%)
  blocking collectives  32.8 us (16%)
  local copies, waits for them, and re-layouts  5.83 us (3%)
    ppermute x32, starting transfers between devices, move(): return lax.ppermute(x, AXES, pairs)  46.1 us
    ppermute x32, waiting for transfers between devices, move(): return lax.ppermute(x, AXES, pairs)  33.9 us
    all_to_all x2, blocking collectives, exchange(): lax.all_to_all(x, AXES, 0, 0, tiled=True, axis_index_groups=group_lists())  32.8 us
    pallas_call x4, Pallas kernels, attend(): pl.pallas_call(body, in_specs=[SM] + [VM] * (1 + len(blocks) + (2 if last...  25.5 us
    all_to_all x2, waiting for transfers between devices, exchange(): lax.all_to_all(x, AXES, 0, 0, tiled=True, axis_index_groups=group_lists())  18.7 us
    pallas_call x4, Pallas kernels, hold(): pl.pallas_call(body, in_specs=[pl.BlockSpec(memory_space=pl.ANY)], out_sp...  9.39 us
    all_to_all x2, starting transfers between devices, exchange(): lax.all_to_all(x, AXES, 0, 0, tiled=True, axis_index_groups=group_lists())  9.18 us
    unnamed x30, local copies, waits for them, and re-layouts  5.57 us
  transfers between devices with their start and end apart: 40, of which 18 were waited for; matrix products, arithmetic and copies ran while one was open for 1% of the time, Pallas kernels for 13%

profile of v1, /device:TPU:1, one launch (start us, length us, event | category | flops | bytes accessed | tf_op | source)
XLA Modules:
  0.0 205.0 jit_solution(5867985706357712498)
XLA Ops:
  2.1 2.8 %collective-permute-start.1 = (bf16[64,3072]{1,0:T(8,128)(2,1)}, bf16[64,3072]{1,0:T(8,128)(2,1)S(1)}, u32[]{:S(2)}, u32[]{:S(2)}) collective-permute-start(bf16[64,3072]{1,0:T(8,128)(2,1)} %bitcast.30), channel_id=1, source_target_pairs={{0,64},{1,65},{2,66},{3,67},{4,68},{5,69},{6,70},{7,71},{8,72},{9,... | collective-permute-start | bytes 1179656 | tf_op jit(solution)/shard_map/ppermute | solution.py:45
  5.7 3.2 %copy-done = bf16[3072,1280]{1,0:T(8,128)(2,1)S(1)} copy-done((bf16[3072,1280]{1,0:T(8,128)(2,1)S(1)}, bf16[3072,1280]{1,0:T(8,128)(2,1)}, u32[]{:S(2)}) %copy-start) | copy-done | bytes 7864344
  11.0 2.5 %modulate_project.2 = (bf16[10,64,128]{2,1,0:T(8,128)(2,1)S(1)}, bf16[10,64,128]{2,1,0:T(8,128)(2,1)S(1)}) custom-call(s32[10]{0:T(128)S(1)} %pad_add_fusion.refs_0_.sc, bf16[64,3072]{1,0:T(8,128)(2,1)S(1)} %bitcast.31, bf16[64,3072]{1,0:T(8,128)(2,1)S(1)} %collective-permute-done.refs_2_.x1, f32[9,3,3072]{2,1,0:T(4,128)S(1)} %copy-done.2, ...), custom_call_target="tpu_custom_call" | custom-call | flops 4000000000 | bytes 10000000 | tf_op jit(solution)/shard_map/modulate_project/pallas_call | solution.py:185
  22.6 5.1 %all-to-all-start = ((bf16[8,3,128,128]{3,2,1,0:T(8,128)(2,1)}), bf16[8,3,128,128]{3,2,1,0:T(8,128)(2,1)S(1)}, u32[]{:S(2)}, u32[]{:S(2)}) async-start(bf16[8,3,128,128]{3,2,1,0:T(8,128)(2,1)} %get-tuple-element.75), calls=%async_computation | async-start | bytes 1572864 | tf_op jit(solution)/shard_map/all_to_all | solution.py:65
  29.8 10.2 %all-to-all-done.refs_1_ = bf16[8,3,128,128]{3,2,1,0:T(8,128)(2,1)S(1)} async-done(((bf16[8,3,128,128]{3,2,1,0:T(8,128)(2,1)}), bf16[8,3,128,128]{3,2,1,0:T(8,128)(2,1)S(1)}, u32[]{:S(2)}, u32[]{:S(2)}) %all-to-all-start) | async-done | bytes 786464 | tf_op jit(solution)/shard_map/all_to_all | solution.py:65
  40.2 2.7 %collective-permute-start.9 = (bf16[2,2,128,128]{3,2,1,0:T(8,128)(2,1)S(1)}, bf16[2,2,128,128]{3,2,1,0:T(8,128)(2,1)S(1)}, u32[]{:S(2)}, u32[]{:S(2)}) collective-permute-start(bf16[2,2,128,128]{3,2,1,0:T(8,128)(2,1)S(1)} %get-tuple-element.143), channel_id=1, source_target_pairs={{0,2},{1,3},{2,0},{3,1},{4,6},{5,7},{6,4},{7,5},{8,10},{9,11},{10,... | collective-permute-start | bytes 393224 | tf_op jit(solution)/shard_map/ppermute | solution.py:45
  44.5 3.4 %collective-permute-start.15 = (bf16[2,2,128,128]{3,2,1,0:T(8,128)(2,1)S(1)}, bf16[2,2,128,128]{3,2,1,0:T(8,128)(2,1)S(1)}, u32[]{:S(2)}, u32[]{:S(2)}) collective-permute-start(bf16[2,2,128,128]{3,2,1,0:T(8,128)(2,1)S(1)} %get-tuple-element.142), channel_id=1, source_target_pairs={{0,16},{1,17},{2,18},{3,19},{4,20},{5,21},{6,22},{7,23},{8,24},{9,... | collective-permute-start | bytes 393224 | tf_op jit(solution)/shard_map/ppermute | solution.py:45
  49.0 3.7 %collective-permute-done.14 = bf16[2,2,128,128]{3,2,1,0:T(8,128)(2,1)S(1)} collective-permute-done((bf16[2,2,128,128]{3,2,1,0:T(8,128)(2,1)S(1)}, bf16[2,2,128,128]{3,2,1,0:T(8,128)(2,1)S(1)}, u32[]{:S(2)}, u32[]{:S(2)}) %collective-permute-start.14) | collective-permute-done | bytes 131104 | tf_op jit(solution)/shard_map/ppermute | solution.py:45
  52.8 3.0 %collective-permute-start.17 = (bf16[12,2,128,128]{3,2,1,0:T(8,128)(2,1)S(1)}, bf16[12,2,128,128]{3,2,1,0:T(8,128)(2,1)S(1)}, u32[]{:S(2)}, u32[]{:S(2)}) collective-permute-start(bf16[12,2,128,128]{3,2,1,0:T(8,128)(2,1)S(1)} %constant_dynamic-update-slice_fusion.refs_2_), channel_id=1, source_target_pairs={{0,32},{1,33},{2,34},{3,35},{4,36},{5,37},{6,38},{7,39},{8,40},{9,... | collective-permute-start | bytes 2359304 | tf_op jit(solution)/shard_map/ppermute | solution.py:45
  59.5 5.0 %span_attention_begin.2 = (f32[4,384,128]{2,1,0:T(8,128)S(1)}, f32[4,384,256]{2,1,0:T(8,128)S(1)}) custom-call(s32[10]{0:T(128)S(1)} %pad_add_fusion.refs_0_.sc, bf16[8,3,128,128]{3,2,1,0:T(8,128)(2,1)S(1)} %all-to-all-done.refs_1_, bf16[12,2,128,128]{3,2,1,0:T(8,128)(2,1)S(1)} %constant_dynamic-update-slice_fusion.refs_2_, ...), custom_call_target="tpu_custom_call" | custom-call | flops 3019898880 | bytes 8000000 | tf_op jit(solution)/shard_map/span_attention_begin/pallas_call | solution.py:364
  72.6 2.7 %collective-permute-done.18.refs_3_ = bf16[20,2,128,128]{3,2,1,0:T(8,128)(2,1)S(1)} collective-permute-done((bf16[20,2,128,128]{3,2,1,0:T(8,128)(2,1)S(1)}, bf16[20,2,128,128]{3,2,1,0:T(8,128)(2,1)S(1)}, u32[]{:S(2)}, u32[]{:S(2)}) %collective-permute-start.18) | collective-permute-done | bytes 1310752 | tf_op jit(solution)/shard_map/ppermute | solution.py:45
  75.3 7.7 %span_attention_end.2 = bf16[24,128,128]{2,1,0:T(8,128)(2,1)S(1)} custom-call(s32[10]{0:T(128)S(1)} %pad_add_fusion.refs_0_.sc, bf16[8,3,128,128]{3,2,1,0:T(8,128)(2,1)S(1)} %all-to-all-done.refs_1_, bf16[20,2,128,128]{3,2,1,0:T(8,128)(2,1)S(1)} %constant_dynamic-update-slice_fusion.5.refs_2_, bf16[20,2,128,128]{3,2,1,0:T(8,128)(2,1)S(1)} %collective-permute-done.18.refs_3_, ...), custom_call_target="tpu_custom_call" | custom-call | flops 5033164800 | bytes 8000000 | tf_op jit(solution)/shard_map/span_attention_end/pallas_call | solution.py:364
  83.5 16.4 %all_to_all.20.refs_1_ = bf16[8,3,128,128]{3,2,1,0:T(8,128)(2,1)S(1)} all-to-all(bf16[8,3,128,128]{3,2,1,0:T(8,128)(2,1)S(1)} %bitcast.27), channel_id=1, replica_groups={{0,1,4,5,64,65,68,69},{2,3,6,7,66,67,70,71},{8,9,12,13,72,73,76,77},{10..., dimensions={0} | all-to-all | bytes 1572864 | tf_op jit(solution)/shard_map/all_to_all | solution.py:65
  102.9 9.7 %collective-permute-done.20.away = bf16[2,128,768]{2,1,0:T(8,128)(2,1)S(1)} collective-permute-done((bf16[2,128,768]{2,1,0:T(8,128)(2,1)S(1)}, bf16[2,128,768]{2,1,0:T(8,128)(2,1)S(1)}, u32[]{:S(2)}, u32[]{:S(2)}) %collective-permute-start.20) | collective-permute-done | bytes 393248 | tf_op jit(solution)/shard_map/ppermute | solution.py:45
  112.6 3.9 %advance_modulate_project.1 = (bf16[10,128,128]{2,1,0:T(8,128)(2,1)S(1)}, bf16[10,128,128]{2,1,0:T(8,128)(2,1)S(1)}, bf16[32,3072]{1,0:T(8,128)(2,1)S(1)}, bf16[...) custom-call(s32[10]{0:T(128)S(1)} %pad_add_fusion.refs_0_.sc, bf16[64,3072]{1,0:T(8,128)(2,1)S(1)} %bitcast.32, ...), custom_call_target="tpu_custom_call" | custom-call | flops 4000000000 | bytes 10000000 | tf_op jit(solution)/shard_map/advance_modulate_project/pallas_call | solution.py:198
  118.1 4.0 %all-to-all-start.2 = ((bf16[8,3,128,128]{3,2,1,0:T(8,128)(2,1)}), bf16[8,3,128,128]{3,2,1,0:T(8,128)(2,1)S(1)}, u32[]{:S(2)}, u32[]{:S(2)}) async-start(bf16[8,3,128,128]{3,2,1,0:T(8,128)(2,1)} %get-tuple-element.105), calls=%async_computation.2 | async-start | bytes 1572864 | tf_op jit(solution)/shard_map/all_to_all | solution.py:65
  124.1 8.4 %all-to-all-done.2.refs_1_ = bf16[8,3,128,128]{3,2,1,0:T(8,128)(2,1)S(1)} async-done(((bf16[8,3,128,128]{3,2,1,0:T(8,128)(2,1)}), bf16[8,3,128,128]{3,2,1,0:T(8,128)(2,1)S(1)}, u32[]{:S(2)}, u32[]{:S(2)}) %all-to-all-start.2) | async-done | bytes 786464 | tf_op jit(solution)/shard_map/all_to_all | solution.py:65
  132.7 2.7 %collective-permute-start.24 = (bf16[2,2,128,128]{3,2,1,0:T(8,128)(2,1)S(1)}, bf16[2,2,128,128]{3,2,1,0:T(8,128)(2,1)S(1)}, u32[]{:S(2)}, u32[]{:S(2)}) collective-permute-start(bf16[2,2,128,128]{3,2,1,0:T(8,128)(2,1)S(1)} %get-tuple-element.141), channel_id=1, source_target_pairs={{0,2},{1,3},{2,0},{3,1},{4,6},{5,7},{6,4},{7,5},{8,10},{9,11},{10,... | collective-permute-start | bytes 393224 | tf_op jit(solution)/shard_map/ppermute | solution.py:45
  142.5 5.5 %collective-permute-start.32 = (bf16[12,2,128,128]{3,2,1,0:T(8,128)(2,1)S(1)}, bf16[12,2,128,128]{3,2,1,0:T(8,128)(2,1)S(1)}, u32[]{:S(2)}, u32[]{:S(2)}) collective-permute-start(bf16[12,2,128,128]{3,2,1,0:T(8,128)(2,1)S(1)} %constant_dynamic-update-slice_fusion.9.refs_2_), channel_id=1, source_target_pairs={{0,32},{1,33},{2,34},{3,35},{4,36},{5,37},{6,38},{7,39},{8,40},{9,... | collective-permute-start | bytes 2359304 | tf_op jit(solution)/shard_map/ppermute | solution.py:45
  152.4 5.0 %span_attention_begin.3 = (f32[4,384,128]{2,1,0:T(8,128)S(1)}, f32[4,384,256]{2,1,0:T(8,128)S(1)}) custom-call(s32[10]{0:T(128)S(1)} %pad_add_fusion.refs_0_.sc, bf16[8,3,128,128]{3,2,1,0:T(8,128)(2,1)S(1)} %all-to-all-done.2.refs_1_, bf16[12,2,128,128]{3,2,1,0:T(8,128)(2,1)S(1)} %constant_dynamic-update-slice_fusion.9.refs_2_, ...), custom_call_target="tpu_custom_call" | custom-call | flops 3019898880 | bytes 8000000 | tf_op jit(solution)/shard_map/span_attention_begin/pallas_call | solution.py:364
  164.9 2.7 %collective-permute-done.33.refs_3_ = bf16[20,2,128,128]{3,2,1,0:T(8,128)(2,1)S(1)} collective-permute-done((bf16[20,2,128,128]{3,2,1,0:T(8,128)(2,1)S(1)}, bf16[20,2,128,128]{3,2,1,0:T(8,128)(2,1)S(1)}, u32[]{:S(2)}, u32[]{:S(2)}) %collective-permute-start.33) | collective-permute-done | bytes 1310752 | tf_op jit(solution)/shard_map/ppermute | solution.py:45
  167.5 7.7 %span_attention_end.3 = bf16[24,128,128]{2,1,0:T(8,128)(2,1)S(1)} custom-call(s32[10]{0:T(128)S(1)} %pad_add_fusion.refs_0_.sc, bf16[8,3,128,128]{3,2,1,0:T(8,128)(2,1)S(1)} %all-to-all-done.2.refs_1_, bf16[20,2,128,128]{3,2,1,0:T(8,128)(2,1)S(1)} %constant_dynamic-update-slice_fusion.14.refs_2_, ...), custom_call_target="tpu_custom_call" | custom-call | flops 5033164800 | bytes 8000000 | tf_op jit(solution)/shard_map/span_attention_end/pallas_call | solution.py:364
  175.2 16.4 %all_to_all.21.refs_1_ = bf16[8,3,128,128]{3,2,1,0:T(8,128)(2,1)S(1)} all-to-all(bf16[8,3,128,128]{3,2,1,0:T(8,128)(2,1)S(1)} %bitcast.28), channel_id=1, replica_groups={{0,1,4,5,64,65,68,69},{2,3,6,7,66,67,70,71},{8,9,12,13,72,73,76,77},{10..., dimensions={0} | all-to-all | bytes 1572864 | tf_op jit(solution)/shard_map/all_to_all | solution.py:65
  199.4 2.9 %collective-permute-done.37.r3 = bf16[2,32,768]{2,1,0:T(8,128)(2,1)S(1)} collective-permute-done((bf16[2,32,768]{2,1,0:T(8,128)(2,1)S(1)}, bf16[2,32,768]{2,1,0:T(8,128)(2,1)S(1)}, u32[]{:S(2)}, u32[]{:S(2)}) %collective-permute-start.37) | collective-permute-done | bytes 98336 | tf_op jit(solution)/shard_map/ppermute | solution.py:45
  (119 shorter events, 66.5 us)
Async XLA Ops:
  2.1 12.4 %collective-permute-start.1 = (bf16[64,3072]{1,0:T(8,128)(2,1)}, bf16[64,3072]{1,0:T(8,128)(2,1)S(1)}, u32[]{:S(2)}, u32[]{:S(2)}) collective-permute-start(bf16[64,3072]{1,0:T(8,128)(2,1)} %bitcast.30), channel_id=1, source_target_pairs={{0,64},{1,65},{2,66},{3,67},{4,68},{5,69},{6,70},{7,71},{8,72},{9,... | collective-permute-start | bytes 1179656 | tf_op jit(solution)/shard_map/ppermute | solution.py:45
  22.2 17.8 %collective-permute-start.5 = (bf16[3072,768]{1,0:T(8,128)(2,1)}, bf16[3072,768]{1,0:T(8,128)(2,1)}, u32[]{:S(2)}, u32[]{:S(2)}) collective-permute-start(bf16[3072,768]{1,0:T(8,128)(2,1)} %x.1), channel_id=1, source_target_pairs={{0,32},{1,33},{2,34},{3,35},{4,36},{5,37},{6,38},{7,39},{8,40},{9,... | collective-permute-start | bytes 14155784 | tf_op jit(solution)/shard_map/ppermute | solution.py:45
  22.6 17.4 %all-to-all-start = ((bf16[8,3,128,128]{3,2,1,0:T(8,128)(2,1)}), bf16[8,3,128,128]{3,2,1,0:T(8,128)(2,1)S(1)}, u32[]{:S(2)}, u32[]{:S(2)}) async-start(bf16[8,3,128,128]{3,2,1,0:T(8,128)(2,1)} %get-tuple-element.75), calls=%async_computation | async-start | bytes 1572864 | tf_op jit(solution)/shard_map/all_to_all | solution.py:65
  40.2 8.4 %collective-permute-start.9 = (bf16[2,2,128,128]{3,2,1,0:T(8,128)(2,1)S(1)}, bf16[2,2,128,128]{3,2,1,0:T(8,128)(2,1)S(1)}, u32[]{:S(2)}, u32[]{:S(2)}) collective-permute-start(bf16[2,2,128,128]{3,2,1,0:T(8,128)(2,1)S(1)} %get-tuple-element.143), channel_id=1, source_target_pairs={{0,2},{1,3},{2,0},{3,1},{4,6},{5,7},{6,4},{7,5},{8,10},{9,11},{10,... | collective-permute-start | bytes 393224 | tf_op jit(solution)/shard_map/ppermute | solution.py:45
  42.9 6.1 %collective-permute-start.13 = (bf16[2,2,128,128]{3,2,1,0:T(8,128)(2,1)S(1)}, bf16[2,2,128,128]{3,2,1,0:T(8,128)(2,1)S(1)}, u32[]{:S(2)}, u32[]{:S(2)}) collective-permute-start(bf16[2,2,128,128]{3,2,1,0:T(8,128)(2,1)S(1)} %get-tuple-element.142), channel_id=1, source_target_pairs={{0,8},{1,9},{2,10},{3,11},{4,12},{5,13},{6,14},{7,15},{8,16},{9,17... | collective-permute-start | bytes 393224 | tf_op jit(solution)/shard_map/ppermute | solution.py:45
  44.5 8.3 %collective-permute-start.15 = (bf16[2,2,128,128]{3,2,1,0:T(8,128)(2,1)S(1)}, bf16[2,2,128,128]{3,2,1,0:T(8,128)(2,1)S(1)}, u32[]{:S(2)}, u32[]{:S(2)}) collective-permute-start(bf16[2,2,128,128]{3,2,1,0:T(8,128)(2,1)S(1)} %get-tuple-element.142), channel_id=1, source_target_pairs={{0,16},{1,17},{2,18},{3,19},{4,20},{5,21},{6,22},{7,23},{8,24},{9,... | collective-permute-start | bytes 393224 | tf_op jit(solution)/shard_map/ppermute | solution.py:45
  52.8 6.7 %collective-permute-start.17 = (bf16[12,2,128,128]{3,2,1,0:T(8,128)(2,1)S(1)}, bf16[12,2,128,128]{3,2,1,0:T(8,128)(2,1)S(1)}, u32[]{:S(2)}, u32[]{:S(2)}) collective-permute-start(bf16[12,2,128,128]{3,2,1,0:T(8,128)(2,1)S(1)} %constant_dynamic-update-slice_fusion.refs_2_), channel_id=1, source_target_pairs={{0,32},{1,33},{2,34},{3,35},{4,36},{5,37},{6,38},{7,39},{8,40},{9,... | collective-permute-start | bytes 2359304 | tf_op jit(solution)/shard_map/ppermute | solution.py:45
  55.8 15.8 %collective-permute-start.16 = (bf16[8,2,128,128]{3,2,1,0:T(8,128)(2,1)S(1)}, bf16[8,2,128,128]{3,2,1,0:T(8,128)(2,1)S(1)}, u32[]{:S(2)}, u32[]{:S(2)}) collective-permute-start(bf16[8,2,128,128]{3,2,1,0:T(8,128)(2,1)S(1)} %pad_maximum_fusion), channel_id=1, source_target_pairs={{0,2},{1,3},{2,0},{3,1},{4,6},{5,7},{6,4},{7,5},{8,10},{9,11},{10,... | collective-permute-start | bytes 1572872 | tf_op jit(solution)/shard_map/ppermute | solution.py:45
  56.2 13.0 %collective-permute-start.12 = (bf16[4,2,128,128]{3,2,1,0:T(8,128)(2,1)S(1)}, bf16[4,2,128,128]{3,2,1,0:T(8,128)(2,1)S(1)}, u32[]{:S(2)}, u32[]{:S(2)}) collective-permute-start(bf16[4,2,128,128]{3,2,1,0:T(8,128)(2,1)S(1)} %pad_maximum_fusion.2), channel_id=1, source_target_pairs={{0,16},{1,17},{2,18},{3,19},{4,20},{5,21},{6,22},{7,23},{8,24},{9,... | collective-permute-start | bytes 786440 | tf_op jit(solution)/shard_map/ppermute | solution.py:45
  58.0 12.7 %collective-permute-start.11 = (bf16[4,2,128,128]{3,2,1,0:T(8,128)(2,1)S(1)}, bf16[4,2,128,128]{3,2,1,0:T(8,128)(2,1)S(1)}, u32[]{:S(2)}, u32[]{:S(2)}) collective-permute-start(bf16[4,2,128,128]{3,2,1,0:T(8,128)(2,1)S(1)} %pad_maximum_fusion.2), channel_id=1, source_target_pairs={{0,24},{1,25},{2,26},{3,27},{4,28},{5,29},{6,30},{7,31},{8,0},{9,1... | collective-permute-start | bytes 786440 | tf_op jit(solution)/shard_map/ppermute | solution.py:45
  59.2 12.4 %collective-permute-start.10 = (bf16[4,2,128,128]{3,2,1,0:T(8,128)(2,1)S(1)}, bf16[4,2,128,128]{3,2,1,0:T(8,128)(2,1)S(1)}, u32[]{:S(2)}, u32[]{:S(2)}) collective-permute-start(bf16[4,2,128,128]{3,2,1,0:T(8,128)(2,1)S(1)} %pad_maximum_fusion.2), channel_id=1, source_target_pairs={{0,8},{1,9},{2,10},{3,11},{4,12},{5,13},{6,14},{7,15},{8,16},{9,17... | collective-permute-start | bytes 786440 | tf_op jit(solution)/shard_map/ppermute | solution.py:45
  83.1 16.8 %collective-permute-start.19 = (bf16[3072,1280]{1,0:T(8,128)(2,1)S(1)}, bf16[3072,1280]{1,0:T(8,128)(2,1)S(1)}, u32[]{:S(2)}, u32[]{:S(2)}) collective-permute-start(bf16[3072,1280]{1,0:T(8,128)(2,1)S(1)} %bitcast.26), channel_id=1, source_target_pairs={{0,32},{1,33},{2,34},{3,35},{4,36},{5,37},{6,38},{7,39},{8,40},{9,... | collective-permute-start | bytes 23592968 | tf_op jit(solution)/shard_map/ppermute | solution.py:45
  101.9 10.7 %collective-permute-start.20 = (bf16[2,128,768]{2,1,0:T(8,128)(2,1)S(1)}, bf16[2,128,768]{2,1,0:T(8,128)(2,1)S(1)}, u32[]{:S(2)}, u32[]{:S(2)}) collective-permute-start(bf16[2,128,768]{2,1,0:T(8,128)(2,1)S(1)} %out_projection.2.here), channel_id=1, source_target_pairs={{0,64},{1,65},{2,66},{3,67},{4,68},{5,69},{6,70},{7,71},{8,72},{9,... | collective-permute-start | bytes 1179656 | tf_op jit(solution)/shard_map/ppermute | solution.py:45
  118.1 14.5 %all-to-all-start.2 = ((bf16[8,3,128,128]{3,2,1,0:T(8,128)(2,1)}), bf16[8,3,128,128]{3,2,1,0:T(8,128)(2,1)S(1)}, u32[]{:S(2)}, u32[]{:S(2)}) async-start(bf16[8,3,128,128]{3,2,1,0:T(8,128)(2,1)} %get-tuple-element.105), calls=%async_computation.2 | async-start | bytes 1572864 | tf_op jit(solution)/shard_map/all_to_all | solution.py:65
  132.7 6.8 %collective-permute-start.24 = (bf16[2,2,128,128]{3,2,1,0:T(8,128)(2,1)S(1)}, bf16[2,2,128,128]{3,2,1,0:T(8,128)(2,1)S(1)}, u32[]{:S(2)}, u32[]{:S(2)}) collective-permute-start(bf16[2,2,128,128]{3,2,1,0:T(8,128)(2,1)S(1)} %get-tuple-element.141), channel_id=1, source_target_pairs={{0,2},{1,3},{2,0},{3,1},{4,6},{5,7},{6,4},{7,5},{8,10},{9,11},{10,... | collective-permute-start | bytes 393224 | tf_op jit(solution)/shard_map/ppermute | solution.py:45
  136.3 6.1 %collective-permute-start.30 = (bf16[2,2,128,128]{3,2,1,0:T(8,128)(2,1)S(1)}, bf16[2,2,128,128]{3,2,1,0:T(8,128)(2,1)S(1)}, u32[]{:S(2)}, u32[]{:S(2)}) collective-permute-start(bf16[2,2,128,128]{3,2,1,0:T(8,128)(2,1)S(1)} %get-tuple-element.140), channel_id=1, source_target_pairs={{0,16},{1,17},{2,18},{3,19},{4,20},{5,21},{6,22},{7,23},{8,24},{9,... | collective-permute-start | bytes 393224 | tf_op jit(solution)/shard_map/ppermute | solution.py:45
  142.5 10.0 %collective-permute-start.32 = (bf16[12,2,128,128]{3,2,1,0:T(8,128)(2,1)S(1)}, bf16[12,2,128,128]{3,2,1,0:T(8,128)(2,1)S(1)}, u32[]{:S(2)}, u32[]{:S(2)}) collective-permute-start(bf16[12,2,128,128]{3,2,1,0:T(8,128)(2,1)S(1)} %constant_dynamic-update-slice_fusion.9.refs_2_), channel_id=1, source_target_pairs={{0,32},{1,33},{2,34},{3,35},{4,36},{5,37},{6,38},{7,39},{8,40},{9,... | collective-permute-start | bytes 2359304 | tf_op jit(solution)/shard_map/ppermute | solution.py:45
  148.0 16.1 %collective-permute-start.31 = (bf16[8,2,128,128]{3,2,1,0:T(8,128)(2,1)S(1)}, bf16[8,2,128,128]{3,2,1,0:T(8,128)(2,1)S(1)}, u32[]{:S(2)}, u32[]{:S(2)}) collective-permute-start(bf16[8,2,128,128]{3,2,1,0:T(8,128)(2,1)S(1)} %pad_maximum_fusion.1), channel_id=1, source_target_pairs={{0,2},{1,3},{2,0},{3,1},{4,6},{5,7},{6,4},{7,5},{8,10},{9,11},{10,... | collective-permute-start | bytes 1572872 | tf_op jit(solution)/shard_map/ppermute | solution.py:45
  148.6 13.6 %collective-permute-start.27 = (bf16[4,2,128,128]{3,2,1,0:T(8,128)(2,1)S(1)}, bf16[4,2,128,128]{3,2,1,0:T(8,128)(2,1)S(1)}, u32[]{:S(2)}, u32[]{:S(2)}) collective-permute-start(bf16[4,2,128,128]{3,2,1,0:T(8,128)(2,1)S(1)} %pad_maximum_fusion.3), channel_id=1, source_target_pairs={{0,16},{1,17},{2,18},{3,19},{4,20},{5,21},{6,22},{7,23},{8,24},{9,... | collective-permute-start | bytes 786440 | tf_op jit(solution)/shard_map/ppermute | solution.py:45
  150.7 12.7 %collective-permute-start.26 = (bf16[4,2,128,128]{3,2,1,0:T(8,128)(2,1)S(1)}, bf16[4,2,128,128]{3,2,1,0:T(8,128)(2,1)S(1)}, u32[]{:S(2)}, u32[]{:S(2)}) collective-permute-start(bf16[4,2,128,128]{3,2,1,0:T(8,128)(2,1)S(1)} %pad_maximum_fusion.3), channel_id=1, source_target_pairs={{0,24},{1,25},{2,26},{3,27},{4,28},{5,29},{6,30},{7,31},{8,0},{9,1... | collective-permute-start | bytes 786440 | tf_op jit(solution)/shard_map/ppermute | solution.py:45
  152.4 11.6 %collective-permute-start.25 = (bf16[4,2,128,128]{3,2,1,0:T(8,128)(2,1)S(1)}, bf16[4,2,128,128]{3,2,1,0:T(8,128)(2,1)S(1)}, u32[]{:S(2)}, u32[]{:S(2)}) collective-permute-start(bf16[4,2,128,128]{3,2,1,0:T(8,128)(2,1)S(1)} %pad_maximum_fusion.3), channel_id=1, source_target_pairs={{0,8},{1,9},{2,10},{3,11},{4,12},{5,13},{6,14},{7,15},{8,16},{9,17... | collective-permute-start | bytes 786440 | tf_op jit(solution)/shard_map/ppermute | solution.py:45
  191.6 11.8 %collective-permute-start.34 = (bf16[32,3840]{1,0:T(8,128)(2,1)S(1)}, bf16[32,3840]{1,0:T(8,128)(2,1)S(1)}, u32[]{:S(2)}, u32[]{:S(2)}) collective-permute-start(bf16[32,3840]{1,0:T(8,128)(2,1)S(1)} %get-tuple-element.124), channel_id=1, source_target_pairs={{0,32},{1,33},{2,34},{3,35},{4,36},{5,37},{6,38},{7,39},{8,40},{9,... | collective-permute-start | bytes 737288 | tf_op jit(solution)/shard_map/ppermute | solution.py:45
  195.7 6.6 %collective-permute-start.37 = (bf16[2,32,768]{2,1,0:T(8,128)(2,1)S(1)}, bf16[2,32,768]{2,1,0:T(8,128)(2,1)S(1)}, u32[]{:S(2)}, u32[]{:S(2)}) collective-permute-start(bf16[2,32,768]{2,1,0:T(8,128)(2,1)S(1)} %get-tuple-element.136), channel_id=1, source_target_pairs={{0,96},{1,97},{2,98},{3,99},{4,100},{5,101},{6,102},{7,103},{8,104... | collective-permute-start | bytes 294920 | tf_op jit(solution)/shard_map/ppermute | solution.py:45
  196.9 6.6 %collective-permute-start.36 = (bf16[2,32,768]{2,1,0:T(8,128)(2,1)S(1)}, bf16[2,32,768]{2,1,0:T(8,128)(2,1)S(1)}, u32[]{:S(2)}, u32[]{:S(2)}) collective-permute-start(bf16[2,32,768]{2,1,0:T(8,128)(2,1)S(1)} %get-tuple-element.137), channel_id=1, source_target_pairs={{0,64},{1,65},{2,66},{3,67},{4,68},{5,69},{6,70},{7,71},{8,72},{9,... | collective-permute-start | bytes 294920 | tf_op jit(solution)/shard_map/ppermute | solution.py:45
  (25 other events, 122.3 us)

commit v2 on v1

--- a/solution.py
+++ b/solution.py
@@ -136,9 +136,29 @@
     project(hidden, w, mine, theirs)
 
 
+def place_heads(h, chip, out, last):
+    nothing = jnp.zeros((ROWS, HD), BF)
+    last[0] = chip[11]
+    last[1] = chip[19]
+
+    @pl.when(h == 0)
+    def _():
+        for n in range(24):
+            out[n // 3, n % 3] = chip[n] if n < 20 else nothing
+
+    @pl.when(h != 0)
+    def _():
+        for g in range(7):
+            out[g, 0] = chip[4 + g]
+            out[g, 1] = chip[12 + g]
+            out[g, 2] = chip[0] if g == 6 else nothing
+        for m in range(3):
+            out[7, m] = chip[1 + m]
+
+
 def second_body(
     sc, x0, x1, x2, x3, here, away, fresh, ada, w, w_pair,
-    mine, other, vel, fin, theirs, hidden, vall,
+    out, last, vel, fin, theirs, hidden, vall, chip,
 ):
     s = sc[8]
     i = s % 2
@@ -168,14 +188,19 @@
 
     vel[...] = vall[row_of(0, s), :]
     theirs[:, :WIDTH] = vall[row_of(0, s ^ 1), :]
-    for out, weights in ((mine, w), (other, w_pair)):
+    for k, weights in enumerate((w, w_pair)):
         product = jnp.dot(hidden[...], weights[...], preferred_element_type=F32).astype(BF)
-        for k in range(out.shape[0]):
-            out[k] = product[:, k * HD : (k + 1) * HD]
+        for m in range(10):
+            chip[10 * (i ^ k) + m] = product[:, m * HD : (m + 1) * HD]
+    place_heads(s // 2, chip, out, last)
 
 
 def projected_shapes(heads, rows):
     return [jax.ShapeDtypeStruct((heads, rows, HD), BF)] * 2
+
+
+def packed_shapes():
+    return [jax.ShapeDtypeStruct(n + (ROWS, HD), BF) for n in ((8, 3), (2,))]
 
 
 def first_projection(sc, xs, far, ada, w):
@@ -199,57 +224,32 @@
         second_body,
         in_specs=[SM] + [VM] * 10,
         out_specs=[VM] * 5,
-        out_shape=projected_shapes(w.shape[1] // HD, ROWS)
+        out_shape=packed_shapes()
         + [jax.ShapeDtypeStruct((HALF, n), BF) for n in (WIDTH, COLS, WIDTH + COLS)],
-        scratch_shapes=[pltpu.VMEM((ROWS, WIDTH), BF)] * 2,
+        scratch_shapes=[pltpu.VMEM((ROWS, WIDTH), BF)] * 2 + [pltpu.VMEM((20, ROWS, HD), BF)],
         compiler_params=params(14),
         cost_estimate=pl.CostEstimate(flops=4 * 10**9, bytes_accessed=10**7, transcendentals=0),
         name="advance_modulate_project",
     )(sc, *xs, here, away, fresh, ada, w, w_pair)
 
 
-def pack_body(step, sc, *refs):
+def pack_body(sc, *refs):
     parts, (out, last, chip) = refs[:-3], refs[-3:]
     i, h = sc[8] % 2, sc[8] // 2
     for k in range(2):
         to = pl.ds(10 * jnp.where(k == 0, i, 1 - i), 10)
-        if step == 1:
-            chip[to] = parts[k][...]
-            continue
         for n in range(2):
             at = pl.multiple_of((h ^ n) * PAIR, PAIR)
             chip[to, pl.ds(at, PAIR)] = parts[2 * k + n][...]
-    nothing = jnp.zeros((ROWS, HD), BF)
-    last[0] = chip[11]
-    last[1] = chip[19]
-
-    @pl.when(h == 0)
-    def _():
-        for n in range(24):
-            out[n // 3, n % 3] = chip[n] if n < 20 else nothing
-
-    @pl.when(h != 0)
-    def _():
-        for g in range(7):
-            out[g, 0] = chip[4 + g]
-            out[g, 1] = chip[12 + g]
-            out[g, 2] = chip[0] if g == 6 else nothing
-        for m in range(3):
-            out[7, m] = chip[1 + m]
-
-
-def pack(step, sc, *parts):
-    def body(*refs):
-        pack_body(step, *refs)
-
-    return pl.pallas_call(
-        body,
+    place_heads(h, chip, out, last)
+
+
+def pack(sc, *parts):
+    return pl.pallas_call(
+        pack_body,
         in_specs=[SM] + [VM] * len(parts),
         out_specs=[VM, VM],
-        out_shape=[
-            jax.ShapeDtypeStruct((8, 3, ROWS, HD), BF),
-            jax.ShapeDtypeStruct((2, ROWS, HD), BF),
-        ],
+        out_shape=packed_shapes(),
         scratch_shapes=[pltpu.VMEM((20, ROWS, HD), BF)],
         compiler_params=params(8),
         name="pack_heads",
@@ -464,14 +464,16 @@
     return out
 
 
-def begin_keys(low, high):
-    low_y = move(low, y=2)
-    high_z = [move(high, z=k) for k in (1, -1, 2)]
-    early = jnp.concatenate([low, high, low_y, *high_z])
-    lows = jnp.concatenate([low, low_y])
-    highs = jnp.concatenate([high, *high_z])
-    late = [move(lows, z=k) for k in (1, -1, 2)] + [move(highs, y=2)]
-    return early, late
+def begin_keys(x, weights):
+    y = move(x[:3], y=2)
+    zs = [move(x[1:], z=k) for k in (1, -1, 2)]
+    _, weights = after(x, weights)
+    y, zs, weights = after(y, zs, [hold(w) for w in weights])
+    early = jnp.concatenate([x, y, *zs])
+    along_z = jnp.concatenate([x[:1], y[:2]])
+    along_y = jnp.concatenate([x[3:], *[z[1:] for z in zs]])
+    late = [move(along_z, z=k) for k in (1, -1, 2)] + [move(along_y, y=2)]
+    return early, late, weights
 
 
 def both_cores(x):
@@ -494,13 +496,11 @@
 
     def attention(step, got, last, weights):
         keys = jnp.where(group[0] == 7, jnp.stack(last), got[4:, :2])
-        early, late = begin_keys(keys[:2], keys[2:])
-        state = attend(step, sc, got, both_cores(early), 768, 192)
-        state, weights = after(state, weights)
-        weights = [hold(w) for w in weights]
-        late, state, weights = after(late, state, weights)
+        early, late, weights = begin_keys(keys, weights)
+        state = attend(step, sc, got, both_cores(early), 1024, 192)
+        late, state = after(late, state)
         late = jnp.concatenate(late)
-        attn = attend(step, sc, got, both_cores(late), 1280, 192, state)
+        attn = attend(step, sc, got, both_cores(late), 1024, 192, state)
         return attn.reshape(8, 3, ROWS, HD), weights
 
     far = move(own, h=1)
@@ -511,17 +511,16 @@
     b = first_projection(sc, (far, far_near), 2, ada_table, w_qkv)
     xs = (own, near, far, far_near)
 
-    packed, last = pack(0, sc, a[0], b[0], move(a[1], i=1), move(b[1], i=1))
+    packed, last = pack(sc, a[0], b[0], move(a[1], i=1), move(b[1], i=1))
     packed, last, w_out_pair = after(packed, last, w_out)
     got, w_out_pair, *others = beside(packed, move(w_out_pair, i=1), *seventh(last))
     attn, held = attention(0, got, [*others, last], [w_out, w_out_pair])
     attn, w_pair = after(attn, w_qkv)
     attn, w_pair = beside(attn, move(w_pair, i=1))
     vel = out_projection(0, sc, attn, ada_table, *held)
-    mine, other, vel, fin, theirs = second_projection(
+    packed, last, vel, fin, theirs = second_projection(
         sc, xs, vel, move(vel, h=1), fresh, ada_table, w_qkv, w_pair
     )
-    packed, last = pack(1, sc, mine, other)
     got, *others = beside(packed, *seventh(last))
     attn, held = attention(1, got, [*others, last], [w_out, w_out_pair])
     attn, theirs = after(exchange(attn), theirs)

time: 206 us -> 202 us (0.981)
  starting transfers between devices: 59.3 us -> 55.2 us
    ppermute x32, starting transfers between devices: 46.1 us -> 42.1 us  [move(): return lax.ppermute(x, AXES, pairs)]
  transfers between devices with their start and end apart: 40 -> 40, of which waited for: 18 -> 19; matrix products, arithmetic and copies ran while one was open for 1% -> 1% of each run, Pallas kernels for 13% -> 14%
where the time goes in v2:
time: 202 us; the launch traced here: 201 us
  starting transfers between devices  55.2 us (27%)
  waiting for transfers between devices  53.1 us (26%)
  Pallas kernels  51.8 us (26%)
  blocking collectives  32.6 us (16%)
  local copies, waits for them, and re-layouts  6 us (3%)
    ppermute x32, starting transfers between devices, move(): return lax.ppermute(x, AXES, pairs)  42.1 us
    ppermute x32, waiting for transfers between devices, move(): return lax.ppermute(x, AXES, pairs)  34.4 us
    all_to_all x2, blocking collectives, exchange(): lax.all_to_all(x, AXES, 0, 0, tiled=True, axis_index_groups=group_lists())  32.6 us
    pallas_call x4, Pallas kernels, attend(): pl.pallas_call(body, in_specs=[SM] + [VM] * (1 + len(blocks) + (2 if last...  25.4 us
    all_to_all x2, waiting for transfers between devices, exchange(): lax.all_to_all(x, AXES, 0, 0, tiled=True, axis_index_groups=group_lists())  18.7 us
    pallas_call x4, Pallas kernels, hold(): pl.pallas_call(body, in_specs=[pl.BlockSpec(memory_space=pl.ANY)], out_sp...  9.38 us
    all_to_all x2, starting transfers between devices, exchange(): lax.all_to_all(x, AXES, 0, 0, tiled=True, axis_index_groups=group_lists())  9.17 us
    unnamed x30, local copies, waits for them, and re-layouts  5.58 us
  transfers between devices with their start and end apart: 40, of which 19 were waited for; matrix products, arithmetic and copies ran while one was open for 1% of the time, Pallas kernels for 14%

profile of v2, /device:TPU:1, one launch (start us, length us, event | category | flops | bytes accessed | tf_op | source)
XLA Modules:
  0.0 200.9 jit_solution(13340511287358049484)
XLA Ops:
  2.1 2.8 %collective-permute-start.1 = (bf16[64,3072]{1,0:T(8,128)(2,1)}, bf16[64,3072]{1,0:T(8,128)(2,1)S(1)}, u32[]{:S(2)}, u32[]{:S(2)}) collective-permute-start(bf16[64,3072]{1,0:T(8,128)(2,1)} %bitcast.30), channel_id=1, source_target_pairs={{0,64},{1,65},{2,66},{3,67},{4,68},{5,69},{6,70},{7,71},{8,72},{9,... | collective-permute-start | bytes 1179656 | tf_op jit(solution)/shard_map/ppermute | solution.py:45
  5.7 3.2 %copy-done = bf16[3072,1280]{1,0:T(8,128)(2,1)S(1)} copy-done((bf16[3072,1280]{1,0:T(8,128)(2,1)S(1)}, bf16[3072,1280]{1,0:T(8,128)(2,1)}, u32[]{:S(2)}) %copy-start) | copy-done | bytes 7864344
  11.0 2.5 %modulate_project.2 = (bf16[10,64,128]{2,1,0:T(8,128)(2,1)S(1)}, bf16[10,64,128]{2,1,0:T(8,128)(2,1)S(1)}) custom-call(s32[10]{0:T(128)S(1)} %pad_add_fusion.refs_0_.sc, bf16[64,3072]{1,0:T(8,128)(2,1)S(1)} %bitcast.31, bf16[64,3072]{1,0:T(8,128)(2,1)S(1)} %collective-permute-done.refs_2_.x1, f32[9,3,3072]{2,1,0:T(4,128)S(1)} %copy-done.2, ...), custom_call_target="tpu_custom_call" | custom-call | flops 4000000000 | bytes 10000000 | tf_op jit(solution)/shard_map/modulate_project/pallas_call | solution.py:210
  16.7 2.5 %modulate_project.3 = (bf16[10,64,128]{2,1,0:T(8,128)(2,1)S(1)}, bf16[10,64,128]{2,1,0:T(8,128)(2,1)S(1)}) custom-call(s32[10]{0:T(128)S(1)} %pad_add_fusion.refs_0_.sc, bf16[64,3072]{1,0:T(8,128)(2,1)S(1)} %collective-permute-done.1.refs_1_.x2, bf16[64,3072]{1,0:T(8,128)(2,1)S(1)} %collective-permute-done.2.refs_2_.x3, f32[9,3,3072]{2,1,0:T(4,128)S(1)} %copy-done.2, ...), custom_call_target="tpu_custom_call" | custom-call | flops 4000000000 | bytes 10000000 | tf_op jit(solution)/shard_map/modulate_project/pallas_call | solution.py:210
  22.6 5.1 %all-to-all-start = ((bf16[8,3,128,128]{3,2,1,0:T(8,128)(2,1)}), bf16[8,3,128,128]{3,2,1,0:T(8,128)(2,1)S(1)}, u32[]{:S(2)}, u32[]{:S(2)}) async-start(bf16[8,3,128,128]{3,2,1,0:T(8,128)(2,1)} %get-tuple-element.77), calls=%async_computation | async-start | bytes 1572864 | tf_op jit(solution)/shard_map/all_to_all | solution.py:65
  29.8 10.2 %all-to-all-done.refs_1_ = bf16[8,3,128,128]{3,2,1,0:T(8,128)(2,1)S(1)} async-done(((bf16[8,3,128,128]{3,2,1,0:T(8,128)(2,1)}), bf16[8,3,128,128]{3,2,1,0:T(8,128)(2,1)S(1)}, u32[]{:S(2)}, u32[]{:S(2)}) %all-to-all-start) | async-done | bytes 786464 | tf_op jit(solution)/shard_map/all_to_all | solution.py:65
  40.2 2.7 %collective-permute-start.9 = (bf16[3,2,128,128]{3,2,1,0:T(8,128)(2,1)S(1)}, bf16[3,2,128,128]{3,2,1,0:T(8,128)(2,1)S(1)}, u32[]{:S(2)}, u32[]{:S(2)}) collective-permute-start(bf16[3,2,128,128]{3,2,1,0:T(8,128)(2,1)S(1)} %get-tuple-element.151), channel_id=1, source_target_pairs={{0,2},{1,3},{2,0},{3,1},{4,6},{5,7},{6,4},{7,5},{8,10},{9,11},{10,... | collective-permute-start | bytes 589832 | tf_op jit(solution)/shard_map/ppermute | solution.py:45
  42.9 3.6 %collective-permute-start.12 = (bf16[3,2,128,128]{3,2,1,0:T(8,128)(2,1)S(1)}, bf16[3,2,128,128]{3,2,1,0:T(8,128)(2,1)S(1)}, u32[]{:S(2)}, u32[]{:S(2)}) collective-permute-start(bf16[3,2,128,128]{3,2,1,0:T(8,128)(2,1)S(1)} %get-tuple-element.150), channel_id=1, source_target_pairs={{0,16},{1,17},{2,18},{3,19},{4,20},{5,21},{6,22},{7,23},{8,24},{9,... | collective-permute-start | bytes 589832 | tf_op jit(solution)/shard_map/ppermute | solution.py:45
  55.1 2.4 %collective-permute-start.17 = (bf16[16,2,128,128]{3,2,1,0:T(8,128)(2,1)S(1)}, bf16[16,2,128,128]{3,2,1,0:T(8,128)(2,1)S(1)}, u32[]{:S(2)}, u32[]{:S(2)}) collective-permute-start(bf16[16,2,128,128]{3,2,1,0:T(8,128)(2,1)S(1)} %constant_dynamic-update-slice_fusion.refs_2_), channel_id=1, source_target_pairs={{0,32},{1,33},{2,34},{3,35},{4,36},{5,37},{6,38},{7,39},{8,40},{9,... | collective-permute-start | bytes 3145736 | tf_op jit(solution)/shard_map/ppermute | solution.py:45
  58.1 2.4 %collective-permute-start.15 = (bf16[3,2,128,128]{3,2,1,0:T(8,128)(2,1)S(1)}, bf16[3,2,128,128]{3,2,1,0:T(8,128)(2,1)S(1)}, u32[]{:S(2)}, u32[]{:S(2)}) collective-permute-start(bf16[3,2,128,128]{3,2,1,0:T(8,128)(2,1)S(1)} %pad_maximum_fusion.2), channel_id=1, source_target_pairs={{0,16},{1,17},{2,18},{3,19},{4,20},{5,21},{6,22},{7,23},{8,24},{9,... | collective-permute-start | bytes 589832 | tf_op jit(solution)/shard_map/ppermute | solution.py:45
  61.9 6.1 %span_attention_begin.2 = (f32[4,384,128]{2,1,0:T(8,128)S(1)}, f32[4,384,256]{2,1,0:T(8,128)S(1)}) custom-call(s32[10]{0:T(128)S(1)} %pad_add_fusion.refs_0_.sc, bf16[8,3,128,128]{3,2,1,0:T(8,128)(2,1)S(1)} %all-to-all-done.refs_1_, bf16[16,2,128,128]{3,2,1,0:T(8,128)(2,1)S(1)} %constant_dynamic-update-slice_fusion.refs_2_, ...), custom_call_target="tpu_custom_call" | custom-call | flops 4026531840 | bytes 8000000 | tf_op jit(solution)/shard_map/span_attention_begin/pallas_call | solution.py:364
  74.8 6.6 %span_attention_end.2 = bf16[24,128,128]{2,1,0:T(8,128)(2,1)S(1)} custom-call(s32[10]{0:T(128)S(1)} %pad_add_fusion.refs_0_.sc, bf16[8,3,128,128]{3,2,1,0:T(8,128)(2,1)S(1)} %all-to-all-done.refs_1_, bf16[16,2,128,128]{3,2,1,0:T(8,128)(2,1)S(1)} %constant_dynamic-update-slice_fusion.5.refs_2_, bf16[16,2,128,128]{3,2,1,0:T(8,128)(2,1)S(1)} %collective-permute-done.18.refs_3_, ...), custom_call_target="tpu_custom_call" | custom-call | flops 4026531840 | bytes 8000000 | tf_op jit(solution)/shard_map/span_attention_end/pallas_call | solution.py:364
  81.8 16.3 %all_to_all.20.refs_1_ = bf16[8,3,128,128]{3,2,1,0:T(8,128)(2,1)S(1)} all-to-all(bf16[8,3,128,128]{3,2,1,0:T(8,128)(2,1)S(1)} %bitcast.27), channel_id=1, replica_groups={{0,1,4,5,64,65,68,69},{2,3,6,7,66,67,70,71},{8,9,12,13,72,73,76,77},{10..., dimensions={0} | all-to-all | bytes 1572864 | tf_op jit(solution)/shard_map/all_to_all | solution.py:65
  101.2 9.7 %collective-permute-done.20.away = bf16[2,128,768]{2,1,0:T(8,128)(2,1)S(1)} collective-permute-done((bf16[2,128,768]{2,1,0:T(8,128)(2,1)S(1)}, bf16[2,128,768]{2,1,0:T(8,128)(2,1)S(1)}, u32[]{:S(2)}, u32[]{:S(2)}) %collective-permute-start.20) | collective-permute-done | bytes 393248 | tf_op jit(solution)/shard_map/ppermute | solution.py:45
  110.9 5.1 %advance_modulate_project.1 = (bf16[8,3,128,128]{3,2,1,0:T(8,128)(2,1)}, bf16[2,128,128]{2,1,0:T(8,128)(2,1)S(1)}, bf16[32,3072]{1,0:T(8,128)(2,1)S(1)}, bf16[32,768]{1,0:T(8,128)(2,1)S(1)}, bf16[32,3840]{1,0:T(8,128)(2,1)S(1)}) custom-call(s32[10]{0:T(128)S(1)} %pad_add_fusion.refs_0_.sc, bf16[64,3072]{1,0:T(8,128)(2,1)S(1)} %bitcast.32, ...), custom_call_target="tpu_custom_call" | custom-call | flops 4000000000 | bytes 10000000 | tf_op jit(solution)/shard_map/advance_modulate_project/pallas_call | solution.py:223
  115.9 4.0 %all-to-all-start.2 = ((bf16[8,3,128,128]{3,2,1,0:T(8,128)(2,1)}), bf16[8,3,128,128]{3,2,1,0:T(8,128)(2,1)S(1)}, u32[]{:S(2)}, u32[]{:S(2)}) async-start(bf16[8,3,128,128]{3,2,1,0:T(8,128)(2,1)} %get-tuple-element.107), calls=%async_computation.2 | async-start | bytes 1572864 | tf_op jit(solution)/shard_map/all_to_all | solution.py:65
  122.0 8.4 %all-to-all-done.2.refs_1_ = bf16[8,3,128,128]{3,2,1,0:T(8,128)(2,1)S(1)} async-done(((bf16[8,3,128,128]{3,2,1,0:T(8,128)(2,1)}), bf16[8,3,128,128]{3,2,1,0:T(8,128)(2,1)S(1)}, u32[]{:S(2)}, u32[]{:S(2)}) %all-to-all-start.2) | async-done | bytes 786464 | tf_op jit(solution)/shard_map/all_to_all | solution.py:65
  130.6 2.3 %collective-permute-start.24 = (bf16[3,2,128,128]{3,2,1,0:T(8,128)(2,1)S(1)}, bf16[3,2,128,128]{3,2,1,0:T(8,128)(2,1)S(1)}, u32[]{:S(2)}, u32[]{:S(2)}) collective-permute-start(bf16[3,2,128,128]{3,2,1,0:T(8,128)(2,1)S(1)} %get-tuple-element.147), channel_id=1, source_target_pairs={{0,2},{1,3},{2,0},{3,1},{4,6},{5,7},{6,4},{7,5},{8,10},{9,11},{10,... | collective-permute-start | bytes 589832 | tf_op jit(solution)/shard_map/ppermute | solution.py:45
  141.3 2.6 %collective-permute-done.25 = bf16[3,2,128,128]{3,2,1,0:T(8,128)(2,1)S(1)} collective-permute-done((bf16[3,2,128,128]{3,2,1,0:T(8,128)(2,1)S(1)}, bf16[3,2,128,128]{3,2,1,0:T(8,128)(2,1)S(1)}, u32[]{:S(2)}, u32[]{:S(2)}) %collective-permute-start.25) | collective-permute-done | bytes 196640 | tf_op jit(solution)/shard_map/ppermute | solution.py:45
  144.0 3.5 %collective-permute-start.32 = (bf16[16,2,128,128]{3,2,1,0:T(8,128)(2,1)S(1)}, bf16[16,2,128,128]{3,2,1,0:T(8,128)(2,1)S(1)}, u32[]{:S(2)}, u32[]{:S(2)}) collective-permute-start(bf16[16,2,128,128]{3,2,1,0:T(8,128)(2,1)S(1)} %constant_dynamic-update-slice_fusion.9.refs_2_), channel_id=1, source_target_pairs={{0,32},{1,33},{2,34},{3,35},{4,36},{5,37},{6,38},{7,39},{8,40},{9,... | collective-permute-start | bytes 3145736 | tf_op jit(solution)/shard_map/ppermute | solution.py:45
  150.9 6.1 %span_attention_begin.3 = (f32[4,384,128]{2,1,0:T(8,128)S(1)}, f32[4,384,256]{2,1,0:T(8,128)S(1)}) custom-call(s32[10]{0:T(128)S(1)} %pad_add_fusion.refs_0_.sc, bf16[8,3,128,128]{3,2,1,0:T(8,128)(2,1)S(1)} %all-to-all-done.2.refs_1_, bf16[16,2,128,128]{3,2,1,0:T(8,128)(2,1)S(1)} %constant_dynamic-update-slice_fusion.9.refs_2_, ...), custom_call_target="tpu_custom_call" | custom-call | flops 4026531840 | bytes 8000000 | tf_op jit(solution)/shard_map/span_attention_begin/pallas_call | solution.py:364
  164.7 6.6 %span_attention_end.3 = bf16[24,128,128]{2,1,0:T(8,128)(2,1)S(1)} custom-call(s32[10]{0:T(128)S(1)} %pad_add_fusion.refs_0_.sc, bf16[8,3,128,128]{3,2,1,0:T(8,128)(2,1)S(1)} %all-to-all-done.2.refs_1_, bf16[16,2,128,128]{3,2,1,0:T(8,128)(2,1)S(1)} %constant_dynamic-update-slice_fusion.14.refs_2_, ...), custom_call_target="tpu_custom_call" | custom-call | flops 4026531840 | bytes 8000000 | tf_op jit(solution)/shard_map/span_attention_end/pallas_call | solution.py:364
  171.3 16.3 %all_to_all.21.refs_1_ = bf16[8,3,128,128]{3,2,1,0:T(8,128)(2,1)S(1)} all-to-all(bf16[8,3,128,128]{3,2,1,0:T(8,128)(2,1)S(1)} %bitcast.28), channel_id=1, replica_groups={{0,1,4,5,64,65,68,69},{2,3,6,7,66,67,70,71},{8,9,12,13,72,73,76,77},{10..., dimensions={0} | all-to-all | bytes 1572864 | tf_op jit(solution)/shard_map/all_to_all | solution.py:65
  195.4 2.9 %collective-permute-done.37.r3 = bf16[2,32,768]{2,1,0:T(8,128)(2,1)S(1)} collective-permute-done((bf16[2,32,768]{2,1,0:T(8,128)(2,1)S(1)}, bf16[2,32,768]{2,1,0:T(8,128)(2,1)S(1)}, u32[]{:S(2)}, u32[]{:S(2)}) %collective-permute-start.37) | collective-permute-done | bytes 98336 | tf_op jit(solution)/shard_map/ppermute | solution.py:45
  (128 shorter events, 65.8 us)
Async XLA Ops:
  2.1 12.4 %collective-permute-start.1 = (bf16[64,3072]{1,0:T(8,128)(2,1)}, bf16[64,3072]{1,0:T(8,128)(2,1)S(1)}, u32[]{:S(2)}, u32[]{:S(2)}) collective-permute-start(bf16[64,3072]{1,0:T(8,128)(2,1)} %bitcast.30), channel_id=1, source_target_pairs={{0,64},{1,65},{2,66},{3,67},{4,68},{5,69},{6,70},{7,71},{8,72},{9,... | collective-permute-start | bytes 1179656 | tf_op jit(solution)/shard_map/ppermute | solution.py:45
  22.2 17.8 %collective-permute-start.5 = (bf16[3072,768]{1,0:T(8,128)(2,1)}, bf16[3072,768]{1,0:T(8,128)(2,1)}, u32[]{:S(2)}, u32[]{:S(2)}) collective-permute-start(bf16[3072,768]{1,0:T(8,128)(2,1)} %x.1), channel_id=1, source_target_pairs={{0,32},{1,33},{2,34},{3,35},{4,36},{5,37},{6,38},{7,39},{8,40},{9,... | collective-permute-start | bytes 14155784 | tf_op jit(solution)/shard_map/ppermute | solution.py:45
  22.6 17.4 %all-to-all-start = ((bf16[8,3,128,128]{3,2,1,0:T(8,128)(2,1)}), bf16[8,3,128,128]{3,2,1,0:T(8,128)(2,1)S(1)}, u32[]{:S(2)}, u32[]{:S(2)}) async-start(bf16[8,3,128,128]{3,2,1,0:T(8,128)(2,1)} %get-tuple-element.77), calls=%async_computation | async-start | bytes 1572864 | tf_op jit(solution)/shard_map/all_to_all | solution.py:65
  40.2 12.5 %collective-permute-start.9 = (bf16[3,2,128,128]{3,2,1,0:T(8,128)(2,1)S(1)}, bf16[3,2,128,128]{3,2,1,0:T(8,128)(2,1)S(1)}, u32[]{:S(2)}, u32[]{:S(2)}) collective-permute-start(bf16[3,2,128,128]{3,2,1,0:T(8,128)(2,1)S(1)} %get-tuple-element.151), channel_id=1, source_target_pairs={{0,2},{1,3},{2,0},{3,1},{4,6},{5,7},{6,4},{7,5},{8,10},{9,11},{10,... | collective-permute-start | bytes 589832 | tf_op jit(solution)/shard_map/ppermute | solution.py:45
  42.9 9.8 %collective-permute-start.12 = (bf16[3,2,128,128]{3,2,1,0:T(8,128)(2,1)S(1)}, bf16[3,2,128,128]{3,2,1,0:T(8,128)(2,1)S(1)}, u32[]{:S(2)}, u32[]{:S(2)}) collective-permute-start(bf16[3,2,128,128]{3,2,1,0:T(8,128)(2,1)S(1)} %get-tuple-element.150), channel_id=1, source_target_pairs={{0,16},{1,17},{2,18},{3,19},{4,20},{5,21},{6,22},{7,23},{8,24},{9,... | collective-permute-start | bytes 589832 | tf_op jit(solution)/shard_map/ppermute | solution.py:45
  46.5 8.3 %collective-permute-start.11 = (bf16[3,2,128,128]{3,2,1,0:T(8,128)(2,1)S(1)}, bf16[3,2,128,128]{3,2,1,0:T(8,128)(2,1)S(1)}, u32[]{:S(2)}, u32[]{:S(2)}) collective-permute-start(bf16[3,2,128,128]{3,2,1,0:T(8,128)(2,1)S(1)} %get-tuple-element.150), channel_id=1, source_target_pairs={{0,24},{1,25},{2,26},{3,27},{4,28},{5,29},{6,30},{7,31},{8,0},{9,1... | collective-permute-start | bytes 589832 | tf_op jit(solution)/shard_map/ppermute | solution.py:45
  46.8 8.2 %collective-permute-start.10 = (bf16[3,2,128,128]{3,2,1,0:T(8,128)(2,1)S(1)}, bf16[3,2,128,128]{3,2,1,0:T(8,128)(2,1)S(1)}, u32[]{:S(2)}, u32[]{:S(2)}) collective-permute-start(bf16[3,2,128,128]{3,2,1,0:T(8,128)(2,1)S(1)} %get-tuple-element.150), channel_id=1, source_target_pairs={{0,8},{1,9},{2,10},{3,11},{4,12},{5,13},{6,14},{7,15},{8,16},{9,17... | collective-permute-start | bytes 589832 | tf_op jit(solution)/shard_map/ppermute | solution.py:45
  55.1 6.8 %collective-permute-start.17 = (bf16[16,2,128,128]{3,2,1,0:T(8,128)(2,1)S(1)}, bf16[16,2,128,128]{3,2,1,0:T(8,128)(2,1)S(1)}, u32[]{:S(2)}, u32[]{:S(2)}) collective-permute-start(bf16[16,2,128,128]{3,2,1,0:T(8,128)(2,1)S(1)} %constant_dynamic-update-slice_fusion.refs_2_), channel_id=1, source_target_pairs={{0,32},{1,33},{2,34},{3,35},{4,36},{5,37},{6,38},{7,39},{8,40},{9,... | collective-permute-start | bytes 3145736 | tf_op jit(solution)/shard_map/ppermute | solution.py:45
  57.7 13.7 %collective-permute-start.16 = (bf16[7,2,128,128]{3,2,1,0:T(8,128)(2,1)S(1)}, bf16[7,2,128,128]{3,2,1,0:T(8,128)(2,1)S(1)}, u32[]{:S(2)}, u32[]{:S(2)}) collective-permute-start(bf16[7,2,128,128]{3,2,1,0:T(8,128)(2,1)S(1)} %pad_maximum_fusion), channel_id=1, source_target_pairs={{0,2},{1,3},{2,0},{3,1},{4,6},{5,7},{6,4},{7,5},{8,10},{9,11},{10,... | collective-permute-start | bytes 1376264 | tf_op jit(solution)/shard_map/ppermute | solution.py:45
  58.1 9.9 %collective-permute-start.15 = (bf16[3,2,128,128]{3,2,1,0:T(8,128)(2,1)S(1)}, bf16[3,2,128,128]{3,2,1,0:T(8,128)(2,1)S(1)}, u32[]{:S(2)}, u32[]{:S(2)}) collective-permute-start(bf16[3,2,128,128]{3,2,1,0:T(8,128)(2,1)S(1)} %pad_maximum_fusion.2), channel_id=1, source_target_pairs={{0,16},{1,17},{2,18},{3,19},{4,20},{5,21},{6,22},{7,23},{8,24},{9,... | collective-permute-start | bytes 589832 | tf_op jit(solution)/shard_map/ppermute | solution.py:45
  60.4 9.6 %collective-permute-start.14 = (bf16[3,2,128,128]{3,2,1,0:T(8,128)(2,1)S(1)}, bf16[3,2,128,128]{3,2,1,0:T(8,128)(2,1)S(1)}, u32[]{:S(2)}, u32[]{:S(2)}) collective-permute-start(bf16[3,2,128,128]{3,2,1,0:T(8,128)(2,1)S(1)} %pad_maximum_fusion.2), channel_id=1, source_target_pairs={{0,24},{1,25},{2,26},{3,27},{4,28},{5,29},{6,30},{7,31},{8,0},{9,1... | collective-permute-start | bytes 589832 | tf_op jit(solution)/shard_map/ppermute | solution.py:45
  61.3 9.1 %collective-permute-start.13 = (bf16[3,2,128,128]{3,2,1,0:T(8,128)(2,1)S(1)}, bf16[3,2,128,128]{3,2,1,0:T(8,128)(2,1)S(1)}, u32[]{:S(2)}, u32[]{:S(2)}) collective-permute-start(bf16[3,2,128,128]{3,2,1,0:T(8,128)(2,1)S(1)} %pad_maximum_fusion.2), channel_id=1, source_target_pairs={{0,8},{1,9},{2,10},{3,11},{4,12},{5,13},{6,14},{7,15},{8,16},{9,17... | collective-permute-start | bytes 589832 | tf_op jit(solution)/shard_map/ppermute | solution.py:45
  81.4 16.8 %collective-permute-start.19 = (bf16[3072,1280]{1,0:T(8,128)(2,1)S(1)}, bf16[3072,1280]{1,0:T(8,128)(2,1)S(1)}, u32[]{:S(2)}, u32[]{:S(2)}) collective-permute-start(bf16[3072,1280]{1,0:T(8,128)(2,1)S(1)} %bitcast.26), channel_id=1, source_target_pairs={{0,32},{1,33},{2,34},{3,35},{4,36},{5,37},{6,38},{7,39},{8,40},{9,... | collective-permute-start | bytes 23592968 | tf_op jit(solution)/shard_map/ppermute | solution.py:45
  100.2 10.7 %collective-permute-start.20 = (bf16[2,128,768]{2,1,0:T(8,128)(2,1)S(1)}, bf16[2,128,768]{2,1,0:T(8,128)(2,1)S(1)}, u32[]{:S(2)}, u32[]{:S(2)}) collective-permute-start(bf16[2,128,768]{2,1,0:T(8,128)(2,1)S(1)} %out_projection.2.here), channel_id=1, source_target_pairs={{0,64},{1,65},{2,66},{3,67},{4,68},{5,69},{6,70},{7,71},{8,72},{9,... | collective-permute-start | bytes 1179656 | tf_op jit(solution)/shard_map/ppermute | solution.py:45
  115.9 14.5 %all-to-all-start.2 = ((bf16[8,3,128,128]{3,2,1,0:T(8,128)(2,1)}), bf16[8,3,128,128]{3,2,1,0:T(8,128)(2,1)S(1)}, u32[]{:S(2)}, u32[]{:S(2)}) async-start(bf16[8,3,128,128]{3,2,1,0:T(8,128)(2,1)} %get-tuple-element.107), calls=%async_computation.2 | async-start | bytes 1572864 | tf_op jit(solution)/shard_map/all_to_all | solution.py:65
  130.6 10.7 %collective-permute-start.24 = (bf16[3,2,128,128]{3,2,1,0:T(8,128)(2,1)S(1)}, bf16[3,2,128,128]{3,2,1,0:T(8,128)(2,1)S(1)}, u32[]{:S(2)}, u32[]{:S(2)}) collective-permute-start(bf16[3,2,128,128]{3,2,1,0:T(8,128)(2,1)S(1)} %get-tuple-element.147), channel_id=1, source_target_pairs={{0,2},{1,3},{2,0},{3,1},{4,6},{5,7},{6,4},{7,5},{8,10},{9,11},{10,... | collective-permute-start | bytes 589832 | tf_op jit(solution)/shard_map/ppermute | solution.py:45
  132.9 8.4 %collective-permute-start.27 = (bf16[3,2,128,128]{3,2,1,0:T(8,128)(2,1)S(1)}, bf16[3,2,128,128]{3,2,1,0:T(8,128)(2,1)S(1)}, u32[]{:S(2)}, u32[]{:S(2)}) collective-permute-start(bf16[3,2,128,128]{3,2,1,0:T(8,128)(2,1)S(1)} %get-tuple-element.146), channel_id=1, source_target_pairs={{0,16},{1,17},{2,18},{3,19},{4,20},{5,21},{6,22},{7,23},{8,24},{9,... | collective-permute-start | bytes 589832 | tf_op jit(solution)/shard_map/ppermute | solution.py:45
  136.0 7.8 %collective-permute-start.25 = (bf16[3,2,128,128]{3,2,1,0:T(8,128)(2,1)S(1)}, bf16[3,2,128,128]{3,2,1,0:T(8,128)(2,1)S(1)}, u32[]{:S(2)}, u32[]{:S(2)}) collective-permute-start(bf16[3,2,128,128]{3,2,1,0:T(8,128)(2,1)S(1)} %get-tuple-element.146), channel_id=1, source_target_pairs={{0,8},{1,9},{2,10},{3,11},{4,12},{5,13},{6,14},{7,15},{8,16},{9,17... | collective-permute-start | bytes 589832 | tf_op jit(solution)/shard_map/ppermute | solution.py:45
  144.0 7.0 %collective-permute-start.32 = (bf16[16,2,128,128]{3,2,1,0:T(8,128)(2,1)S(1)}, bf16[16,2,128,128]{3,2,1,0:T(8,128)(2,1)S(1)}, u32[]{:S(2)}, u32[]{:S(2)}) collective-permute-start(bf16[16,2,128,128]{3,2,1,0:T(8,128)(2,1)S(1)} %constant_dynamic-update-slice_fusion.9.refs_2_), channel_id=1, source_target_pairs={{0,32},{1,33},{2,34},{3,35},{4,36},{5,37},{6,38},{7,39},{8,40},{9,... | collective-permute-start | bytes 3145736 | tf_op jit(solution)/shard_map/ppermute | solution.py:45
  147.7 13.7 %collective-permute-start.31 = (bf16[7,2,128,128]{3,2,1,0:T(8,128)(2,1)S(1)}, bf16[7,2,128,128]{3,2,1,0:T(8,128)(2,1)S(1)}, u32[]{:S(2)}, u32[]{:S(2)}) collective-permute-start(bf16[7,2,128,128]{3,2,1,0:T(8,128)(2,1)S(1)} %pad_maximum_fusion.1), channel_id=1, source_target_pairs={{0,2},{1,3},{2,0},{3,1},{4,6},{5,7},{6,4},{7,5},{8,10},{9,11},{10,... | collective-permute-start | bytes 1376264 | tf_op jit(solution)/shard_map/ppermute | solution.py:45
  148.5 8.6 %collective-permute-start.30 = (bf16[3,2,128,128]{3,2,1,0:T(8,128)(2,1)S(1)}, bf16[3,2,128,128]{3,2,1,0:T(8,128)(2,1)S(1)}, u32[]{:S(2)}, u32[]{:S(2)}) collective-permute-start(bf16[3,2,128,128]{3,2,1,0:T(8,128)(2,1)S(1)} %pad_maximum_fusion.3), channel_id=1, source_target_pairs={{0,16},{1,17},{2,18},{3,19},{4,20},{5,21},{6,22},{7,23},{8,24},{9,... | collective-permute-start | bytes 589832 | tf_op jit(solution)/shard_map/ppermute | solution.py:45
  149.5 9.7 %collective-permute-start.29 = (bf16[3,2,128,128]{3,2,1,0:T(8,128)(2,1)S(1)}, bf16[3,2,128,128]{3,2,1,0:T(8,128)(2,1)S(1)}, u32[]{:S(2)}, u32[]{:S(2)}) collective-permute-start(bf16[3,2,128,128]{3,2,1,0:T(8,128)(2,1)S(1)} %pad_maximum_fusion.3), channel_id=1, source_target_pairs={{0,24},{1,25},{2,26},{3,27},{4,28},{5,29},{6,30},{7,31},{8,0},{9,1... | collective-permute-start | bytes 589832 | tf_op jit(solution)/shard_map/ppermute | solution.py:45
  150.4 10.7 %collective-permute-start.28 = (bf16[3,2,128,128]{3,2,1,0:T(8,128)(2,1)S(1)}, bf16[3,2,128,128]{3,2,1,0:T(8,128)(2,1)S(1)}, u32[]{:S(2)}, u32[]{:S(2)}) collective-permute-start(bf16[3,2,128,128]{3,2,1,0:T(8,128)(2,1)S(1)} %pad_maximum_fusion.3), channel_id=1, source_target_pairs={{0,8},{1,9},{2,10},{3,11},{4,12},{5,13},{6,14},{7,15},{8,16},{9,17... | collective-permute-start | bytes 589832 | tf_op jit(solution)/shard_map/ppermute | solution.py:45
  187.6 11.9 %collective-permute-start.34 = (bf16[32,3840]{1,0:T(8,128)(2,1)S(1)}, bf16[32,3840]{1,0:T(8,128)(2,1)S(1)}, u32[]{:S(2)}, u32[]{:S(2)}) collective-permute-start(bf16[32,3840]{1,0:T(8,128)(2,1)S(1)} %get-tuple-element.128), channel_id=1, source_target_pairs={{0,32},{1,33},{2,34},{3,35},{4,36},{5,37},{6,38},{7,39},{8,40},{9,... | collective-permute-start | bytes 737288 | tf_op jit(solution)/shard_map/ppermute | solution.py:45
  (25 other events, 134.4 us)

commit v3 on v2

--- a/solution.py
+++ b/solution.py
@@ -367,7 +367,7 @@
         out_specs=VM if last else [VM, VM],
         out_shape=out_shape,
         scratch_shapes=scratch,
-        compiler_params=params(20 if last else 12),
+        compiler_params=params(20 if last else 18),
         cost_estimate=pl.CostEstimate(
             flops=pairs * HD * 8, bytes_accessed=8 * 10**6, transcendentals=pairs
         ),
@@ -497,10 +497,10 @@
     def attention(step, got, last, weights):
         keys = jnp.where(group[0] == 7, jnp.stack(last), got[4:, :2])
         early, late, weights = begin_keys(keys, weights)
-        state = attend(step, sc, got, both_cores(early), 1024, 192)
+        state = attend(step, sc, got, both_cores(early), 4096, 192)
         late, state = after(late, state)
         late = jnp.concatenate(late)
-        attn = attend(step, sc, got, both_cores(late), 1024, 192, state)
+        attn = attend(step, sc, got, both_cores(late), 4096, 192, state)
         return attn.reshape(8, 3, ROWS, HD), weights
 
     far = move(own, h=1)

time: 202 us -> 201 us (level)
  no operation moved by 1% of the time
where the time goes in v3:
time: 201 us; the launch traced here: 200 us
  starting transfers between devices  55.5 us (28%)
  waiting for transfers between devices  53.1 us (26%)
  Pallas kernels  50.7 us (25%)
  blocking collectives  32.4 us (16%)
  local copies, waits for them, and re-layouts  6 us (3%)
    ppermute x32, starting transfers between devices, move(): return lax.ppermute(x, AXES, pairs)  42.4 us
    ppermute x32, waiting for transfers between devices, move(): return lax.ppermute(x, AXES, pairs)  34.8 us
    all_to_all x2, blocking collectives, exchange(): lax.all_to_all(x, AXES, 0, 0, tiled=True, axis_index_groups=group_lists())  32.4 us
    pallas_call x4, Pallas kernels, attend(): pl.pallas_call(body, in_specs=[SM] + [VM] * (1 + len(blocks) + (2 if last...  24.5 us
    all_to_all x2, waiting for transfers between devices, exchange(): lax.all_to_all(x, AXES, 0, 0, tiled=True, axis_index_groups=group_lists())  18.3 us
    pallas_call x4, Pallas kernels, hold(): pl.pallas_call(body, in_specs=[pl.BlockSpec(memory_space=pl.ANY)], out_sp...  9.38 us
    all_to_all x2, starting transfers between devices, exchange(): lax.all_to_all(x, AXES, 0, 0, tiled=True, axis_index_groups=group_lists())  9.19 us
    unnamed x30, local copies, waits for them, and re-layouts  5.58 us
  transfers between devices with their start and end apart: 40, of which 19 were waited for; matrix products, arithmetic and copies ran while one was open for 1% of the time, Pallas kernels for 14%

profile of v3, /device:TPU:1, one launch (start us, length us, event | category | flops | bytes accessed | tf_op | source)
XLA Modules:
  0.0 200.0 jit_solution(15282455580510414423)
XLA Ops:
  2.1 2.8 %collective-permute-start.1 = (bf16[64,3072]{1,0:T(8,128)(2,1)}, bf16[64,3072]{1,0:T(8,128)(2,1)S(1)}, u32[]{:S(2)}, u32[]{:S(2)}) collective-permute-start(bf16[64,3072]{1,0:T(8,128)(2,1)} %bitcast.30), channel_id=1, source_target_pairs={{0,64},{1,65},{2,66},{3,67},{4,68},{5,69},{6,70},{7,71},{8,72},{9,... | collective-permute-start | bytes 1179656 | tf_op jit(solution)/shard_map/ppermute | solution.py:45
  5.7 3.2 %copy-done = bf16[3072,1280]{1,0:T(8,128)(2,1)S(1)} copy-done((bf16[3072,1280]{1,0:T(8,128)(2,1)S(1)}, bf16[3072,1280]{1,0:T(8,128)(2,1)}, u32[]{:S(2)}) %copy-start) | copy-done | bytes 7864344
  11.0 2.5 %modulate_project.2 = (bf16[10,64,128]{2,1,0:T(8,128)(2,1)S(1)}, bf16[10,64,128]{2,1,0:T(8,128)(2,1)S(1)}) custom-call(s32[10]{0:T(128)S(1)} %pad_add_fusion.refs_0_.sc, bf16[64,3072]{1,0:T(8,128)(2,1)S(1)} %bitcast.31, bf16[64,3072]{1,0:T(8,128)(2,1)S(1)} %collective-permute-done.refs_2_.x1, f32[9,3,3072]{2,1,0:T(4,128)S(1)} %copy-done.2, ...), custom_call_target="tpu_custom_call" | custom-call | flops 4000000000 | bytes 10000000 | tf_op jit(solution)/shard_map/modulate_project/pallas_call | solution.py:210
  16.7 2.5 %modulate_project.3 = (bf16[10,64,128]{2,1,0:T(8,128)(2,1)S(1)}, bf16[10,64,128]{2,1,0:T(8,128)(2,1)S(1)}) custom-call(s32[10]{0:T(128)S(1)} %pad_add_fusion.refs_0_.sc, bf16[64,3072]{1,0:T(8,128)(2,1)S(1)} %collective-permute-done.1.refs_1_.x2, bf16[64,3072]{1,0:T(8,128)(2,1)S(1)} %collective-permute-done.2.refs_2_.x3, f32[9,3,3072]{2,1,0:T(4,128)S(1)} %copy-done.2, ...), custom_call_target="tpu_custom_call" | custom-call | flops 4000000000 | bytes 10000000 | tf_op jit(solution)/shard_map/modulate_project/pallas_call | solution.py:210
  22.6 5.1 %all-to-all-start = ((bf16[8,3,128,128]{3,2,1,0:T(8,128)(2,1)}), bf16[8,3,128,128]{3,2,1,0:T(8,128)(2,1)S(1)}, u32[]{:S(2)}, u32[]{:S(2)}) async-start(bf16[8,3,128,128]{3,2,1,0:T(8,128)(2,1)} %get-tuple-element.77), calls=%async_computation | async-start | bytes 1572864 | tf_op jit(solution)/shard_map/all_to_all | solution.py:65
  29.8 10.2 %all-to-all-done.refs_1_ = bf16[8,3,128,128]{3,2,1,0:T(8,128)(2,1)S(1)} async-done(((bf16[8,3,128,128]{3,2,1,0:T(8,128)(2,1)}), bf16[8,3,128,128]{3,2,1,0:T(8,128)(2,1)S(1)}, u32[]{:S(2)}, u32[]{:S(2)}) %all-to-all-start) | async-done | bytes 786464 | tf_op jit(solution)/shard_map/all_to_all | solution.py:65
  40.2 2.7 %collective-permute-start.9 = (bf16[3,2,128,128]{3,2,1,0:T(8,128)(2,1)S(1)}, bf16[3,2,128,128]{3,2,1,0:T(8,128)(2,1)S(1)}, u32[]{:S(2)}, u32[]{:S(2)}) collective-permute-start(bf16[3,2,128,128]{3,2,1,0:T(8,128)(2,1)S(1)} %get-tuple-element.151), channel_id=1, source_target_pairs={{0,2},{1,3},{2,0},{3,1},{4,6},{5,7},{6,4},{7,5},{8,10},{9,11},{10,... | collective-permute-start | bytes 589832 | tf_op jit(solution)/shard_map/ppermute | solution.py:45
  42.9 3.6 %collective-permute-start.12 = (bf16[3,2,128,128]{3,2,1,0:T(8,128)(2,1)S(1)}, bf16[3,2,128,128]{3,2,1,0:T(8,128)(2,1)S(1)}, u32[]{:S(2)}, u32[]{:S(2)}) collective-permute-start(bf16[3,2,128,128]{3,2,1,0:T(8,128)(2,1)S(1)} %get-tuple-element.150), channel_id=1, source_target_pairs={{0,16},{1,17},{2,18},{3,19},{4,20},{5,21},{6,22},{7,23},{8,24},{9,... | collective-permute-start | bytes 589832 | tf_op jit(solution)/shard_map/ppermute | solution.py:45
  55.1 2.4 %collective-permute-start.17 = (bf16[16,2,128,128]{3,2,1,0:T(8,128)(2,1)S(1)}, bf16[16,2,128,128]{3,2,1,0:T(8,128)(2,1)S(1)}, u32[]{:S(2)}, u32[]{:S(2)}) collective-permute-start(bf16[16,2,128,128]{3,2,1,0:T(8,128)(2,1)S(1)} %constant_dynamic-update-slice_fusion.refs_2_), channel_id=1, source_target_pairs={{0,32},{1,33},{2,34},{3,35},{4,36},{5,37},{6,38},{7,39},{8,40},{9,... | collective-permute-start | bytes 3145736 | tf_op jit(solution)/shard_map/ppermute | solution.py:45
  58.1 2.4 %collective-permute-start.15 = (bf16[3,2,128,128]{3,2,1,0:T(8,128)(2,1)S(1)}, bf16[3,2,128,128]{3,2,1,0:T(8,128)(2,1)S(1)}, u32[]{:S(2)}, u32[]{:S(2)}) collective-permute-start(bf16[3,2,128,128]{3,2,1,0:T(8,128)(2,1)S(1)} %pad_maximum_fusion.2), channel_id=1, source_target_pairs={{0,16},{1,17},{2,18},{3,19},{4,20},{5,21},{6,22},{7,23},{8,24},{9,... | collective-permute-start | bytes 589832 | tf_op jit(solution)/shard_map/ppermute | solution.py:45
  61.9 5.9 %span_attention_begin.2 = (f32[4,384,128]{2,1,0:T(8,128)S(1)}, f32[4,384,256]{2,1,0:T(8,128)S(1)}) custom-call(s32[10]{0:T(128)S(1)} %pad_add_fusion.refs_0_.sc, bf16[8,3,128,128]{3,2,1,0:T(8,128)(2,1)S(1)} %all-to-all-done.refs_1_, bf16[16,2,128,128]{3,2,1,0:T(8,128)(2,1)S(1)} %constant_dynamic-update-slice_fusion.refs_2_, ...), custom_call_target="tpu_custom_call" | custom-call | flops 4026531840 | bytes 8000000 | tf_op jit(solution)/shard_map/span_attention_begin/pallas_call | solution.py:364
  74.8 6.3 %span_attention_end.2 = bf16[24,128,128]{2,1,0:T(8,128)(2,1)S(1)} custom-call(s32[10]{0:T(128)S(1)} %pad_add_fusion.refs_0_.sc, bf16[8,3,128,128]{3,2,1,0:T(8,128)(2,1)S(1)} %all-to-all-done.refs_1_, bf16[16,2,128,128]{3,2,1,0:T(8,128)(2,1)S(1)} %constant_dynamic-update-slice_fusion.5.refs_2_, bf16[16,2,128,128]{3,2,1,0:T(8,128)(2,1)S(1)} %collective-permute-done.18.refs_3_, ...), custom_call_target="tpu_custom_call" | custom-call | flops 4026531840 | bytes 8000000 | tf_op jit(solution)/shard_map/span_attention_end/pallas_call | solution.py:364
  81.5 16.3 %all_to_all.20.refs_1_ = bf16[8,3,128,128]{3,2,1,0:T(8,128)(2,1)S(1)} all-to-all(bf16[8,3,128,128]{3,2,1,0:T(8,128)(2,1)S(1)} %bitcast.27), channel_id=1, replica_groups={{0,1,4,5,64,65,68,69},{2,3,6,7,66,67,70,71},{8,9,12,13,72,73,76,77},{10..., dimensions={0} | all-to-all | bytes 1572864 | tf_op jit(solution)/shard_map/all_to_all | solution.py:65
  100.9 9.7 %collective-permute-done.20.away = bf16[2,128,768]{2,1,0:T(8,128)(2,1)S(1)} collective-permute-done((bf16[2,128,768]{2,1,0:T(8,128)(2,1)S(1)}, bf16[2,128,768]{2,1,0:T(8,128)(2,1)S(1)}, u32[]{:S(2)}, u32[]{:S(2)}) %collective-permute-start.20) | collective-permute-done | bytes 393248 | tf_op jit(solution)/shard_map/ppermute | solution.py:45
  110.6 4.8 %advance_modulate_project.1 = (bf16[8,3,128,128]{3,2,1,0:T(8,128)(2,1)}, bf16[2,128,128]{2,1,0:T(8,128)(2,1)S(1)}, bf16[32,3072]{1,0:T(8,128)(2,1)S(1)}, bf16[32,768]{1,0:T(8,128)(2,1)S(1)}, bf16[32,3840]{1,0:T(8,128)(2,1)S(1)}) custom-call(s32[10]{0:T(128)S(1)} %pad_add_fusion.refs_0_.sc, bf16[64,3072]{1,0:T(8,128)(2,1)S(1)} %bitcast.32, ...), custom_call_target="tpu_custom_call" | custom-call | flops 4000000000 | bytes 10000000 | tf_op jit(solution)/shard_map/advance_modulate_project/pallas_call | solution.py:223
  115.4 4.1 %all-to-all-start.2 = ((bf16[8,3,128,128]{3,2,1,0:T(8,128)(2,1)}), bf16[8,3,128,128]{3,2,1,0:T(8,128)(2,1)S(1)}, u32[]{:S(2)}, u32[]{:S(2)}) async-start(bf16[8,3,128,128]{3,2,1,0:T(8,128)(2,1)} %get-tuple-element.107), calls=%async_computation.2 | async-start | bytes 1572864 | tf_op jit(solution)/shard_map/all_to_all | solution.py:65
  121.5 8.1 %all-to-all-done.2.refs_1_ = bf16[8,3,128,128]{3,2,1,0:T(8,128)(2,1)S(1)} async-done(((bf16[8,3,128,128]{3,2,1,0:T(8,128)(2,1)}), bf16[8,3,128,128]{3,2,1,0:T(8,128)(2,1)S(1)}, u32[]{:S(2)}, u32[]{:S(2)}) %all-to-all-start.2) | async-done | bytes 786464 | tf_op jit(solution)/shard_map/all_to_all | solution.py:65
  129.7 2.4 %collective-permute-start.24 = (bf16[3,2,128,128]{3,2,1,0:T(8,128)(2,1)S(1)}, bf16[3,2,128,128]{3,2,1,0:T(8,128)(2,1)S(1)}, u32[]{:S(2)}, u32[]{:S(2)}) collective-permute-start(bf16[3,2,128,128]{3,2,1,0:T(8,128)(2,1)S(1)} %get-tuple-element.147), channel_id=1, source_target_pairs={{0,2},{1,3},{2,0},{3,1},{4,6},{5,7},{6,4},{7,5},{8,10},{9,11},{10,... | collective-permute-start | bytes 589832 | tf_op jit(solution)/shard_map/ppermute | solution.py:45
  140.5 2.6 %collective-permute-done.25 = bf16[3,2,128,128]{3,2,1,0:T(8,128)(2,1)S(1)} collective-permute-done((bf16[3,2,128,128]{3,2,1,0:T(8,128)(2,1)S(1)}, bf16[3,2,128,128]{3,2,1,0:T(8,128)(2,1)S(1)}, u32[]{:S(2)}, u32[]{:S(2)}) %collective-permute-start.25) | collective-permute-done | bytes 196640 | tf_op jit(solution)/shard_map/ppermute | solution.py:45
  143.2 3.8 %collective-permute-start.32 = (bf16[16,2,128,128]{3,2,1,0:T(8,128)(2,1)S(1)}, bf16[16,2,128,128]{3,2,1,0:T(8,128)(2,1)S(1)}, u32[]{:S(2)}, u32[]{:S(2)}) collective-permute-start(bf16[16,2,128,128]{3,2,1,0:T(8,128)(2,1)S(1)} %constant_dynamic-update-slice_fusion.9.refs_2_), channel_id=1, source_target_pairs={{0,32},{1,33},{2,34},{3,35},{4,36},{5,37},{6,38},{7,39},{8,40},{9,... | collective-permute-start | bytes 3145736 | tf_op jit(solution)/shard_map/ppermute | solution.py:45
  150.4 6.1 %span_attention_begin.3 = (f32[4,384,128]{2,1,0:T(8,128)S(1)}, f32[4,384,256]{2,1,0:T(8,128)S(1)}) custom-call(s32[10]{0:T(128)S(1)} %pad_add_fusion.refs_0_.sc, bf16[8,3,128,128]{3,2,1,0:T(8,128)(2,1)S(1)} %all-to-all-done.2.refs_1_, bf16[16,2,128,128]{3,2,1,0:T(8,128)(2,1)S(1)} %constant_dynamic-update-slice_fusion.9.refs_2_, ...), custom_call_target="tpu_custom_call" | custom-call | flops 4026531840 | bytes 8000000 | tf_op jit(solution)/shard_map/span_attention_begin/pallas_call | solution.py:364
  164.2 6.3 %span_attention_end.3 = bf16[24,128,128]{2,1,0:T(8,128)(2,1)S(1)} custom-call(s32[10]{0:T(128)S(1)} %pad_add_fusion.refs_0_.sc, bf16[8,3,128,128]{3,2,1,0:T(8,128)(2,1)S(1)} %all-to-all-done.2.refs_1_, bf16[16,2,128,128]{3,2,1,0:T(8,128)(2,1)S(1)} %constant_dynamic-update-slice_fusion.14.refs_2_, ...), custom_call_target="tpu_custom_call" | custom-call | flops 4026531840 | bytes 8000000 | tf_op jit(solution)/shard_map/span_attention_end/pallas_call | solution.py:364
  170.5 16.1 %all_to_all.21.refs_1_ = bf16[8,3,128,128]{3,2,1,0:T(8,128)(2,1)S(1)} all-to-all(bf16[8,3,128,128]{3,2,1,0:T(8,128)(2,1)S(1)} %bitcast.28), channel_id=1, replica_groups={{0,1,4,5,64,65,68,69},{2,3,6,7,66,67,70,71},{8,9,12,13,72,73,76,77},{10..., dimensions={0} | all-to-all | bytes 1572864 | tf_op jit(solution)/shard_map/all_to_all | solution.py:65
  194.5 2.9 %collective-permute-done.37.r3 = bf16[2,32,768]{2,1,0:T(8,128)(2,1)S(1)} collective-permute-done((bf16[2,32,768]{2,1,0:T(8,128)(2,1)S(1)}, bf16[2,32,768]{2,1,0:T(8,128)(2,1)S(1)}, u32[]{:S(2)}, u32[]{:S(2)}) %collective-permute-start.37) | collective-permute-done | bytes 98336 | tf_op jit(solution)/shard_map/ppermute | solution.py:45
  (128 shorter events, 66.1 us)
Async XLA Ops:
  2.1 12.4 %collective-permute-start.1 = (bf16[64,3072]{1,0:T(8,128)(2,1)}, bf16[64,3072]{1,0:T(8,128)(2,1)S(1)}, u32[]{:S(2)}, u32[]{:S(2)}) collective-permute-start(bf16[64,3072]{1,0:T(8,128)(2,1)} %bitcast.30), channel_id=1, source_target_pairs={{0,64},{1,65},{2,66},{3,67},{4,68},{5,69},{6,70},{7,71},{8,72},{9,... | collective-permute-start | bytes 1179656 | tf_op jit(solution)/shard_map/ppermute | solution.py:45
  22.2 17.8 %collective-permute-start.5 = (bf16[3072,768]{1,0:T(8,128)(2,1)}, bf16[3072,768]{1,0:T(8,128)(2,1)}, u32[]{:S(2)}, u32[]{:S(2)}) collective-permute-start(bf16[3072,768]{1,0:T(8,128)(2,1)} %x.1), channel_id=1, source_target_pairs={{0,32},{1,33},{2,34},{3,35},{4,36},{5,37},{6,38},{7,39},{8,40},{9,... | collective-permute-start | bytes 14155784 | tf_op jit(solution)/shard_map/ppermute | solution.py:45
  22.6 17.4 %all-to-all-start = ((bf16[8,3,128,128]{3,2,1,0:T(8,128)(2,1)}), bf16[8,3,128,128]{3,2,1,0:T(8,128)(2,1)S(1)}, u32[]{:S(2)}, u32[]{:S(2)}) async-start(bf16[8,3,128,128]{3,2,1,0:T(8,128)(2,1)} %get-tuple-element.77), calls=%async_computation | async-start | bytes 1572864 | tf_op jit(solution)/shard_map/all_to_all | solution.py:65
  40.2 12.5 %collective-permute-start.9 = (bf16[3,2,128,128]{3,2,1,0:T(8,128)(2,1)S(1)}, bf16[3,2,128,128]{3,2,1,0:T(8,128)(2,1)S(1)}, u32[]{:S(2)}, u32[]{:S(2)}) collective-permute-start(bf16[3,2,128,128]{3,2,1,0:T(8,128)(2,1)S(1)} %get-tuple-element.151), channel_id=1, source_target_pairs={{0,2},{1,3},{2,0},{3,1},{4,6},{5,7},{6,4},{7,5},{8,10},{9,11},{10,... | collective-permute-start | bytes 589832 | tf_op jit(solution)/shard_map/ppermute | solution.py:45
  42.9 9.8 %collective-permute-start.12 = (bf16[3,2,128,128]{3,2,1,0:T(8,128)(2,1)S(1)}, bf16[3,2,128,128]{3,2,1,0:T(8,128)(2,1)S(1)}, u32[]{:S(2)}, u32[]{:S(2)}) collective-permute-start(bf16[3,2,128,128]{3,2,1,0:T(8,128)(2,1)S(1)} %get-tuple-element.150), channel_id=1, source_target_pairs={{0,16},{1,17},{2,18},{3,19},{4,20},{5,21},{6,22},{7,23},{8,24},{9,... | collective-permute-start | bytes 589832 | tf_op jit(solution)/shard_map/ppermute | solution.py:45
  46.5 8.3 %collective-permute-start.11 = (bf16[3,2,128,128]{3,2,1,0:T(8,128)(2,1)S(1)}, bf16[3,2,128,128]{3,2,1,0:T(8,128)(2,1)S(1)}, u32[]{:S(2)}, u32[]{:S(2)}) collective-permute-start(bf16[3,2,128,128]{3,2,1,0:T(8,128)(2,1)S(1)} %get-tuple-element.150), channel_id=1, source_target_pairs={{0,24},{1,25},{2,26},{3,27},{4,28},{5,29},{6,30},{7,31},{8,0},{9,1... | collective-permute-start | bytes 589832 | tf_op jit(solution)/shard_map/ppermute | solution.py:45
  46.8 8.2 %collective-permute-start.10 = (bf16[3,2,128,128]{3,2,1,0:T(8,128)(2,1)S(1)}, bf16[3,2,128,128]{3,2,1,0:T(8,128)(2,1)S(1)}, u32[]{:S(2)}, u32[]{:S(2)}) collective-permute-start(bf16[3,2,128,128]{3,2,1,0:T(8,128)(2,1)S(1)} %get-tuple-element.150), channel_id=1, source_target_pairs={{0,8},{1,9},{2,10},{3,11},{4,12},{5,13},{6,14},{7,15},{8,16},{9,17... | collective-permute-start | bytes 589832 | tf_op jit(solution)/shard_map/ppermute | solution.py:45
  55.1 6.8 %collective-permute-start.17 = (bf16[16,2,128,128]{3,2,1,0:T(8,128)(2,1)S(1)}, bf16[16,2,128,128]{3,2,1,0:T(8,128)(2,1)S(1)}, u32[]{:S(2)}, u32[]{:S(2)}) collective-permute-start(bf16[16,2,128,128]{3,2,1,0:T(8,128)(2,1)S(1)} %constant_dynamic-update-slice_fusion.refs_2_), channel_id=1, source_target_pairs={{0,32},{1,33},{2,34},{3,35},{4,36},{5,37},{6,38},{7,39},{8,40},{9,... | collective-permute-start | bytes 3145736 | tf_op jit(solution)/shard_map/ppermute | solution.py:45
  57.7 13.7 %collective-permute-start.16 = (bf16[7,2,128,128]{3,2,1,0:T(8,128)(2,1)S(1)}, bf16[7,2,128,128]{3,2,1,0:T(8,128)(2,1)S(1)}, u32[]{:S(2)}, u32[]{:S(2)}) collective-permute-start(bf16[7,2,128,128]{3,2,1,0:T(8,128)(2,1)S(1)} %pad_maximum_fusion), channel_id=1, source_target_pairs={{0,2},{1,3},{2,0},{3,1},{4,6},{5,7},{6,4},{7,5},{8,10},{9,11},{10,... | collective-permute-start | bytes 1376264 | tf_op jit(solution)/shard_map/ppermute | solution.py:45
  58.1 9.7 %collective-permute-start.15 = (bf16[3,2,128,128]{3,2,1,0:T(8,128)(2,1)S(1)}, bf16[3,2,128,128]{3,2,1,0:T(8,128)(2,1)S(1)}, u32[]{:S(2)}, u32[]{:S(2)}) collective-permute-start(bf16[3,2,128,128]{3,2,1,0:T(8,128)(2,1)S(1)} %pad_maximum_fusion.2), channel_id=1, source_target_pairs={{0,16},{1,17},{2,18},{3,19},{4,20},{5,21},{6,22},{7,23},{8,24},{9,... | collective-permute-start | bytes 589832 | tf_op jit(solution)/shard_map/ppermute | solution.py:45
  60.4 9.6 %collective-permute-start.14 = (bf16[3,2,128,128]{3,2,1,0:T(8,128)(2,1)S(1)}, bf16[3,2,128,128]{3,2,1,0:T(8,128)(2,1)S(1)}, u32[]{:S(2)}, u32[]{:S(2)}) collective-permute-start(bf16[3,2,128,128]{3,2,1,0:T(8,128)(2,1)S(1)} %pad_maximum_fusion.2), channel_id=1, source_target_pairs={{0,24},{1,25},{2,26},{3,27},{4,28},{5,29},{6,30},{7,31},{8,0},{9,1... | collective-permute-start | bytes 589832 | tf_op jit(solution)/shard_map/ppermute | solution.py:45
  61.3 9.1 %collective-permute-start.13 = (bf16[3,2,128,128]{3,2,1,0:T(8,128)(2,1)S(1)}, bf16[3,2,128,128]{3,2,1,0:T(8,128)(2,1)S(1)}, u32[]{:S(2)}, u32[]{:S(2)}) collective-permute-start(bf16[3,2,128,128]{3,2,1,0:T(8,128)(2,1)S(1)} %pad_maximum_fusion.2), channel_id=1, source_target_pairs={{0,8},{1,9},{2,10},{3,11},{4,12},{5,13},{6,14},{7,15},{8,16},{9,17... | collective-permute-start | bytes 589832 | tf_op jit(solution)/shard_map/ppermute | solution.py:45
  81.1 16.8 %collective-permute-start.19 = (bf16[3072,1280]{1,0:T(8,128)(2,1)S(1)}, bf16[3072,1280]{1,0:T(8,128)(2,1)S(1)}, u32[]{:S(2)}, u32[]{:S(2)}) collective-permute-start(bf16[3072,1280]{1,0:T(8,128)(2,1)S(1)} %bitcast.26), channel_id=1, source_target_pairs={{0,32},{1,33},{2,34},{3,35},{4,36},{5,37},{6,38},{7,39},{8,40},{9,... | collective-permute-start | bytes 23592968 | tf_op jit(solution)/shard_map/ppermute | solution.py:45
  99.9 10.7 %collective-permute-start.20 = (bf16[2,128,768]{2,1,0:T(8,128)(2,1)S(1)}, bf16[2,128,768]{2,1,0:T(8,128)(2,1)S(1)}, u32[]{:S(2)}, u32[]{:S(2)}) collective-permute-start(bf16[2,128,768]{2,1,0:T(8,128)(2,1)S(1)} %out_projection.2.here), channel_id=1, source_target_pairs={{0,64},{1,65},{2,66},{3,67},{4,68},{5,69},{6,70},{7,71},{8,72},{9,... | collective-permute-start | bytes 1179656 | tf_op jit(solution)/shard_map/ppermute | solution.py:45
  115.4 14.2 %all-to-all-start.2 = ((bf16[8,3,128,128]{3,2,1,0:T(8,128)(2,1)}), bf16[8,3,128,128]{3,2,1,0:T(8,128)(2,1)S(1)}, u32[]{:S(2)}, u32[]{:S(2)}) async-start(bf16[8,3,128,128]{3,2,1,0:T(8,128)(2,1)} %get-tuple-element.107), calls=%async_computation.2 | async-start | bytes 1572864 | tf_op jit(solution)/shard_map/all_to_all | solution.py:65
  129.7 10.7 %collective-permute-start.24 = (bf16[3,2,128,128]{3,2,1,0:T(8,128)(2,1)S(1)}, bf16[3,2,128,128]{3,2,1,0:T(8,128)(2,1)S(1)}, u32[]{:S(2)}, u32[]{:S(2)}) collective-permute-start(bf16[3,2,128,128]{3,2,1,0:T(8,128)(2,1)S(1)} %get-tuple-element.147), channel_id=1, source_target_pairs={{0,2},{1,3},{2,0},{3,1},{4,6},{5,7},{6,4},{7,5},{8,10},{9,11},{10,... | collective-permute-start | bytes 589832 | tf_op jit(solution)/shard_map/ppermute | solution.py:45
  132.1 8.4 %collective-permute-start.27 = (bf16[3,2,128,128]{3,2,1,0:T(8,128)(2,1)S(1)}, bf16[3,2,128,128]{3,2,1,0:T(8,128)(2,1)S(1)}, u32[]{:S(2)}, u32[]{:S(2)}) collective-permute-start(bf16[3,2,128,128]{3,2,1,0:T(8,128)(2,1)S(1)} %get-tuple-element.146), channel_id=1, source_target_pairs={{0,16},{1,17},{2,18},{3,19},{4,20},{5,21},{6,22},{7,23},{8,24},{9,... | collective-permute-start | bytes 589832 | tf_op jit(solution)/shard_map/ppermute | solution.py:45
  135.2 7.9 %collective-permute-start.25 = (bf16[3,2,128,128]{3,2,1,0:T(8,128)(2,1)S(1)}, bf16[3,2,128,128]{3,2,1,0:T(8,128)(2,1)S(1)}, u32[]{:S(2)}, u32[]{:S(2)}) collective-permute-start(bf16[3,2,128,128]{3,2,1,0:T(8,128)(2,1)S(1)} %get-tuple-element.146), channel_id=1, source_target_pairs={{0,8},{1,9},{2,10},{3,11},{4,12},{5,13},{6,14},{7,15},{8,16},{9,17... | collective-permute-start | bytes 589832 | tf_op jit(solution)/shard_map/ppermute | solution.py:45
  143.2 7.2 %collective-permute-start.32 = (bf16[16,2,128,128]{3,2,1,0:T(8,128)(2,1)S(1)}, bf16[16,2,128,128]{3,2,1,0:T(8,128)(2,1)S(1)}, u32[]{:S(2)}, u32[]{:S(2)}) collective-permute-start(bf16[16,2,128,128]{3,2,1,0:T(8,128)(2,1)S(1)} %constant_dynamic-update-slice_fusion.9.refs_2_), channel_id=1, source_target_pairs={{0,32},{1,33},{2,34},{3,35},{4,36},{5,37},{6,38},{7,39},{8,40},{9,... | collective-permute-start | bytes 3145736 | tf_op jit(solution)/shard_map/ppermute | solution.py:45
  147.2 13.7 %collective-permute-start.31 = (bf16[7,2,128,128]{3,2,1,0:T(8,128)(2,1)S(1)}, bf16[7,2,128,128]{3,2,1,0:T(8,128)(2,1)S(1)}, u32[]{:S(2)}, u32[]{:S(2)}) collective-permute-start(bf16[7,2,128,128]{3,2,1,0:T(8,128)(2,1)S(1)} %pad_maximum_fusion.1), channel_id=1, source_target_pairs={{0,2},{1,3},{2,0},{3,1},{4,6},{5,7},{6,4},{7,5},{8,10},{9,11},{10,... | collective-permute-start | bytes 1376264 | tf_op jit(solution)/shard_map/ppermute | solution.py:45
  148.0 8.5 %collective-permute-start.30 = (bf16[3,2,128,128]{3,2,1,0:T(8,128)(2,1)S(1)}, bf16[3,2,128,128]{3,2,1,0:T(8,128)(2,1)S(1)}, u32[]{:S(2)}, u32[]{:S(2)}) collective-permute-start(bf16[3,2,128,128]{3,2,1,0:T(8,128)(2,1)S(1)} %pad_maximum_fusion.3), channel_id=1, source_target_pairs={{0,16},{1,17},{2,18},{3,19},{4,20},{5,21},{6,22},{7,23},{8,24},{9,... | collective-permute-start | bytes 589832 | tf_op jit(solution)/shard_map/ppermute | solution.py:45
  149.0 9.7 %collective-permute-start.29 = (bf16[3,2,128,128]{3,2,1,0:T(8,128)(2,1)S(1)}, bf16[3,2,128,128]{3,2,1,0:T(8,128)(2,1)S(1)}, u32[]{:S(2)}, u32[]{:S(2)}) collective-permute-start(bf16[3,2,128,128]{3,2,1,0:T(8,128)(2,1)S(1)} %pad_maximum_fusion.3), channel_id=1, source_target_pairs={{0,24},{1,25},{2,26},{3,27},{4,28},{5,29},{6,30},{7,31},{8,0},{9,1... | collective-permute-start | bytes 589832 | tf_op jit(solution)/shard_map/ppermute | solution.py:45
  149.9 10.7 %collective-permute-start.28 = (bf16[3,2,128,128]{3,2,1,0:T(8,128)(2,1)S(1)}, bf16[3,2,128,128]{3,2,1,0:T(8,128)(2,1)S(1)}, u32[]{:S(2)}, u32[]{:S(2)}) collective-permute-start(bf16[3,2,128,128]{3,2,1,0:T(8,128)(2,1)S(1)} %pad_maximum_fusion.3), channel_id=1, source_target_pairs={{0,8},{1,9},{2,10},{3,11},{4,12},{5,13},{6,14},{7,15},{8,16},{9,17... | collective-permute-start | bytes 589832 | tf_op jit(solution)/shard_map/ppermute | solution.py:45
  186.6 11.9 %collective-permute-start.34 = (bf16[32,3840]{1,0:T(8,128)(2,1)S(1)}, bf16[32,3840]{1,0:T(8,128)(2,1)S(1)}, u32[]{:S(2)}, u32[]{:S(2)}) collective-permute-start(bf16[32,3840]{1,0:T(8,128)(2,1)S(1)} %get-tuple-element.128), channel_id=1, source_target_pairs={{0,32},{1,33},{2,34},{3,35},{4,36},{5,37},{6,38},{7,39},{8,40},{9,... | collective-permute-start | bytes 737288 | tf_op jit(solution)/shard_map/ppermute | solution.py:45
  (25 other events, 133.5 us)

commit v4 on v3

--- a/solution.py
+++ b/solution.py
@@ -259,10 +259,12 @@
 QROWS = 4 * 3 * HALF
 
 
-def attend_body(step, parts, chunk, block, last, sc, q, *refs):
+def attend_body(step, parts, chunk, block, last, sc, *refs):
+    if not last:
+        q, refs = refs[0], refs[1:]
     blocks, refs = refs[:parts], refs[parts:]
     if last:
-        top_in, acc_in, out, qs, ks, vs = refs
+        top_in, acc_in, qs, out, ks, vs = refs
     else:
         top_out, acc_out, qs, ks, vs = refs
     keys = ks.shape[0] // SLOTS
@@ -277,17 +279,18 @@
                 vs[to, :HD] = ref[b, 1, rows, :]
             at += 1
     vs[:, HD:] = jnp.ones((SLOTS * keys, HD), BF)
-    factor = LOG2E / math.sqrt(HD)
-    for c in range(4):
-        for m in range(3):
-            near = q[c, m].astype(F32)
-            other = q[4 + c, m].astype(F32)
-            if m == 2:
-                near = near + other
-            both = (jnp.where(sc[9] == 7, other, near) * factor).astype(BF)
-            for j in range(SLOTS):
-                to = pl.ds(pl.multiple_of(ranks[j] * QROWS + (c * 3 + m) * HALF, HALF), HALF)
-                qs[to, :] = both[j * HALF : (j + 1) * HALF]
+    if not last:
+        factor = LOG2E / math.sqrt(HD)
+        for c in range(4):
+            for m in range(3):
+                near = q[c, m].astype(F32)
+                other = q[4 + c, m].astype(F32)
+                if m == 2:
+                    near = near + other
+                both = (jnp.where(sc[9] == 7, other, near) * factor).astype(BF)
+                for j in range(SLOTS):
+                    to = pl.ds(pl.multiple_of(ranks[j] * QROWS + (c * 3 + m) * HALF, HALF), HALF)
+                    qs[to, :] = both[j * HALF : (j + 1) * HALF]
 
     def some_rows(index, _):
         r = pl.multiple_of(index * block, block)
@@ -349,7 +352,6 @@
         attend_body(step, len(blocks), chunk, block, last, *refs)
 
     scratch = [
-        pltpu.VMEM((SLOTS * QROWS, HD), BF),
         pltpu.VMEM((SLOTS * keys, HD), BF),
         pltpu.VMEM((SLOTS * keys, 2 * HD), BF),
     ]
@@ -359,12 +361,13 @@
         out_shape = [
             jax.ShapeDtypeStruct((SLOTS, QROWS, HD), F32),
             jax.ShapeDtypeStruct((SLOTS, QROWS, 2 * HD), F32),
+            jax.ShapeDtypeStruct((SLOTS * QROWS, HD), BF),
         ]
     pairs = 10 * QROWS * keys
     return pl.pallas_call(
         body,
-        in_specs=[SM] + [VM] * (1 + len(blocks) + (2 if last else 0)),
-        out_specs=VM if last else [VM, VM],
+        in_specs=[SM] + [VM] * (len(blocks) + (3 if last else 1)),
+        out_specs=VM if last else [VM] * 3,
         out_shape=out_shape,
         scratch_shapes=scratch,
         compiler_params=params(20 if last else 18),
@@ -372,7 +375,7 @@
             flops=pairs * HD * 8, bytes_accessed=8 * 10**6, transcendentals=pairs
         ),
         name="span_attention_end" if last else "span_attention_begin",
-    )(sc, q, *blocks, *(state or ()))
+    )(sc, *(() if last else (q,)), *blocks, *(state or ()))
 
 
 def out_body(step, sc, mine, ada, w, w_pair, out, attn):

time: 201 us -> 201 us (level)
  no operation moved by 1% of the time
where the time goes in v4:
time: 201 us; the launch traced here: 200 us
  starting transfers between devices  55.5 us (28%)
  waiting for transfers between devices  53.4 us (27%)
  Pallas kernels  50.2 us (25%)
  blocking collectives  32.6 us (16%)
  local copies, waits for them, and re-layouts  6 us (3%)
    ppermute x32, starting transfers between devices, move(): return lax.ppermute(x, AXES, pairs)  42.1 us
    ppermute x32, waiting for transfers between devices, move(): return lax.ppermute(x, AXES, pairs)  34.9 us
    all_to_all x2, blocking collectives, exchange(): lax.all_to_all(x, AXES, 0, 0, tiled=True, axis_index_groups=group_lists())  32.6 us
    pallas_call x4, Pallas kernels, attend(): pl.pallas_call(body, in_specs=[SM] + [VM] * (len(blocks) + (3 if last els...  24 us
    all_to_all x2, waiting for transfers between devices, exchange(): lax.all_to_all(x, AXES, 0, 0, tiled=True, axis_index_groups=group_lists())  18.5 us
    pallas_call x4, Pallas kernels, hold(): pl.pallas_call(body, in_specs=[pl.BlockSpec(memory_space=pl.ANY)], out_sp...  9.38 us
    all_to_all x2, starting transfers between devices, exchange(): lax.all_to_all(x, AXES, 0, 0, tiled=True, axis_index_groups=group_lists())  9.18 us
    unnamed x30, local copies, waits for them, and re-layouts  5.58 us
  transfers between devices with their start and end apart: 40, of which 19 were waited for; matrix products, arithmetic and copies ran while one was open for 1% of the time, Pallas kernels for 14%

profile of v4, /device:TPU:1, one launch (start us, length us, event | category | flops | bytes accessed | tf_op | source)
XLA Modules:
  0.0 199.9 jit_solution(3567517105525049142)
XLA Ops:
  2.1 2.8 %collective-permute-start.1 = (bf16[64,3072]{1,0:T(8,128)(2,1)}, bf16[64,3072]{1,0:T(8,128)(2,1)S(1)}, u32[]{:S(2)}, u32[]{:S(2)}) collective-permute-start(bf16[64,3072]{1,0:T(8,128)(2,1)} %bitcast.30), channel_id=1, source_target_pairs={{0,64},{1,65},{2,66},{3,67},{4,68},{5,69},{6,70},{7,71},{8,72},{9,... | collective-permute-start | bytes 1179656 | tf_op jit(solution)/shard_map/ppermute | solution.py:45
  5.7 3.2 %copy-done = bf16[3072,1280]{1,0:T(8,128)(2,1)S(1)} copy-done((bf16[3072,1280]{1,0:T(8,128)(2,1)S(1)}, bf16[3072,1280]{1,0:T(8,128)(2,1)}, u32[]{:S(2)}) %copy-start) | copy-done | bytes 7864344
  11.0 2.5 %modulate_project.2 = (bf16[10,64,128]{2,1,0:T(8,128)(2,1)S(1)}, bf16[10,64,128]{2,1,0:T(8,128)(2,1)S(1)}) custom-call(s32[10]{0:T(128)S(1)} %pad_add_fusion.refs_0_.sc, bf16[64,3072]{1,0:T(8,128)(2,1)S(1)} %bitcast.31, bf16[64,3072]{1,0:T(8,128)(2,1)S(1)} %collective-permute-done.refs_2_.x1, f32[9,3,3072]{2,1,0:T(4,128)S(1)} %copy-done.2, ...), custom_call_target="tpu_custom_call" | custom-call | flops 4000000000 | bytes 10000000 | tf_op jit(solution)/shard_map/modulate_project/pallas_call | solution.py:210
  16.7 2.5 %modulate_project.3 = (bf16[10,64,128]{2,1,0:T(8,128)(2,1)S(1)}, bf16[10,64,128]{2,1,0:T(8,128)(2,1)S(1)}) custom-call(s32[10]{0:T(128)S(1)} %pad_add_fusion.refs_0_.sc, bf16[64,3072]{1,0:T(8,128)(2,1)S(1)} %collective-permute-done.1.refs_1_.x2, bf16[64,3072]{1,0:T(8,128)(2,1)S(1)} %collective-permute-done.2.refs_2_.x3, f32[9,3,3072]{2,1,0:T(4,128)S(1)} %copy-done.2, ...), custom_call_target="tpu_custom_call" | custom-call | flops 4000000000 | bytes 10000000 | tf_op jit(solution)/shard_map/modulate_project/pallas_call | solution.py:210
  22.6 5.1 %all-to-all-start = ((bf16[8,3,128,128]{3,2,1,0:T(8,128)(2,1)}), bf16[8,3,128,128]{3,2,1,0:T(8,128)(2,1)S(1)}, u32[]{:S(2)}, u32[]{:S(2)}) async-start(bf16[8,3,128,128]{3,2,1,0:T(8,128)(2,1)} %get-tuple-element.81), calls=%async_computation | async-start | bytes 1572864 | tf_op jit(solution)/shard_map/all_to_all | solution.py:65
  29.8 10.2 %all-to-all-done.refs_1_ = bf16[8,3,128,128]{3,2,1,0:T(8,128)(2,1)S(1)} async-done(((bf16[8,3,128,128]{3,2,1,0:T(8,128)(2,1)}), bf16[8,3,128,128]{3,2,1,0:T(8,128)(2,1)S(1)}, u32[]{:S(2)}, u32[]{:S(2)}) %all-to-all-start) | async-done | bytes 786464 | tf_op jit(solution)/shard_map/all_to_all | solution.py:65
  40.2 2.7 %collective-permute-start.9 = (bf16[3,2,128,128]{3,2,1,0:T(8,128)(2,1)S(1)}, bf16[3,2,128,128]{3,2,1,0:T(8,128)(2,1)S(1)}, u32[]{:S(2)}, u32[]{:S(2)}) collective-permute-start(bf16[3,2,128,128]{3,2,1,0:T(8,128)(2,1)S(1)} %get-tuple-element.159), channel_id=1, source_target_pairs={{0,2},{1,3},{2,0},{3,1},{4,6},{5,7},{6,4},{7,5},{8,10},{9,11},{10,... | collective-permute-start | bytes 589832 | tf_op jit(solution)/shard_map/ppermute | solution.py:45
  42.9 3.6 %collective-permute-start.12 = (bf16[3,2,128,128]{3,2,1,0:T(8,128)(2,1)S(1)}, bf16[3,2,128,128]{3,2,1,0:T(8,128)(2,1)S(1)}, u32[]{:S(2)}, u32[]{:S(2)}) collective-permute-start(bf16[3,2,128,128]{3,2,1,0:T(8,128)(2,1)S(1)} %get-tuple-element.158), channel_id=1, source_target_pairs={{0,16},{1,17},{2,18},{3,19},{4,20},{5,21},{6,22},{7,23},{8,24},{9,... | collective-permute-start | bytes 589832 | tf_op jit(solution)/shard_map/ppermute | solution.py:45
  55.2 2.4 %collective-permute-start.17 = (bf16[16,2,128,128]{3,2,1,0:T(8,128)(2,1)S(1)}, bf16[16,2,128,128]{3,2,1,0:T(8,128)(2,1)S(1)}, u32[]{:S(2)}, u32[]{:S(2)}) collective-permute-start(bf16[16,2,128,128]{3,2,1,0:T(8,128)(2,1)S(1)} %constant_dynamic-update-slice_fusion.refs_2_), channel_id=1, source_target_pairs={{0,32},{1,33},{2,34},{3,35},{4,36},{5,37},{6,38},{7,39},{8,40},{9,... | collective-permute-start | bytes 3145736 | tf_op jit(solution)/shard_map/ppermute | solution.py:45
  61.9 5.9 %span_attention_begin.2 = (f32[4,384,128]{2,1,0:T(8,128)S(1)}, f32[4,384,256]{2,1,0:T(8,128)S(1)}, bf16[1536,128]{1,0:T(8,128)(2,1)S(1)}) custom-call(s32[10]{0:T(128)S(1)} %pad_add_fusion.refs_0_.sc, bf16[8,3,128,128]{3,2,1,0:T(8,128)(2,1)S(1)} %all-to-all-done.refs_1_, bf16[16,2,128,128]{3,2,1,0:T(8,128)(2,1)S(1)} %constant_dynamic-update-slice_fusion.refs_2_, ...), custom_call_target="tpu_custom_call" | custom-call | flops 4026531840 | bytes 8000000 | tf_op jit(solution)/shard_map/span_attention_begin/pallas_call | solution.py:367
  74.8 6.1 %span_attention_end.2 = bf16[24,128,128]{2,1,0:T(8,128)(2,1)S(1)} custom-call(s32[10]{0:T(128)S(1)} %pad_add_fusion.refs_0_.sc, bf16[16,2,128,128]{3,2,1,0:T(8,128)(2,1)S(1)} %constant_dynamic-update-slice_fusion.5.refs_1_, bf16[16,2,128,128]{3,2,1,0:T(8,128)(2,1)S(1)} %collective-permute-done.18.refs_2_, f32[4,384,128]{2,1,0:T(8,128)S(1)} %get-tuple-element.102.refs_3_, ...), custom_call_target="tpu_custom_call" | custom-call | flops 4026531840 | bytes 8000000 | tf_op jit(solution)/shard_map/span_attention_end/pallas_call | solution.py:367
  81.5 16.3 %all_to_all.20.refs_1_ = bf16[8,3,128,128]{3,2,1,0:T(8,128)(2,1)S(1)} all-to-all(bf16[8,3,128,128]{3,2,1,0:T(8,128)(2,1)S(1)} %bitcast.27), channel_id=1, replica_groups={{0,1,4,5,64,65,68,69},{2,3,6,7,66,67,70,71},{8,9,12,13,72,73,76,77},{10..., dimensions={0} | all-to-all | bytes 1572864 | tf_op jit(solution)/shard_map/all_to_all | solution.py:65
  100.8 9.7 %collective-permute-done.20.away = bf16[2,128,768]{2,1,0:T(8,128)(2,1)S(1)} collective-permute-done((bf16[2,128,768]{2,1,0:T(8,128)(2,1)S(1)}, bf16[2,128,768]{2,1,0:T(8,128)(2,1)S(1)}, u32[]{:S(2)}, u32[]{:S(2)}) %collective-permute-start.20) | collective-permute-done | bytes 393248 | tf_op jit(solution)/shard_map/ppermute | solution.py:45
  110.5 4.8 %advance_modulate_project.1 = (bf16[8,3,128,128]{3,2,1,0:T(8,128)(2,1)}, bf16[2,128,128]{2,1,0:T(8,128)(2,1)S(1)}, bf16[32,3072]{1,0:T(8,128)(2,1)S(1)}, bf16[32,768]{1,0:T(8,128)(2,1)S(1)}, bf16[32,3840]{1,0:T(8,128)(2,1)S(1)}) custom-call(s32[10]{0:T(128)S(1)} %pad_add_fusion.refs_0_.sc, bf16[64,3072]{1,0:T(8,128)(2,1)S(1)} %bitcast.32, ...), custom_call_target="tpu_custom_call" | custom-call | flops 4000000000 | bytes 10000000 | tf_op jit(solution)/shard_map/advance_modulate_project/pallas_call | solution.py:223
  115.3 4.1 %all-to-all-start.2 = ((bf16[8,3,128,128]{3,2,1,0:T(8,128)(2,1)}), bf16[8,3,128,128]{3,2,1,0:T(8,128)(2,1)S(1)}, u32[]{:S(2)}, u32[]{:S(2)}) async-start(bf16[8,3,128,128]{3,2,1,0:T(8,128)(2,1)} %get-tuple-element.113), calls=%async_computation.2 | async-start | bytes 1572864 | tf_op jit(solution)/shard_map/all_to_all | solution.py:65
  121.6 8.2 %all-to-all-done.2.refs_1_ = bf16[8,3,128,128]{3,2,1,0:T(8,128)(2,1)S(1)} async-done(((bf16[8,3,128,128]{3,2,1,0:T(8,128)(2,1)}), bf16[8,3,128,128]{3,2,1,0:T(8,128)(2,1)S(1)}, u32[]{:S(2)}, u32[]{:S(2)}) %all-to-all-start.2) | async-done | bytes 786464 | tf_op jit(solution)/shard_map/all_to_all | solution.py:65
  130.0 2.4 %collective-permute-start.24 = (bf16[3,2,128,128]{3,2,1,0:T(8,128)(2,1)S(1)}, bf16[3,2,128,128]{3,2,1,0:T(8,128)(2,1)S(1)}, u32[]{:S(2)}, u32[]{:S(2)}) collective-permute-start(bf16[3,2,128,128]{3,2,1,0:T(8,128)(2,1)S(1)} %get-tuple-element.155), channel_id=1, source_target_pairs={{0,2},{1,3},{2,0},{3,1},{4,6},{5,7},{6,4},{7,5},{8,10},{9,11},{10,... | collective-permute-start | bytes 589832 | tf_op jit(solution)/shard_map/ppermute | solution.py:45
  140.7 2.6 %collective-permute-done.25 = bf16[3,2,128,128]{3,2,1,0:T(8,128)(2,1)S(1)} collective-permute-done((bf16[3,2,128,128]{3,2,1,0:T(8,128)(2,1)S(1)}, bf16[3,2,128,128]{3,2,1,0:T(8,128)(2,1)S(1)}, u32[]{:S(2)}, u32[]{:S(2)}) %collective-permute-start.25) | collective-permute-done | bytes 196640 | tf_op jit(solution)/shard_map/ppermute | solution.py:45
  143.4 3.5 %collective-permute-start.32 = (bf16[16,2,128,128]{3,2,1,0:T(8,128)(2,1)S(1)}, bf16[16,2,128,128]{3,2,1,0:T(8,128)(2,1)S(1)}, u32[]{:S(2)}, u32[]{:S(2)}) collective-permute-start(bf16[16,2,128,128]{3,2,1,0:T(8,128)(2,1)S(1)} %constant_dynamic-update-slice_fusion.9.refs_2_), channel_id=1, source_target_pairs={{0,32},{1,33},{2,34},{3,35},{4,36},{5,37},{6,38},{7,39},{8,40},{9,... | collective-permute-start | bytes 3145736 | tf_op jit(solution)/shard_map/ppermute | solution.py:45
  150.3 5.9 %span_attention_begin.3 = (f32[4,384,128]{2,1,0:T(8,128)S(1)}, f32[4,384,256]{2,1,0:T(8,128)S(1)}, bf16[1536,128]{1,0:T(8,128)(2,1)S(1)}) custom-call(s32[10]{0:T(128)S(1)} %pad_add_fusion.refs_0_.sc, bf16[8,3,128,128]{3,2,1,0:T(8,128)(2,1)S(1)} %all-to-all-done.2.refs_1_, bf16[16,2,128,128]{3,2,1,0:T(8,128)(2,1)S(1)} %constant_dynamic-update-slice_fusion.9.refs_2_, ...), custom_call_target="tpu_custom_call" | custom-call | flops 4026531840 | bytes 8000000 | tf_op jit(solution)/shard_map/span_attention_begin/pallas_call | solution.py:367
  156.2 2.4 %collective-permute-done.29 = bf16[3,2,128,128]{3,2,1,0:T(8,128)(2,1)S(1)} collective-permute-done((bf16[3,2,128,128]{3,2,1,0:T(8,128)(2,1)S(1)}, bf16[3,2,128,128]{3,2,1,0:T(8,128)(2,1)S(1)}, u32[]{:S(2)}, u32[]{:S(2)}) %collective-permute-start.29) | collective-permute-done | bytes 196640 | tf_op jit(solution)/shard_map/ppermute | solution.py:45
  164.1 6.1 %span_attention_end.3 = bf16[24,128,128]{2,1,0:T(8,128)(2,1)S(1)} custom-call(s32[10]{0:T(128)S(1)} %pad_add_fusion.refs_0_.sc, bf16[16,2,128,128]{3,2,1,0:T(8,128)(2,1)S(1)} %constant_dynamic-update-slice_fusion.14.refs_1_, bf16[16,2,128,128]{3,2,1,0:T(8,128)(2,1)S(1)} %collective-permute-done.33.refs_2_, f32[4,384,128]{2,1,0:T(8,128)S(1)} %get-tuple-element.132.refs_3_, ...), custom_call_target="tpu_custom_call" | custom-call | flops 4026531840 | bytes 8000000 | tf_op jit(solution)/shard_map/span_attention_end/pallas_call | solution.py:367
  170.3 16.2 %all_to_all.21.refs_1_ = bf16[8,3,128,128]{3,2,1,0:T(8,128)(2,1)S(1)} all-to-all(bf16[8,3,128,128]{3,2,1,0:T(8,128)(2,1)S(1)} %bitcast.28), channel_id=1, replica_groups={{0,1,4,5,64,65,68,69},{2,3,6,7,66,67,70,71},{8,9,12,13,72,73,76,77},{10..., dimensions={0} | all-to-all | bytes 1572864 | tf_op jit(solution)/shard_map/all_to_all | solution.py:65
  194.4 2.9 %collective-permute-done.37.r3 = bf16[2,32,768]{2,1,0:T(8,128)(2,1)S(1)} collective-permute-done((bf16[2,32,768]{2,1,0:T(8,128)(2,1)S(1)}, bf16[2,32,768]{2,1,0:T(8,128)(2,1)S(1)}, u32[]{:S(2)}, u32[]{:S(2)}) %collective-permute-start.37) | collective-permute-done | bytes 98336 | tf_op jit(solution)/shard_map/ppermute | solution.py:45
  (128 shorter events, 66.6 us)
Async XLA Ops:
  2.1 12.4 %collective-permute-start.1 = (bf16[64,3072]{1,0:T(8,128)(2,1)}, bf16[64,3072]{1,0:T(8,128)(2,1)S(1)}, u32[]{:S(2)}, u32[]{:S(2)}) collective-permute-start(bf16[64,3072]{1,0:T(8,128)(2,1)} %bitcast.30), channel_id=1, source_target_pairs={{0,64},{1,65},{2,66},{3,67},{4,68},{5,69},{6,70},{7,71},{8,72},{9,... | collective-permute-start | bytes 1179656 | tf_op jit(solution)/shard_map/ppermute | solution.py:45
  22.2 17.8 %collective-permute-start.5 = (bf16[3072,768]{1,0:T(8,128)(2,1)}, bf16[3072,768]{1,0:T(8,128)(2,1)}, u32[]{:S(2)}, u32[]{:S(2)}) collective-permute-start(bf16[3072,768]{1,0:T(8,128)(2,1)} %x.1), channel_id=1, source_target_pairs={{0,32},{1,33},{2,34},{3,35},{4,36},{5,37},{6,38},{7,39},{8,40},{9,... | collective-permute-start | bytes 14155784 | tf_op jit(solution)/shard_map/ppermute | solution.py:45
  22.6 17.4 %all-to-all-start = ((bf16[8,3,128,128]{3,2,1,0:T(8,128)(2,1)}), bf16[8,3,128,128]{3,2,1,0:T(8,128)(2,1)S(1)}, u32[]{:S(2)}, u32[]{:S(2)}) async-start(bf16[8,3,128,128]{3,2,1,0:T(8,128)(2,1)} %get-tuple-element.81), calls=%async_computation | async-start | bytes 1572864 | tf_op jit(solution)/shard_map/all_to_all | solution.py:65
  40.2 12.5 %collective-permute-start.9 = (bf16[3,2,128,128]{3,2,1,0:T(8,128)(2,1)S(1)}, bf16[3,2,128,128]{3,2,1,0:T(8,128)(2,1)S(1)}, u32[]{:S(2)}, u32[]{:S(2)}) collective-permute-start(bf16[3,2,128,128]{3,2,1,0:T(8,128)(2,1)S(1)} %get-tuple-element.159), channel_id=1, source_target_pairs={{0,2},{1,3},{2,0},{3,1},{4,6},{5,7},{6,4},{7,5},{8,10},{9,11},{10,... | collective-permute-start | bytes 589832 | tf_op jit(solution)/shard_map/ppermute | solution.py:45
  42.9 9.8 %collective-permute-start.12 = (bf16[3,2,128,128]{3,2,1,0:T(8,128)(2,1)S(1)}, bf16[3,2,128,128]{3,2,1,0:T(8,128)(2,1)S(1)}, u32[]{:S(2)}, u32[]{:S(2)}) collective-permute-start(bf16[3,2,128,128]{3,2,1,0:T(8,128)(2,1)S(1)} %get-tuple-element.158), channel_id=1, source_target_pairs={{0,16},{1,17},{2,18},{3,19},{4,20},{5,21},{6,22},{7,23},{8,24},{9,... | collective-permute-start | bytes 589832 | tf_op jit(solution)/shard_map/ppermute | solution.py:45
  46.5 8.3 %collective-permute-start.11 = (bf16[3,2,128,128]{3,2,1,0:T(8,128)(2,1)S(1)}, bf16[3,2,128,128]{3,2,1,0:T(8,128)(2,1)S(1)}, u32[]{:S(2)}, u32[]{:S(2)}) collective-permute-start(bf16[3,2,128,128]{3,2,1,0:T(8,128)(2,1)S(1)} %get-tuple-element.158), channel_id=1, source_target_pairs={{0,24},{1,25},{2,26},{3,27},{4,28},{5,29},{6,30},{7,31},{8,0},{9,1... | collective-permute-start | bytes 589832 | tf_op jit(solution)/shard_map/ppermute | solution.py:45
  46.9 8.2 %collective-permute-start.10 = (bf16[3,2,128,128]{3,2,1,0:T(8,128)(2,1)S(1)}, bf16[3,2,128,128]{3,2,1,0:T(8,128)(2,1)S(1)}, u32[]{:S(2)}, u32[]{:S(2)}) collective-permute-start(bf16[3,2,128,128]{3,2,1,0:T(8,128)(2,1)S(1)} %get-tuple-element.158), channel_id=1, source_target_pairs={{0,8},{1,9},{2,10},{3,11},{4,12},{5,13},{6,14},{7,15},{8,16},{9,17... | collective-permute-start | bytes 589832 | tf_op jit(solution)/shard_map/ppermute | solution.py:45
  55.2 6.8 %collective-permute-start.17 = (bf16[16,2,128,128]{3,2,1,0:T(8,128)(2,1)S(1)}, bf16[16,2,128,128]{3,2,1,0:T(8,128)(2,1)S(1)}, u32[]{:S(2)}, u32[]{:S(2)}) collective-permute-start(bf16[16,2,128,128]{3,2,1,0:T(8,128)(2,1)S(1)} %constant_dynamic-update-slice_fusion.refs_2_), channel_id=1, source_target_pairs={{0,32},{1,33},{2,34},{3,35},{4,36},{5,37},{6,38},{7,39},{8,40},{9,... | collective-permute-start | bytes 3145736 | tf_op jit(solution)/shard_map/ppermute | solution.py:45
  57.7 13.7 %collective-permute-start.16 = (bf16[7,2,128,128]{3,2,1,0:T(8,128)(2,1)S(1)}, bf16[7,2,128,128]{3,2,1,0:T(8,128)(2,1)S(1)}, u32[]{:S(2)}, u32[]{:S(2)}) collective-permute-start(bf16[7,2,128,128]{3,2,1,0:T(8,128)(2,1)S(1)} %pad_maximum_fusion), channel_id=1, source_target_pairs={{0,2},{1,3},{2,0},{3,1},{4,6},{5,7},{6,4},{7,5},{8,10},{9,11},{10,... | collective-permute-start | bytes 1376264 | tf_op jit(solution)/shard_map/ppermute | solution.py:45
  58.1 9.7 %collective-permute-start.15 = (bf16[3,2,128,128]{3,2,1,0:T(8,128)(2,1)S(1)}, bf16[3,2,128,128]{3,2,1,0:T(8,128)(2,1)S(1)}, u32[]{:S(2)}, u32[]{:S(2)}) collective-permute-start(bf16[3,2,128,128]{3,2,1,0:T(8,128)(2,1)S(1)} %pad_maximum_fusion.2), channel_id=1, source_target_pairs={{0,16},{1,17},{2,18},{3,19},{4,20},{5,21},{6,22},{7,23},{8,24},{9,... | collective-permute-start | bytes 589832 | tf_op jit(solution)/shard_map/ppermute | solution.py:45
  60.5 9.6 %collective-permute-start.14 = (bf16[3,2,128,128]{3,2,1,0:T(8,128)(2,1)S(1)}, bf16[3,2,128,128]{3,2,1,0:T(8,128)(2,1)S(1)}, u32[]{:S(2)}, u32[]{:S(2)}) collective-permute-start(bf16[3,2,128,128]{3,2,1,0:T(8,128)(2,1)S(1)} %pad_maximum_fusion.2), channel_id=1, source_target_pairs={{0,24},{1,25},{2,26},{3,27},{4,28},{5,29},{6,30},{7,31},{8,0},{9,1... | collective-permute-start | bytes 589832 | tf_op jit(solution)/shard_map/ppermute | solution.py:45
  61.4 9.1 %collective-permute-start.13 = (bf16[3,2,128,128]{3,2,1,0:T(8,128)(2,1)S(1)}, bf16[3,2,128,128]{3,2,1,0:T(8,128)(2,1)S(1)}, u32[]{:S(2)}, u32[]{:S(2)}) collective-permute-start(bf16[3,2,128,128]{3,2,1,0:T(8,128)(2,1)S(1)} %pad_maximum_fusion.2), channel_id=1, source_target_pairs={{0,8},{1,9},{2,10},{3,11},{4,12},{5,13},{6,14},{7,15},{8,16},{9,17... | collective-permute-start | bytes 589832 | tf_op jit(solution)/shard_map/ppermute | solution.py:45
  81.0 16.8 %collective-permute-start.19 = (bf16[3072,1280]{1,0:T(8,128)(2,1)S(1)}, bf16[3072,1280]{1,0:T(8,128)(2,1)S(1)}, u32[]{:S(2)}, u32[]{:S(2)}) collective-permute-start(bf16[3072,1280]{1,0:T(8,128)(2,1)S(1)} %bitcast.26), channel_id=1, source_target_pairs={{0,32},{1,33},{2,34},{3,35},{4,36},{5,37},{6,38},{7,39},{8,40},{9,... | collective-permute-start | bytes 23592968 | tf_op jit(solution)/shard_map/ppermute | solution.py:45
  99.8 10.7 %collective-permute-start.20 = (bf16[2,128,768]{2,1,0:T(8,128)(2,1)S(1)}, bf16[2,128,768]{2,1,0:T(8,128)(2,1)S(1)}, u32[]{:S(2)}, u32[]{:S(2)}) collective-permute-start(bf16[2,128,768]{2,1,0:T(8,128)(2,1)S(1)} %out_projection.2.here), channel_id=1, source_target_pairs={{0,64},{1,65},{2,66},{3,67},{4,68},{5,69},{6,70},{7,71},{8,72},{9,... | collective-permute-start | bytes 1179656 | tf_op jit(solution)/shard_map/ppermute | solution.py:45
  115.3 14.5 %all-to-all-start.2 = ((bf16[8,3,128,128]{3,2,1,0:T(8,128)(2,1)}), bf16[8,3,128,128]{3,2,1,0:T(8,128)(2,1)S(1)}, u32[]{:S(2)}, u32[]{:S(2)}) async-start(bf16[8,3,128,128]{3,2,1,0:T(8,128)(2,1)} %get-tuple-element.113), calls=%async_computation.2 | async-start | bytes 1572864 | tf_op jit(solution)/shard_map/all_to_all | solution.py:65
  130.0 10.7 %collective-permute-start.24 = (bf16[3,2,128,128]{3,2,1,0:T(8,128)(2,1)S(1)}, bf16[3,2,128,128]{3,2,1,0:T(8,128)(2,1)S(1)}, u32[]{:S(2)}, u32[]{:S(2)}) collective-permute-start(bf16[3,2,128,128]{3,2,1,0:T(8,128)(2,1)S(1)} %get-tuple-element.155), channel_id=1, source_target_pairs={{0,2},{1,3},{2,0},{3,1},{4,6},{5,7},{6,4},{7,5},{8,10},{9,11},{10,... | collective-permute-start | bytes 589832 | tf_op jit(solution)/shard_map/ppermute | solution.py:45
  132.3 8.4 %collective-permute-start.27 = (bf16[3,2,128,128]{3,2,1,0:T(8,128)(2,1)S(1)}, bf16[3,2,128,128]{3,2,1,0:T(8,128)(2,1)S(1)}, u32[]{:S(2)}, u32[]{:S(2)}) collective-permute-start(bf16[3,2,128,128]{3,2,1,0:T(8,128)(2,1)S(1)} %get-tuple-element.154), channel_id=1, source_target_pairs={{0,16},{1,17},{2,18},{3,19},{4,20},{5,21},{6,22},{7,23},{8,24},{9,... | collective-permute-start | bytes 589832 | tf_op jit(solution)/shard_map/ppermute | solution.py:45
  135.4 7.8 %collective-permute-start.25 = (bf16[3,2,128,128]{3,2,1,0:T(8,128)(2,1)S(1)}, bf16[3,2,128,128]{3,2,1,0:T(8,128)(2,1)S(1)}, u32[]{:S(2)}, u32[]{:S(2)}) collective-permute-start(bf16[3,2,128,128]{3,2,1,0:T(8,128)(2,1)S(1)} %get-tuple-element.154), channel_id=1, source_target_pairs={{0,8},{1,9},{2,10},{3,11},{4,12},{5,13},{6,14},{7,15},{8,16},{9,17... | collective-permute-start | bytes 589832 | tf_op jit(solution)/shard_map/ppermute | solution.py:45
  143.4 6.9 %collective-permute-start.32 = (bf16[16,2,128,128]{3,2,1,0:T(8,128)(2,1)S(1)}, bf16[16,2,128,128]{3,2,1,0:T(8,128)(2,1)S(1)}, u32[]{:S(2)}, u32[]{:S(2)}) collective-permute-start(bf16[16,2,128,128]{3,2,1,0:T(8,128)(2,1)S(1)} %constant_dynamic-update-slice_fusion.9.refs_2_), channel_id=1, source_target_pairs={{0,32},{1,33},{2,34},{3,35},{4,36},{5,37},{6,38},{7,39},{8,40},{9,... | collective-permute-start | bytes 3145736 | tf_op jit(solution)/shard_map/ppermute | solution.py:45
  147.1 13.7 %collective-permute-start.31 = (bf16[7,2,128,128]{3,2,1,0:T(8,128)(2,1)S(1)}, bf16[7,2,128,128]{3,2,1,0:T(8,128)(2,1)S(1)}, u32[]{:S(2)}, u32[]{:S(2)}) collective-permute-start(bf16[7,2,128,128]{3,2,1,0:T(8,128)(2,1)S(1)} %pad_maximum_fusion.1), channel_id=1, source_target_pairs={{0,2},{1,3},{2,0},{3,1},{4,6},{5,7},{6,4},{7,5},{8,10},{9,11},{10,... | collective-permute-start | bytes 1376264 | tf_op jit(solution)/shard_map/ppermute | solution.py:45
  147.9 8.3 %collective-permute-start.30 = (bf16[3,2,128,128]{3,2,1,0:T(8,128)(2,1)S(1)}, bf16[3,2,128,128]{3,2,1,0:T(8,128)(2,1)S(1)}, u32[]{:S(2)}, u32[]{:S(2)}) collective-permute-start(bf16[3,2,128,128]{3,2,1,0:T(8,128)(2,1)S(1)} %pad_maximum_fusion.3), channel_id=1, source_target_pairs={{0,16},{1,17},{2,18},{3,19},{4,20},{5,21},{6,22},{7,23},{8,24},{9,... | collective-permute-start | bytes 589832 | tf_op jit(solution)/shard_map/ppermute | solution.py:45
  148.9 9.7 %collective-permute-start.29 = (bf16[3,2,128,128]{3,2,1,0:T(8,128)(2,1)S(1)}, bf16[3,2,128,128]{3,2,1,0:T(8,128)(2,1)S(1)}, u32[]{:S(2)}, u32[]{:S(2)}) collective-permute-start(bf16[3,2,128,128]{3,2,1,0:T(8,128)(2,1)S(1)} %pad_maximum_fusion.3), channel_id=1, source_target_pairs={{0,24},{1,25},{2,26},{3,27},{4,28},{5,29},{6,30},{7,31},{8,0},{9,1... | collective-permute-start | bytes 589832 | tf_op jit(solution)/shard_map/ppermute | solution.py:45
  149.8 10.7 %collective-permute-start.28 = (bf16[3,2,128,128]{3,2,1,0:T(8,128)(2,1)S(1)}, bf16[3,2,128,128]{3,2,1,0:T(8,128)(2,1)S(1)}, u32[]{:S(2)}, u32[]{:S(2)}) collective-permute-start(bf16[3,2,128,128]{3,2,1,0:T(8,128)(2,1)S(1)} %pad_maximum_fusion.3), channel_id=1, source_target_pairs={{0,8},{1,9},{2,10},{3,11},{4,12},{5,13},{6,14},{7,15},{8,16},{9,17... | collective-permute-start | bytes 589832 | tf_op jit(solution)/shard_map/ppermute | solution.py:45
  186.5 11.9 %collective-permute-start.34 = (bf16[32,3840]{1,0:T(8,128)(2,1)S(1)}, bf16[32,3840]{1,0:T(8,128)(2,1)S(1)}, u32[]{:S(2)}, u32[]{:S(2)}) collective-permute-start(bf16[32,3840]{1,0:T(8,128)(2,1)S(1)} %get-tuple-element.136), channel_id=1, source_target_pairs={{0,32},{1,33},{2,34},{3,35},{4,36},{5,37},{6,38},{7,39},{8,40},{9,... | collective-permute-start | bytes 737288 | tf_op jit(solution)/shard_map/ppermute | solution.py:45
  (25 other events, 133.6 us)
